TPU v7x, 128 devices: a whole 4x4x4 slice. The times are simulated.
128 devices in a mesh: gx: 16 (over z_lo, x, core), gy: 8 (over z_hi, y).
Axes of the slice: x: 4, y: 4, z: 4 (z_hi: 2, z_lo: 2; z = z_hi * 2 + z_lo), core: 2. Of those that a mesh axis runs over, the one named last changes fastest.
Arguments:
- adjoint_in: float32 [4, 72, 512, 1024], P(None, None, 'gx', 'gy'), may hold values from -6 to 6
- courant_x: float32 [72, 512, 1024], P(None, 'gx', 'gy'), may hold values from -0.9 to 0.9
- courant_y: float32 [72, 512, 1024], P(None, 'gx', 'gy'), may hold values from -0.9 to 0.9
- mixing: float32 [71, 512, 1024], P(None, 'gx', 'gy'), may hold values from 0.05 to 5
- kernel_rows: bfloat16 [72, 524288], P(None, ('gx', 'gy')), may hold values from -6 to 6
- tracer_weights: bfloat16 [4, 524288], P(None, ('gx', 'gy')), may hold values from 0.25 to 1.5
- column_ids: int32 [524288], P(('gx', 'gy')), may hold values from 0 to 4095
- counts: int32 [128, 128], P(('gx', 'gy')), may hold values from 0 to 32, as said below
Outputs:
- adjoint_out: float32 [4, 72, 512, 1024], P(None, None, 'gx', 'gy')
- flux_gradient: float32 [4, 512, 1024], P(None, 'gx', 'gy')
Inputs may be any that keep to these rules, and one draw needn't show every extreme that they name: `counts`: live slots from one device to another; 32 is reached by one receiving device from every sender. `column_ids`: column id in the receiving tile, longitude-major.
All inputs are finite; a program needn't handle non-finite values.
Results may differ from a plain program's by a relative error of at most 0.0003.
Values may be sent and summed in bfloat16 or wider, within the bound.
No kernel may reach another device: no remote copies, remote signals or barrier semaphores. Data moves between devices by JAX's collectives and lax.ppermute only.
A program may use at most 320 MiB of HBM per device.

v0:
```python
import jax
import jax.numpy as jnp
from jax import lax
from jax.sharding import PartitionSpec as P

STEPS = 2


first_coef = (0.75, -0.15, 1.0 / 60.0)
second_coef = (1.5, -0.15, 1.0 / 90.0)
second_center = -49.0 / 18.0


def extended(cells, sides, width, closed):
    for axis, dim in sides:
        count = lax.axis_size(axis)
        ends = count if closed else count - 1
        head = lax.slice_in_dim(cells, 0, width, axis=dim)
        tail = lax.slice_in_dim(cells, cells.shape[dim] - width, cells.shape[dim], axis=dim)
        cells = jnp.concatenate(
            [
                lax.ppermute(tail, axis, [(i, (i + 1) % count) for i in range(ends)]),
                cells,
                lax.ppermute(head, axis, [((i + 1) % count, i) for i in range(ends)]),
            ],
            axis=dim,
        )
    return cells


def advect(padded, courant, axis, length):

    def piece(offset):
        return lax.slice_in_dim(padded, 3 + offset, 3 + offset + length, axis=axis)

    center = piece(0)
    slope = first_coef[0] * (piece(1) - piece(-1))
    curve = second_center * center + second_coef[0] * (piece(1) + piece(-1))
    for shift_k in (2, 3):
        slope = slope + first_coef[shift_k - 1] * (piece(shift_k) - piece(-shift_k))
        curve = curve + second_coef[shift_k - 1] * (piece(shift_k) + piece(-shift_k))
    return center + courant * slope + 0.5 * courant * courant * curve


def factor(mixing):
    levels = mixing.shape[0] + 1
    cps = []
    invs = []
    for level in range(levels):
        diag_part = jnp.ones_like(mixing[0])
        if level > 0:
            diag_part = diag_part + mixing[level - 1]
        if level < levels - 1:
            diag_part = diag_part + mixing[level]
        if level > 0:
            diag_part = diag_part - mixing[level - 1] * cps[level - 1] * -1.0
        inverse = 1.0 / diag_part
        invs.append(inverse)
        if level < levels - 1:
            cps.append(-mixing[level] * inverse)
    return (cps, invs)


def solve(field, mixing, cps, invs):
    levels = len(invs)
    carry = field[..., 0, :, :] * invs[0]
    forward = [carry]
    for level in range(1, levels):
        carry = (field[..., level, :, :] + mixing[level - 1] * carry) * invs[level]
        forward.append(carry)
    result = [None] * levels
    result[levels - 1] = forward[levels - 1]
    for level in range(levels - 2, -1, -1):
        result[level] = forward[level] - cps[level] * result[level + 1]
    return jnp.stack(result, axis=-3)


def local(
    adjoint_in, courant_x, courant_y, mixing, kernel_rows, tracer_weights, column_ids, counts
):
    tracer_count, level_count, lon_cells, lat_cells = adjoint_in.shape
    devices = lax.axis_size(("gx", "gy"))
    slot_count = kernel_rows.shape[1] // devices
    slot_place = jnp.arange(devices * slot_count, dtype=jnp.int32) % slot_count
    limits = jnp.repeat(counts[0], slot_count, total_repeat_length=devices * slot_count)
    live_rows = jnp.where((slot_place < limits)[None, :], kernel_rows, jnp.zeros_like(kernel_rows))
    got_rows, got_weights = (
        lax.all_to_all(live_rows, ("gx", "gy"), split_axis=1, concat_axis=1, tiled=True),
        lax.all_to_all(tracer_weights, ("gx", "gy"), split_axis=1, concat_axis=1, tiled=True),
    )
    cell_range = jnp.arange(lon_cells * lat_cells, dtype=jnp.int32)
    onehot = (column_ids[:, None] == cell_range[None, :]).astype(jnp.bfloat16)
    forcing_list = []
    for tracer in range(tracer_count):
        placed = onehot * got_weights[tracer][:, None]
        forcing_list.append(jnp.dot(got_rows, placed, preferred_element_type=jnp.float32))
    forcing = jnp.stack(forcing_list, axis=0)
    state = adjoint_in + forcing.reshape(tracer_count, level_count, lon_cells, lat_cells)
    cps, invs = factor(mixing)
    gradient = jnp.zeros((tracer_count, lon_cells, lat_cells), jnp.float32)
    for step in range(STEPS):
        wrapped = extended(state, (("gx", 2),), 3, True)
        zonal = advect(wrapped, courant_x, 2, lon_cells)
        padded = extended(zonal, (("gy", 3),), 3, False)
        meridional = advect(padded, courant_y, 3, lat_cells)
        state = solve(meridional, mixing, cps, invs)
        gradient = gradient + state[:, 0]
    return (state, gradient)


def solution(mesh):
    in_specs = (
        P(None, None, "gx", "gy"),
        P(None, "gx", "gy"),
        P(None, "gx", "gy"),
        P(None, "gx", "gy"),
        P(None, ("gx", "gy")),
        P(None, ("gx", "gy")),
        P(("gx", "gy")),
        P(("gx", "gy"), None),
    )
    out_specs = (P(None, None, "gx", "gy"), P(None, "gx", "gy"))
    return jax.shard_map(local, mesh=mesh, in_specs=in_specs, out_specs=out_specs, check_vma=False)
```

profile of v0, /device:TPU:64, one launch (start us, length us, event | category | flops | bytes accessed | tf_op | source)
XLA Modules:
  0.0 418.8 jit_solution(15522353103420576083)
XLA Ops:
  2.3 10.0 %all-to-all-start.1 = ((bf16[4,128,32]{2,0,1:T(4,128)(2,1)}), bf16[4,128,32]{2,0,1:T(4,128)(2,1)S(1)}, u32[]{:S(2)}, u32[]{:S(2)}) async-start(bf16[4,128,32]{2,0,1:T(4,128)(2,1)} %copy.1397), calls=%async_computation.1 | async-start | bytes 262144 | tf_op jit(solution)/shard_map/all_to_all | solution.py:89
  17.0 24.7 %gather_fusion = s32[4096]{0:T(1024)S(1)} fusion(s32[128]{0:T(128)S(1)} %bitcast.3716, s32[4096]{0:T(1024)S(1)} %broadcast_clamp_fusion), kind=kCustom, calls=%fused_computation | custom fusion | bytes 49152 | tf_op jit(solution)/shard_map/jit(_take)/gather | solution.py:85
  66.1 10.6 %all-to-all-start = ((bf16[72,128,32]{0,2,1:T(8,128)(2,1)}), bf16[72,128,32]{0,2,1:T(8,128)(2,1)}, u32[]{:S(2)}, u32[]{:S(2)}) async-start(bf16[72,128,32]{0,2,1:T(8,128)(2,1)} %bitcast.6), calls=%async_computation | async-start | bytes 2097152 | tf_op jit(solution)/shard_map/all_to_all | solution.py:88
  86.3 7.5 %all-to-all-done = bf16[72,128,32]{0,2,1:T(8,128)(2,1)} async-done(((bf16[72,128,32]{0,2,1:T(8,128)(2,1)}), bf16[72,128,32]{0,2,1:T(8,128)(2,1)}, u32[]{:S(2)}, u32[]{:S(2)}) %all-to-all-start) | async-done | bytes 589856 | tf_op jit(solution)/shard_map/all_to_all | solution.py:88
  93.8 13.3 %fusion.3 = f32[72,32,128]{2,0,1:T(8,128)S(1)} fusion(bf16[72,4096,1]{0,1,2:T(8,128)(2,1)} %bitcast.8, s32[32,128]{1,0:T(8,128)} %multiply_add_fusion.4, s32[4096]{0:T(1024)} %param.16, bf16[4096]{0:T(1024)(128)(2,1)} %mul.20172), kind=kOutput, calls=%fused_computation.8 | convolution fusion | flops 2449473536 | bytes 1810432 | tf_op jit(solution)/shard_map/dot_general | solution.py:96
  107.2 13.1 %fusion.2 = f32[72,32,128]{2,0,1:T(8,128)S(1)} fusion(bf16[72,4096,1]{0,1,2:T(8,128)(2,1)} %bitcast.8, s32[32,128]{1,0:T(8,128)S(1)} %copy-done.212, s32[4096]{0:T(1024)S(1)} %copy-done.216, bf16[4096]{0:T(1024)(128)(2,1)S(1)} %copy-done.213), kind=kOutput, calls=%fused_computation.7 | convolution fusion | flops 2449473536 | bytes 1810432 | tf_op jit(solution)/shard_map/dot_general | solution.py:96
  120.3 13.3 %fusion.1 = f32[72,32,128]{2,0,1:T(8,128)S(1)} fusion(bf16[72,4096,1]{0,1,2:T(8,128)(2,1)} %bitcast.8, s32[32,128]{1,0:T(8,128)S(1)} %copy-done.212, s32[4096]{0:T(1024)S(1)} %copy-done.216, bf16[4096]{0:T(1024)(128)(2,1)S(1)} %copy-done.214), kind=kOutput, calls=%fused_computation.6 | convolution fusion | flops 2449473536 | bytes 1810432 | tf_op jit(solution)/shard_map/dot_general | solution.py:96
  133.6 13.2 %fusion = f32[72,32,128]{2,0,1:T(8,128)S(1)} fusion(bf16[72,4096,1]{0,1,2:T(8,128)(2,1)} %bitcast.8, s32[32,128]{1,0:T(8,128)S(1)} %copy-done.212, s32[4096]{0:T(1024)S(1)} %copy-done.216, bf16[4096]{0:T(1024)(128)(2,1)S(1)} %mul.20163), kind=kOutput, calls=%fused_computation.5 | convolution fusion | flops 2449473536 | bytes 1810432 | tf_op jit(solution)/shard_map/dot_general | solution.py:96
  152.9 3.7 collective-permute-done
  156.8 4.1 collective-permute-done.1
  161.0 6.4 %multiply_add_fusion.3 = f32[4,72,32,128]{3,2,0,1:T(8,128)S(1)} fusion(f32[4,72,32,128]{3,2,0,1:T(8,128)S(1)} %maximum_add_fusion, f32[4,72,3,128]{3,2,0,1:T(4,128)S(1)} %copy.1408, f32[4,72,3,128]{3,2,0,1:T(4,128)S(1)} %copy.1410, f32[72,32,128]{2,1,0:T(8,128)S(1)} %multiply_multiply_fusion.1, f32[72,32,128]{2,1,0:T(8,128)S(1)} %copy-done.6), kind=kLoop, calls=%fused_computation.94 | loop fusion | flops 33030144 | bytes 12681216 | tf_op jit(solution)/shard_map/add | solution.py:42
  167.5 5.4 %fusion.559 = (f32[4,72,32,3]{3,2,0,1:T(8,128)}, f32[4,72,32,3]{3,2,0,1:T(8,128)}) fusion(f32[4,72,32,128]{3,2,0,1:T(8,128)S(1)} %multiply_add_fusion.3), kind=kLoop, calls=%fused_computation.1324 | loop fusion | bytes 442368 | tf_op jit(solution)/shard_map/slice | solution.py:19
  172.8 4.1 copy.1413
  176.9 4.0 copy.1411
  187.2 8.2 %collective-permute-done.3 = f32[4,72,32,3]{1,2,3,0:T(8,128)S(1)} collective-permute-done((f32[4,72,32,3]{1,2,3,0:T(8,128)S(1)}, f32[4,72,32,3]{1,2,3,0:T(8,128)S(1)}, u32[]{:S(2)}, u32[]{:S(2)}) %collective-permute-start.3) | collective-permute-done | bytes 110624 | tf_op jit(solution)/shard_map/ppermute | solution.py:22
  195.4 5.0 %copy.1414 = f32[4,72,32,3]{3,2,0,1:T(8,128)} copy(f32[4,72,32,3]{1,2,3,0:T(8,128)S(1)} %collective-permute-done.3) | data formatting | bytes 221184 | tf_op jit(solution)/shard_map/ppermute | solution.py:22
  200.4 5.1 %copy.1412 = f32[4,72,32,3]{3,2,0,1:T(8,128)} copy(f32[4,72,32,3]{1,2,3,0:T(8,128)S(1)} %collective-permute-done.2) | data formatting | bytes 221184 | tf_op jit(solution)/shard_map/ppermute | solution.py:24
  205.8 32.6 %multiply_add_fusion.2 = f32[4,72,32,128]{3,2,0,1:T(8,128)S(1)} fusion(f32[4,72,32,128]{3,2,0,1:T(8,128)} %copy-done.3, f32[4,72,32,3]{3,2,0,1:T(8,128)} %copy.1412, f32[4,72,32,3]{3,2,0,1:T(8,128)} %copy.1414, f32[72,32,128]{2,1,0:T(8,128)S(1)} %copy-done.11, f32[72,32,128]{2,1,0:T(8,128)S(1)} %copy-done.9), kind=kLoop, calls=%fused_computation.93 | loop fusion | flops 33030144 | bytes 12017664 | tf_op jit(solution)/shard_map/add | solution.py:42
  241.0 3.9 constant_dynamic-update-slice_fusion.71
  263.9 6.9 %collective-permute-done.5 = f32[4,72,3,128]{3,1,2,0:T(8,128)S(1)} collective-permute-done((f32[4,72,3,128]{3,1,2,0:T(8,128)S(1)}, f32[4,72,3,128]{3,1,2,0:T(8,128)S(1)}, u32[]{:S(2)}, u32[]{:S(2)}) %collective-permute-start.5) | collective-permute-done | bytes 442400 | tf_op jit(solution)/shard_map/ppermute | solution.py:22
  271.2 22.3 %add_multiply_fusion.5 = (f32[4,72,32,128]{3,2,0,1:T(8,128)}, f32[4,72,32,128]{3,2,0,1:T(8,128)}, f32[4,72,32,128]{3,2,0,1:T(8,128)}, f32[4,72,32,128]{3,2,0,1:T(8,128)}) fusion(f32[4,72,35,128]{3,2,0,1:T(8,128)S(1)} %copy_dynamic-update-slice_fusion, f32[4,72,32,128]{3,2,0,1:T(8,128)} %get-tuple-element.305, f32[4,72,3,128]{3,2,0,1:T(4,128)S(1)} %copy.1522, ...), kind=kLoop, calls=%fused_computation.91 | loop fusion | flops 24772608 | bytes 39370752 | tf_op jit(solution)/shard_map/mul | solution.py:38
  293.5 9.6 %copy_add_fusion.4 = f32[4,72,32,128]{3,2,1,0:T(8,128)S(1)} fusion(f32[4,72,32,128]{3,2,0,1:T(8,128)} %get-tuple-element.298, f32[4,72,32,128]{3,2,0,1:T(8,128)} %get-tuple-element.297, f32[4,72,32,128]{3,2,0,1:T(8,128)} %get-tuple-element.299, f32[4,72,32,128]{3,2,0,1:T(8,128)} %get-tuple-element.296, f32[4,72,32,128]{3,2,1,0:T(8,128)} %copy-done.4, ...), kind=kLoop, calls=%fused_computation.80 | loop fusion | flops 7077888 | bytes 29491200 | tf_op jit(solution)/shard_map/add | solution.py:42
  303.1 5.4 %fusion.557 = (f32[4,72,32,3]{3,2,1,0:T(8,128)}, f32[4,72,32,3]{3,2,1,0:T(8,128)}) fusion(f32[4,72,32,128]{3,2,1,0:T(8,128)S(1)} %copy_add_fusion.4), kind=kLoop, calls=%fused_computation.1322 | loop fusion | bytes 442368 | tf_op jit(solution)/shard_map/slice | solution.py:19
  308.5 4.0 copy.1534
  314.4 4.0 copy.1531
  318.4 7.5 %collective-permute-start.6 = (f32[4,72,32,3]{1,2,3,0:T(8,128)S(1)}, f32[4,72,32,3]{1,2,3,0:T(8,128)S(1)}, u32[]{:S(2)}, u32[]{:S(2)}) collective-permute-start(f32[4,72,32,3]{1,2,3,0:T(8,128)S(1)} %copy.1531), channel_id=1, source_target_pairs={{1,0},{2,1},{3,2},{4,3},{5,4},{6,5},{7,6},{9,8},{10,9},{11,10},{12... | collective-permute-start | bytes 331784 | tf_op jit(solution)/shard_map/ppermute | solution.py:24
  325.9 5.2 %copy.1537 = f32[4,72,32,128]{3,2,0,1:T(8,128)} copy(f32[4,72,32,128]{3,2,1,0:T(8,128)} %copy-done.2) | data formatting | bytes 9437184 | tf_op jit(solution)/shard_map/add | solution.py:42
  331.2 5.2 %copy.1535 = f32[4,72,32,3]{3,2,0,1:T(8,128)} copy(f32[4,72,32,3]{1,2,3,0:T(8,128)S(1)} %collective-permute-done.7) | data formatting | bytes 221184 | tf_op jit(solution)/shard_map/ppermute | solution.py:22
  336.4 4.9 %copy.1533 = f32[4,72,32,3]{3,2,0,1:T(8,128)} copy(f32[4,72,32,3]{1,2,3,0:T(8,128)S(1)} %collective-permute-done.6) | data formatting | bytes 221184 | tf_op jit(solution)/shard_map/ppermute | solution.py:24
  341.4 45.7 %add_multiply_fusion.2 = (f32[4,72,32,128]{3,2,0,1:T(8,128)}, f32[4,72,32,128]{3,2,0,1:T(8,128)}, f32[4,72,32,128]{3,2,0,1:T(8,128)}) fusion(f32[4,72,32,3]{3,2,0,1:T(8,128)} %copy.1533, f32[4,72,32,128]{3,2,0,1:T(8,128)} %copy.1537, f32[4,72,32,3]{3,2,0,1:T(8,128)} %copy.1535, f32[72,32,128]{2,1,0:T(8,128)S(1)} %copy-done.10), kind=kLoop, calls=%fused_computation.87 | loop fusion | flops 25952256 | bytes 20275200 | tf_op jit(solution)/shard_map/mul | solution.py:38
  387.4 11.0 %copy_add_fusion = f32[4,72,32,128]{3,2,1,0:T(8,128)S(1)} fusion(f32[4,72,32,128]{3,2,0,1:T(8,128)} %get-tuple-element.294, f32[4,72,32,128]{3,2,0,1:T(8,128)} %get-tuple-element.295, f32[4,72,32,128]{3,2,0,1:T(8,128)} %get-tuple-element.293, f32[4,72,32,128]{3,2,1,0:T(8,128)S(1)} %bitcast.3718, f32[72,32,128]{2,1,0:T(8,128)S(1)} %copy-done.12, ...), kind=kLoop, calls=%fused_computation.75 | loop fusion | flops 11796480 | bytes 29712384 | tf_op jit(solution)/shard_map/add | solution.py:42
  400.8 4.5 %fusion.442 = (f32[4,32,128]{2,1,0:T(8,128)}, f32[4,32,128]{2,1,0:T(8,128)S(1)}, f32[4,32,128]{2,1,0:T(8,128)S(1)}, f32[4,32,128]{2,1,0:T(8,128)S(1)}, f32[4,32,...) fusion(f32[4,32,128]{2,1,0:T(8,128)} %get-tuple-element.140, ...), kind=kLoop, calls=%fused_computation.1321 | loop fusion | flops 5210112 | bytes 10092544 | tf_op jit(solution)/shard_map/add | solution.py:107
  (672 shorter events, 89.2 us)
Async XLA Ops:
  2.3 63.8 %all-to-all-start.1 = ((bf16[4,128,32]{2,0,1:T(4,128)(2,1)}), bf16[4,128,32]{2,0,1:T(4,128)(2,1)S(1)}, u32[]{:S(2)}, u32[]{:S(2)}) async-start(bf16[4,128,32]{2,0,1:T(4,128)(2,1)} %copy.1397), calls=%async_computation.1 | async-start | bytes 262144 | tf_op jit(solution)/shard_map/all_to_all | solution.py:89
  16.2 42.6 %copy-start.50 = (f32[32,128]{1,0:T(8,128)}, f32[32,128]{1,0:T(8,128)S(1)}, u32[]{:S(2)}) copy-start(f32[32,128]{1,0:T(8,128)S(1)} %get-tuple-element.201) | copy-start | bytes 49156
  66.1 27.7 %all-to-all-start = ((bf16[72,128,32]{0,2,1:T(8,128)(2,1)}), bf16[72,128,32]{0,2,1:T(8,128)(2,1)}, u32[]{:S(2)}, u32[]{:S(2)}) async-start(bf16[72,128,32]{0,2,1:T(8,128)(2,1)} %bitcast.6), calls=%async_computation | async-start | bytes 2097152 | tf_op jit(solution)/shard_map/all_to_all | solution.py:88
  78.1 82.9 %copy-start.7 = (f32[72,32,128]{2,1,0:T(8,128)}, f32[72,32,128]{2,1,0:T(8,128)S(1)}, u32[]{:S(2)}) copy-start(f32[72,32,128]{2,1,0:T(8,128)S(1)} %multiply_multiply_fusion.1) | copy-start | bytes 3538948
  149.5 7.1 %collective-permute-start = (f32[4,72,3,128]{3,1,2,0:T(8,128)S(1)}, f32[4,72,3,128]{3,1,2,0:T(8,128)S(1)}, u32[]{:S(2)}, u32[]{:S(2)}) collective-permute-start(f32[4,72,3,128]{3,1,2,0:T(8,128)S(1)} %copy.1407), channel_id=1, source_target_pairs={{8,0},{16,8},{24,16},{32,24},{40,32},{48,40},{56,48},{64,56},{72,6... | collective-permute-start | bytes 1327112 | tf_op jit(solution)/shard_map/ppermute | solution.py:24
  150.8 10.0 %collective-permute-start.1 = (f32[4,72,3,128]{3,1,2,0:T(8,128)S(1)}, f32[4,72,3,128]{3,1,2,0:T(8,128)S(1)}, u32[]{:S(2)}, u32[]{:S(2)}) collective-permute-start(f32[4,72,3,128]{3,1,2,0:T(8,128)S(1)} %copy.1409), channel_id=1, source_target_pairs={{0,8},{8,16},{16,24},{24,32},{32,40},{40,48},{48,56},{56,64},{64,7... | collective-permute-start | bytes 1327112 | tf_op jit(solution)/shard_map/ppermute | solution.py:22
  180.9 19.5 %collective-permute-start.2 = (f32[4,72,32,3]{1,2,3,0:T(8,128)S(1)}, f32[4,72,32,3]{1,2,3,0:T(8,128)S(1)}, u32[]{:S(2)}, u32[]{:S(2)}) collective-permute-start(f32[4,72,32,3]{1,2,3,0:T(8,128)S(1)} %copy.1411), channel_id=1, source_target_pairs={{1,0},{2,1},{3,2},{4,3},{5,4},{6,5},{7,6},{9,8},{10,9},{11,10},{12... | collective-permute-start | bytes 331784 | tf_op jit(solution)/shard_map/ppermute | solution.py:24
  184.2 11.2 %collective-permute-start.3 = (f32[4,72,32,3]{1,2,3,0:T(8,128)S(1)}, f32[4,72,32,3]{1,2,3,0:T(8,128)S(1)}, u32[]{:S(2)}, u32[]{:S(2)}) collective-permute-start(f32[4,72,32,3]{1,2,3,0:T(8,128)S(1)} %copy.1413), channel_id=1, source_target_pairs={{0,1},{1,2},{2,3},{3,4},{4,5},{5,6},{6,7},{8,9},{9,10},{10,11},{11... | collective-permute-start | bytes 331784 | tf_op jit(solution)/shard_map/ppermute | solution.py:22
  187.1 51.3 %copy-start.204 = (f32[32,128]{1,0:T(8,128)}, f32[32,128]{1,0:T(8,128)S(1)}, u32[]{:S(2)}) copy-start(f32[32,128]{1,0:T(8,128)S(1)} %get-tuple-element.503) | copy-start | bytes 49156
  187.1 53.5 %copy-start.192 = (f32[32,128]{1,0:T(8,128)}, f32[32,128]{1,0:T(8,128)S(1)}, u32[]{:S(2)}) copy-start(f32[32,128]{1,0:T(8,128)S(1)} %get-tuple-element.504) | copy-start | bytes 49156
  187.1 53.5 %copy-start.202 = (f32[32,128]{1,0:T(8,128)}, f32[32,128]{1,0:T(8,128)S(1)}, u32[]{:S(2)}) copy-start(f32[32,128]{1,0:T(8,128)S(1)} %get-tuple-element.356) | copy-start | bytes 49156
  187.1 53.5 %copy-start.203 = (f32[32,128]{1,0:T(8,128)}, f32[32,128]{1,0:T(8,128)S(1)}, u32[]{:S(2)}) copy-start(f32[32,128]{1,0:T(8,128)S(1)} %get-tuple-element.502) | copy-start | bytes 49156
  187.1 60.7 %copy-start.135 = (f32[32,128]{1,0:T(8,128)}, f32[32,128]{1,0:T(8,128)S(1)}, u32[]{:S(2)}) copy-start(f32[32,128]{1,0:T(8,128)S(1)} %get-tuple-element.357) | copy-start | bytes 49156
  187.1 60.7 %copy-start.137 = (f32[32,128]{1,0:T(8,128)}, f32[32,128]{1,0:T(8,128)S(1)}, u32[]{:S(2)}) copy-start(f32[32,128]{1,0:T(8,128)S(1)} %get-tuple-element.501) | copy-start | bytes 49156
  205.5 33.0 %copy-start.19 = (f32[1,32,128]{2,1,0:T(8,128)S(1)}, f32[1,32,128]{2,1,0:T(8,128)}, u32[]{:S(2)}) copy-start(f32[1,32,128]{2,1,0:T(8,128)} %copy-done.18) | copy-start | bytes 49156
  205.5 33.0 %copy-start.21 = (f32[1,32,128]{2,1,0:T(8,128)S(1)}, f32[1,32,128]{2,1,0:T(8,128)}, u32[]{:S(2)}) copy-start(f32[1,32,128]{2,1,0:T(8,128)} %copy-done.20) | copy-start | bytes 49156
  205.5 33.0 %copy-start.23 = (f32[1,32,128]{2,1,0:T(8,128)S(1)}, f32[1,32,128]{2,1,0:T(8,128)}, u32[]{:S(2)}) copy-start(f32[1,32,128]{2,1,0:T(8,128)} %copy-done.22) | copy-start | bytes 49156
  205.5 33.0 %copy-start.25 = (f32[1,32,128]{2,1,0:T(8,128)S(1)}, f32[1,32,128]{2,1,0:T(8,128)}, u32[]{:S(2)}) copy-start(f32[1,32,128]{2,1,0:T(8,128)} %copy-done.24) | copy-start | bytes 49156
  205.5 33.0 %copy-start.27 = (f32[1,32,128]{2,1,0:T(8,128)S(1)}, f32[1,32,128]{2,1,0:T(8,128)}, u32[]{:S(2)}) copy-start(f32[1,32,128]{2,1,0:T(8,128)} %copy-done.26) | copy-start | bytes 49156
  205.5 33.0 %copy-start.29 = (f32[1,32,128]{2,1,0:T(8,128)S(1)}, f32[1,32,128]{2,1,0:T(8,128)}, u32[]{:S(2)}) copy-start(f32[1,32,128]{2,1,0:T(8,128)} %copy-done.28) | copy-start | bytes 49156
  205.5 33.0 %copy-start.31 = (f32[1,32,128]{2,1,0:T(8,128)S(1)}, f32[1,32,128]{2,1,0:T(8,128)}, u32[]{:S(2)}) copy-start(f32[1,32,128]{2,1,0:T(8,128)} %copy-done.30) | copy-start | bytes 49156
  205.6 33.0 %copy-start.33 = (f32[1,32,128]{2,1,0:T(8,128)S(1)}, f32[1,32,128]{2,1,0:T(8,128)}, u32[]{:S(2)}) copy-start(f32[1,32,128]{2,1,0:T(8,128)} %copy-done.32) | copy-start | bytes 49156
  205.6 33.0 %copy-start.35 = (f32[1,32,128]{2,1,0:T(8,128)S(1)}, f32[1,32,128]{2,1,0:T(8,128)}, u32[]{:S(2)}) copy-start(f32[1,32,128]{2,1,0:T(8,128)} %copy-done.34) | copy-start | bytes 49156
  205.6 33.0 %copy-start.37 = (f32[1,32,128]{2,1,0:T(8,128)S(1)}, f32[1,32,128]{2,1,0:T(8,128)}, u32[]{:S(2)}) copy-start(f32[1,32,128]{2,1,0:T(8,128)} %copy-done.36) | copy-start | bytes 49156
  205.6 33.0 %copy-start.39 = (f32[1,32,128]{2,1,0:T(8,128)S(1)}, f32[1,32,128]{2,1,0:T(8,128)}, u32[]{:S(2)}) copy-start(f32[1,32,128]{2,1,0:T(8,128)} %copy-done.38) | copy-start | bytes 49156
  259.6 11.3 %collective-permute-start.4 = (f32[4,72,3,128]{3,1,2,0:T(8,128)S(1)}, f32[4,72,3,128]{3,1,2,0:T(8,128)S(1)}, u32[]{:S(2)}, u32[]{:S(2)}) collective-permute-start(f32[4,72,3,128]{3,1,2,0:T(8,128)S(1)} %copy.1518), channel_id=1, source_target_pairs={{8,0},{16,8},{24,16},{32,24},{40,32},{48,40},{56,48},{64,56},{72,6... | collective-permute-start | bytes 1327112 | tf_op jit(solution)/shard_map/ppermute | solution.py:24
  260.9 9.8 %collective-permute-start.5 = (f32[4,72,3,128]{3,1,2,0:T(8,128)S(1)}, f32[4,72,3,128]{3,1,2,0:T(8,128)S(1)}, u32[]{:S(2)}, u32[]{:S(2)}) collective-permute-start(f32[4,72,3,128]{3,1,2,0:T(8,128)S(1)} %copy.1521), channel_id=1, source_target_pairs={{0,8},{8,16},{16,24},{24,32},{32,40},{40,48},{48,56},{56,64},{64,7... | collective-permute-start | bytes 1327112 | tf_op jit(solution)/shard_map/ppermute | solution.py:22
  312.5 18.7 %collective-permute-start.7 = (f32[4,72,32,3]{1,2,3,0:T(8,128)S(1)}, f32[4,72,32,3]{1,2,3,0:T(8,128)S(1)}, u32[]{:S(2)}, u32[]{:S(2)}) collective-permute-start(f32[4,72,32,3]{1,2,3,0:T(8,128)S(1)} %copy.1534), channel_id=1, source_target_pairs={{0,1},{1,2},{2,3},{3,4},{4,5},{5,6},{6,7},{8,9},{9,10},{10,11},{11... | collective-permute-start | bytes 331784 | tf_op jit(solution)/shard_map/ppermute | solution.py:22
  318.4 18.0 %collective-permute-start.6 = (f32[4,72,32,3]{1,2,3,0:T(8,128)S(1)}, f32[4,72,32,3]{1,2,3,0:T(8,128)S(1)}, u32[]{:S(2)}, u32[]{:S(2)}) collective-permute-start(f32[4,72,32,3]{1,2,3,0:T(8,128)S(1)} %copy.1531), channel_id=1, source_target_pairs={{1,0},{2,1},{3,2},{4,3},{5,4},{6,5},{7,6},{9,8},{10,9},{11,10},{12... | collective-permute-start | bytes 331784 | tf_op jit(solution)/shard_map/ppermute | solution.py:24
  336.4 50.7 %slice-start = ((s8[4718592]{0:T(1024)(128)(4,1)}), s8[524288]{0:T(1024)(128)(4,1)S(1)}, s32[]{:S(2)}) async-start(s8[4718592]{0:T(1024)(128)(4,1)} %bitcast.3717), calls=%async_computation.2 | async-start | bytes 1048576
  341.3 45.7 %slice-start.1 = ((s8[4718592]{0:T(1024)(128)(4,1)}), s8[4194304]{0:T(1024)(128)(4,1)S(1)}, s32[]{:S(2)}) async-start(s8[4718592]{0:T(1024)(128)(4,1)} %bitcast.3717), calls=%async_computation.3 | async-start | bytes 8388608
  341.4 45.7 %copy-start.12 = (f32[72,32,128]{2,1,0:T(8,128)S(1)}, f32[72,32,128]{2,1,0:T(8,128)}, u32[]{:S(2)}) copy-start(f32[72,32,128]{2,1,0:T(8,128)} %multiply_multiply_fusion) | copy-start | bytes 3538948
  (199 other events, 2444.9 us)
where the time goes:
time: 425 us; the launch traced here: 419 us
  other arithmetic  194 us (46%)
  local copies, waits for them, and re-layouts  97.1 us (23%)
  matrix products  52.9 us (12%)
  starting transfers between devices  38.9 us (9%)
  waiting for transfers between devices  30.4 us (7%)
  between operations  5.31 us (1%)
    mul x2, other arithmetic, advect(): curve = second_center * center + second_coef[0] * (piece(1) + piece(-1))  68 us
    add x4, other arithmetic, advect(): return center + courant * slope + 0.5 * courant * courant * curve  59.5 us
    dot_general x4, matrix products, local(): jnp.dot(got_rows, placed, preferred_element_type=jnp.float32)  52.9 us
    unnamed x75, other arithmetic  27 us
    gather x1, local copies, waits for them, and re-layouts, local(): jnp.repeat(counts[0], slot_count, total_repeat_length=devices * slot_count)  24.7 us
    slice x8, local copies, waits for them, and re-layouts, extended(): lax.slice_in_dim(cells, cells.shape[dim] - width, cells.shape[dim], axis=...  19.4 us
    ppermute x4, waiting for transfers between devices, extended(): lax.ppermute(tail, axis, [(i, (i + 1) % count) for i in range(ends)])  19.1 us
    ppermute x4, starting transfers between devices, extended(): lax.ppermute(head, axis, [((i + 1) % count, i) for i in range(ends)])  13.4 us
  transfers between devices with their start and end apart: 10, of which 5 were waited for; matrix products, arithmetic and copies ran while one was open for 21% of the time, Pallas kernels for 0%

commit v1 on v0

v1 whole, which is shorter than its diff:
```python
import jax
import jax.numpy as jnp
from jax import lax
from jax.experimental import pallas as pl
from jax.experimental.pallas import tpu as pltpu
from jax.sharding import PartitionSpec as P

STEPS = 2
LB = 8

D1, D2, D3 = 0.75, -0.15, 1.0 / 60.0
E1, E2, E3 = 1.5, -0.15, 1.0 / 90.0
E0 = -49.0 / 18.0

f32 = jnp.float32
bf16 = jnp.bfloat16


def swap_blocks(x, lane):
    upper = (lane & 64) != 0
    odd = (lane & 32) != 0
    y = [None] * 4
    for a in (0, 1):
        y[a] = jnp.where(upper, pltpu.roll(x[a + 2], 64, 1), x[a])
        y[a + 2] = jnp.where(upper, x[a + 2], pltpu.roll(x[a], 64, 1))
    z = [None] * 4
    for a in (0, 2):
        z[a] = jnp.where(odd, pltpu.roll(y[a + 1], 32, 1), y[a])
        z[a + 1] = jnp.where(odd, y[a + 1], pltpu.roll(y[a], 96, 1))
    return z


def split(value):
    hi = value.astype(bf16)
    return hi, (value - hi.astype(f32)).astype(bf16)


def pack_kernel(counts, rows, weights, out):
    lane = lax.broadcasted_iota(jnp.int32, (24, 128), 1)
    block = lane >> 5

    def group(g, _):
        lanes = pl.ds(pl.multiple_of(g * 128, 128), 128)
        limit = jnp.where(
            block < 2,
            jnp.where(block == 0, counts[0, 4 * g], counts[0, 4 * g + 1]),
            jnp.where(block == 2, counts[0, 4 * g + 2], counts[0, 4 * g + 3]),
        )
        live = (lane & 31) < limit
        parts = [jnp.where(live, rows[24 * q : 24 * q + 24, lanes].astype(f32), 0.0) for q in range(3)]
        parts.append(jnp.concatenate([weights[:, lanes].astype(f32), jnp.zeros((20, 128), f32)], axis=0))
        for i, piece in enumerate(swap_blocks(parts, lane)):
            out[4 * g + i] = piece.astype(bf16)
        return 0

    lax.fori_loop(0, out.shape[0] // 4, group, 0, unroll=2)


def factor_kernel(mixing, inv_out, q_out):
    levels = inv_out.shape[0]
    top = mixing[0]
    inv = 1.0 / (1.0 + top)
    q = top * inv
    inv_out[0] = inv
    q_out[0] = q

    def level(l, carry):
        below, q = carry
        above = mixing[l]
        inv = 1.0 / (1.0 + below + above - below * q)
        q = above * inv
        inv_out[l] = inv
        q_out[l] = q
        return above, q

    below, q = lax.fori_loop(1, levels - 1, level, (top, q))
    inv_out[levels - 1] = 1.0 / (1.0 + below - below * q)
    q_out[levels - 1] = jnp.zeros_like(q)


def forcing_kernel(got, code, adjoint, state, x_low, x_high, lhs):
    step = pl.program_id(0)
    lane = lax.broadcasted_iota(jnp.int32, (24, 128), 1)
    half = lhs.shape[0] // 2
    slots = lhs.shape[1]

    @pl.when(step == 0)
    def _():
        def group(g, _):
            lanes = pl.ds(pl.multiple_of(g * 128, 128), 128)
            parts = swap_blocks([got[4 * g + i].astype(f32) for i in range(4)], lane)
            for t in range(4):
                weight = parts[3][t : t + 1, :]
                for q in range(3):
                    hi, lo = split(parts[q] * weight)
                    row = 72 * t + 24 * q
                    lhs[row : row + 24, lanes] = hi
                    lhs[half + row : half + row + 24, lanes] = lo
            return 0

        lax.fori_loop(0, slots // 128, group, 0)

    chunk = min(1024, slots)
    one, zero = jnp.ones((), bf16), jnp.zeros((), bf16)
    results = []
    for pair in range(4):
        lon = step * 8 + 2 * pair
        total = None
        for k in range(slots // chunk):
            part = code[k * chunk : (k + 1) * chunk, :]
            placed = jnp.concatenate(
                [jnp.where(part == (lon + a).astype(f32).astype(bf16), one, zero) for a in range(2)], axis=1
            )
            product = jnp.dot(lhs[:, k * chunk : (k + 1) * chunk], placed, preferred_element_type=f32)
            total = product if total is None else total + product
        total = total[:half] + total[half:]
        for a in range(2):
            cell = adjoint[:, 2 * pair + a, :] + total[:, 128 * a : 128 * a + 128]
            state[:, 2 * pair + a, :] = cell

    @pl.when(step == 0)
    def _():
        low_edge(state, x_low)

    @pl.when(step == pl.num_programs(0) - 1)
    def _():
        high_edge(state, x_high)


def low_edge(state, out):
    out[0], out[1] = split(state[:, 0, :])
    out[2] = state[:, 1, :].astype(bf16)
    out[3] = state[:, 2, :].astype(bf16)


def high_edge(state, out):
    out[0], out[1] = split(state[:, 7, :])
    out[2] = state[:, 6, :].astype(bf16)
    out[3] = state[:, 5, :].astype(bf16)


def zonal_kernel(state, courant, left, right, zonal, to_left, to_right, pad):
    lane = lax.broadcasted_iota(jnp.int32, (8, 128), 1)
    group = lane >> 2
    for t in range(4):
        base = t * LB * 48
        for where, halo in ((0, left), (1, right)):
            near = halo[0, t].astype(f32) + halo[1, t].astype(f32)
            for k, value in enumerate((near, halo[2, t].astype(f32), halo[3, t].astype(f32))):
                row = base + (7 - k if where == 0 else 40 + k)
                pad[pl.ds(row, LB, stride=48), :] = value
        for l in range(LB):
            for r in range(4):
                pad[base + 48 * l + 8 + 8 * r : base + 48 * l + 16 + 8 * r, :] = state[t, l, 8 * r : 8 * r + 8, :]
    for r in range(4):
        lefts = jnp.zeros((8, 128), f32)
        rights = jnp.zeros((8, 128), f32)
        for l in range(LB):
            c = courant[l, 8 * r : 8 * r + 8, :]
            c2 = 0.5 * c * c
            for t in range(4):
                base = (t * LB + l) * 48 + 8 + 8 * r
                v = {k: pad[base + k : base + k + 8, :] for k in range(-3, 4)}
                out = stencil(v, c, c2)
                zonal[t, l, 8 * r : 8 * r + 8, :] = out
                i = t * LB + l
                mine = group == i
                lefts = jnp.where(mine, turn(out, 4 * i), lefts)
                rights = jnp.where(mine, turn(out, 4 * i + 3), rights)
        rest = (lane & 3) == 3
        for source, shift, dest in ((lefts, 3, to_left), (rights, 1, to_right)):
            hi = source.astype(bf16).astype(f32)
            dest[0, 8 * r : 8 * r + 8, :] = jnp.where(rest, pltpu.roll(source - hi, shift, 1), hi).astype(bf16)


def turn(value, shift):
    shift = shift % 128
    return value if shift == 0 else pltpu.roll(value, shift, 1)


def stencil(v, c, c2):
    slope = D1 * (v[1] - v[-1]) + D2 * (v[2] - v[-2]) + D3 * (v[3] - v[-3])
    curve = E0 * v[0] + E1 * (v[1] + v[-1]) + E2 * (v[2] + v[-2]) + E3 * (v[3] + v[-3])
    return v[0] + c * slope + c2 * curve


def column_kernel(first, zonal, courant, mixing, inv, q, left, right, *rest):
    if first:
        state, gradient, x_low, x_high = rest
    else:
        before, state, gradient = rest
    step = pl.program_id(0)
    levels = inv.shape[0]
    lane = lax.broadcasted_iota(jnp.int32, (8, 128), 1)
    third = (lane & 3) == 2
    zeroth = (lane & 3) == 0
    middle = lane < 64

    def block(b, carry):
        ml = left[b].astype(f32)
        ml = ml + jnp.where(third, pltpu.roll(ml, 127, 1), 0.0)
        mr = right[b].astype(f32)
        mr = mr + jnp.where(zeroth, pltpu.roll(mr, 125, 1), 0.0)
        for l in range(LB):
            level = b * LB + l
            c = courant[level]
            c2 = 0.5 * c * c
            m = mixing[jnp.maximum(level - 1, 0)]
            iv = inv[level]
            after = []
            for t in range(4):
                i = t * LB + l
                x = zonal[t, level]
                halo = jnp.where(middle, turn(mr, -4 * i), turn(ml, 125 - 4 * i))
                v = {0: x}
                for k in (1, 2, 3):
                    v[-k] = pltpu.roll(jnp.where(lane >= 128 - k, halo, x), k, 1)
                    v[k] = pltpu.roll(jnp.where(lane < k, halo, x), 128 - k, 1)
                y = stencil(v, c, c2)
                y = (y + m * carry[t]) * iv
                state[t, level] = y
                after.append(y)
            carry = tuple(after)
        return carry

    carry = tuple(jnp.zeros((8, 128), f32) for _ in range(4))
    carry = lax.fori_loop(0, levels // LB, block, carry)

    def back(j, carry):
        level = levels - 2 - j
        qq = q[level]
        after = []
        for t in range(4):
            y = state[t, level] + qq * carry[t]
            state[t, level] = y
            after.append(y)
        return tuple(after)

    carry = lax.fori_loop(0, levels - 1, back, carry, unroll=4)
    for t in range(4):
        gradient[t] = carry[t] if first else before[t] + carry[t]
    if first:

        @pl.when(step == 0)
        def _():
            for t in range(4):
                rows = slice(72 * t, 72 * t + 72)
                x_low[0, rows], x_low[1, rows] = split(state[t, :, 0, :])
                x_low[2, rows] = state[t, :, 1, :].astype(bf16)
                x_low[3, rows] = state[t, :, 2, :].astype(bf16)

        @pl.when(step == pl.num_programs(0) - 1)
        def _():
            for t in range(4):
                rows = slice(72 * t, 72 * t + 72)
                x_high[0, rows], x_high[1, rows] = split(state[t, :, 7, :])
                x_high[2, rows] = state[t, :, 6, :].astype(bf16)
                x_high[3, rows] = state[t, :, 5, :].astype(bf16)


def cost(flops, size):
    return pl.CostEstimate(flops=flops, bytes_accessed=size, transcendentals=0)


def params(mib):
    return pltpu.CompilerParams(vmem_limit_bytes=mib * 2**20)


def shape(dims, kind=f32):
    return jax.ShapeDtypeStruct(dims, kind)


def whole(dims):
    return pl.BlockSpec(dims, lambda i: (0,) * len(dims))


def shift(value, axis, closed, forward):
    count = lax.axis_size(axis)
    ends = count if closed else count - 1
    pairs = [(i, (i + 1) % count) for i in range(ends)]
    if not forward:
        pairs = [(b, a) for a, b in pairs]
    return lax.ppermute(value, axis, pairs)


def local(adjoint_in, courant_x, courant_y, mixing, kernel_rows, tracer_weights, column_ids, counts):
    tracers, levels, lons, lats = adjoint_in.shape
    devices = lax.axis_size(("gx", "gy"))
    slots = kernel_rows.shape[1]
    fields = tracers * levels
    size = fields * lons * lats * 4

    packed = pl.pallas_call(
        pack_kernel,
        out_shape=shape((devices, 24, 128), bf16),
        in_specs=[pl.BlockSpec(memory_space=pltpu.SMEM), pl.BlockSpec(), pl.BlockSpec()],
        compiler_params=params(16),
        name="pack",
    )(counts, kernel_rows, tracer_weights)
    got = lax.all_to_all(packed, ("gx", "gy"), split_axis=0, concat_axis=0, tiled=True)

    inv, q = pl.pallas_call(
        factor_kernel,
        out_shape=[shape((levels, lons, lats))] * 2,
        compiler_params=params(16),
        cost_estimate=cost(30 * levels * lons * lats, 3 * levels * lons * lats * 4),
        name="factor",
    )(mixing)
    lat_range = jnp.arange(lats, dtype=jnp.int32)
    code = jnp.where(
        (column_ids % lats)[:, None] == lat_range[None, :], (column_ids // lats)[:, None], -1
    ).astype(bf16)

    edge = shape((4, fields, lats), bf16)
    state, x_low, x_high = pl.pallas_call(
        forcing_kernel,
        grid=(lons // 8,),
        in_specs=[
            whole((devices, 24, 128)),
            whole((slots, lats)),
            pl.BlockSpec((fields, 8, lats), lambda i: (0, i, 0)),
        ],
        out_specs=[
            pl.BlockSpec((fields, 8, lats), lambda i: (0, i, 0)),
            whole((4, fields, lats)),
            whole((4, fields, lats)),
        ],
        out_shape=[shape((fields, lons, lats)), edge, edge],
        scratch_shapes=[pltpu.VMEM((2 * fields, slots), bf16)],
        compiler_params=params(40),
        cost_estimate=cost(4 * fields * slots * lons * lats, 2 * size),
        name="forcing",
    )(got, code, adjoint_in.reshape(fields, lons, lats))

    for step in range(STEPS):
        from_left = shift(x_high, "gx", True, True)
        from_right = shift(x_low, "gx", True, False)
        blocks = levels // LB
        halo_spec = pl.BlockSpec((4, tracers, LB, lats), lambda b: (0, 0, b, 0))
        field_spec = pl.BlockSpec((tracers, LB, lons, lats), lambda b: (0, b, 0, 0))
        note_spec = pl.BlockSpec((1, lons, 128), lambda b: (b, 0, 0))
        zonal, to_left, to_right = pl.pallas_call(
            zonal_kernel,
            grid=(blocks,),
            in_specs=[
                field_spec,
                pl.BlockSpec((LB, lons, lats), lambda b: (b, 0, 0)),
                halo_spec,
                halo_spec,
            ],
            out_specs=[field_spec, note_spec, note_spec],
            out_shape=[
                shape((tracers, levels, lons, lats)),
                shape((blocks, lons, 128), bf16),
                shape((blocks, lons, 128), bf16),
            ],
            scratch_shapes=[pltpu.VMEM((tracers * LB * 48, lats), f32)],
            compiler_params=params(24),
            cost_estimate=cost(20 * size // 4, 2 * size),
            name="zonal",
        )(
            state.reshape(tracers, levels, lons, lats),
            courant_x,
            from_left.reshape(4, tracers, levels, lats),
            from_right.reshape(4, tracers, levels, lats),
        )
        y_left = shift(to_right, "gy", False, True)
        y_right = shift(to_left, "gy", False, False)
        first = step == 0
        field_spec = pl.BlockSpec((tracers, levels, 8, lats), lambda r: (0, 0, r, 0))
        level_spec = pl.BlockSpec((levels, 8, lats), lambda r: (0, r, 0))
        note_spec = pl.BlockSpec((blocks, 8, 128), lambda r: (0, r, 0))
        gradient_spec = pl.BlockSpec((tracers, 8, lats), lambda r: (0, r, 0))
        mixing_spec = pl.BlockSpec((levels - 1, 8, lats), lambda r: (0, r, 0))
        operands = [zonal, courant_y, mixing, inv, q, y_left, y_right]
        in_specs = [field_spec, level_spec, mixing_spec, level_spec, level_spec, note_spec, note_spec]
        out_specs = [field_spec, gradient_spec]
        out_shape = [shape((tracers, levels, lons, lats)), shape((tracers, lons, lats))]
        if first:
            out_specs += [whole((4, fields, lats))] * 2
            out_shape += [edge, edge]
        else:
            operands.append(gradient)
            in_specs.append(gradient_spec)

        def kernel(*refs, first=first):
            column_kernel(first, *refs)

        out = pl.pallas_call(
            kernel,
            grid=(lons // 8,),
            in_specs=in_specs,
            out_specs=out_specs,
            out_shape=out_shape,
            compiler_params=params(32),
            cost_estimate=cost(40 * size // 4, 2 * size),
            name="column",
        )(*operands)
        if first:
            state, gradient, x_low, x_high = out
        else:
            state, gradient = out
    return state, gradient


def solution(mesh):
    in_specs = (
        P(None, None, "gx", "gy"),
        P(None, "gx", "gy"),
        P(None, "gx", "gy"),
        P(None, "gx", "gy"),
        P(None, ("gx", "gy")),
        P(None, ("gx", "gy")),
        P(("gx", "gy")),
        P(("gx", "gy"), None),
    )
    out_specs = (P(None, None, "gx", "gy"), P(None, "gx", "gy"))
    return jax.shard_map(local, mesh=mesh, in_specs=in_specs, out_specs=out_specs, check_vma=False)
```

time: 425 us -> 193 us (0.45)
  the two profiles are of different devices: /device:TPU:64 before, /device:TPU:24 now
where the time goes in v1:
time: 193 us
  Pallas kernels  119 us (62%)
  waiting for transfers between devices  35.2 us (18%)
  starting transfers between devices  31.1 us (16%)
  local copies, waits for them, and re-layouts  4.82 us (2%)
    pallas_call x2, Pallas kernels, local(): pl.pallas_call(kernel, grid=(lons // 8,), in_specs=in_specs, out_specs=ou...  68.2 us
    pallas_call x1, Pallas kernels, local(): pl.pallas_call(forcing_kernel, grid=(lons // 8,), in_specs=[whole((device...  32.9 us
    ppermute x8, waiting for transfers between devices, shift(): return lax.ppermute(value, axis, pairs)  21.8 us
    ppermute x8, starting transfers between devices, shift(): return lax.ppermute(value, axis, pairs)  20.8 us
    all_to_all x1, waiting for transfers between devices, local(): lax.all_to_all(packed, ('gx', 'gy'), split_axis=0, concat_axis=0, tiled=T...  13.4 us
    pallas_call x2, Pallas kernels, local(): pl.pallas_call(zonal_kernel, grid=(blocks,), in_specs=[field_spec, pl.Blo...  13.1 us
    all_to_all x1, starting transfers between devices, local(): lax.all_to_all(packed, ('gx', 'gy'), split_axis=0, concat_axis=0, tiled=T...  10.3 us
    unnamed x16, local copies, waits for them, and re-layouts  4.82 us
  transfers between devices with their start and end apart: 9, of which 6 were waited for; matrix products, arithmetic and copies ran while one was open for 1% of the time, Pallas kernels for 0%

profile of v1, /device:TPU:24, one launch (start us, length us, event | category | flops | bytes accessed | tf_op | source)
XLA Modules:
  0.0 192.5 jit_solution(12888651001028418892)
XLA Ops:
  0.6 0.0 copy-start.3
  0.6 1.1 copy-done.3
  1.7 0.8 copy-done.4
  2.5 0.7 copy-done.5
  3.1 4.1 %pack.1 = bf16[128,24,128]{2,1,0:T(8,128)(2,1)} custom-call(s32[1,128]{1,0:T(1,128)S(1)} %copy-done.5, bf16[72,4096]{1,0:T(8,128)(2,1)S(1)} %copy-done.3, bf16[4,4096]{1,0:T(4,128)(2,1)S(1)} %copy-done.4), custom_call_target="tpu_custom_call" | custom-call | tf_op jit(solution)/shard_map/pack/pallas_call | solution.py:293
  7.2 10.3 %all-to-all-start = ((bf16[128,24,128]{2,1,0:T(8,128)(2,1)}), bf16[128,24,128]{2,1,0:T(8,128)(2,1)S(1)}, u32[]{:S(2)}, u32[]{:S(2)}) async-start(bf16[128,24,128]{2,1,0:T(8,128)(2,1)} %pack.1), calls=%async_computation | async-start | bytes 1572864 | tf_op jit(solution)/shard_map/all_to_all | solution.py:300
  17.5 1.4 select_convert_fusion.code
  18.9 13.4 %all-to-all-done.got = bf16[128,24,128]{2,1,0:T(8,128)(2,1)S(1)} async-done(((bf16[128,24,128]{2,1,0:T(8,128)(2,1)}), bf16[128,24,128]{2,1,0:T(8,128)(2,1)S(1)}, u32[]{:S(2)}, u32[]{:S(2)}) %all-to-all-start) | async-done | bytes 786464 | tf_op jit(solution)/shard_map/all_to_all | solution.py:300
  32.3 2.3 %copy-done.6 = f32[4,72,32,128]{3,2,1,0:T(8,128)S(1)} copy-done((f32[4,72,32,128]{3,2,1,0:T(8,128)S(1)}, f32[4,72,32,128]{3,2,1,0:T(8,128)}, u32[]{:S(2)}) %copy-start.6) | copy-done | bytes 4718616
  34.7 32.9 %forcing.1 = (f32[288,32,128]{2,1,0:T(8,128)S(1)}, bf16[4,288,128]{2,1,0:T(8,128)(2,1)S(1)}, bf16[4,288,128]{2,1,0:T(8,128)(2,1)S(1)}) custom-call(bf16[128,24,128]{2,1,0:T(8,128)(2,1)S(1)} %all-to-all-done.got, bf16[4096,128]{1,0:T(8,128)(2,1)S(1)} %select_convert_fusion.code, f32[288,32,128]{2,1,0:T(8,128)S(1)} %bitcast.11), custom_call_target="tpu_custom_call" | custom-call | flops 19327352832 | bytes 9437184 | tf_op jit(solution)/shard_map/forcing/pallas_call | solution.py:315
  67.6 0.1 collective-permute-start
  67.6 3.8 %collective-permute-start.1 = (bf16[4,288,128]{2,1,0:T(8,128)(2,1)S(1)}, bf16[4,288,128]{2,1,0:T(8,128)(2,1)S(1)}, u32[]{:S(2)}, u32[]{:S(2)}) collective-permute-start(bf16[4,288,128]{2,1,0:T(8,128)(2,1)S(1)} %get-tuple-element.19), channel_id=1, source_target_pairs={{8,0},{16,8},{24,16},{32,24},{40,32},{48,40},{56,48},{64,56},{72,6... | collective-permute-start | bytes 884744 | tf_op jit(solution)/shard_map/ppermute | solution.py:283
  71.5 4.4 %collective-permute-done = bf16[4,288,128]{2,1,0:T(8,128)(2,1)S(1)} collective-permute-done((bf16[4,288,128]{2,1,0:T(8,128)(2,1)S(1)}, bf16[4,288,128]{2,1,0:T(8,128)(2,1)S(1)}, u32[]{:S(2)}, u32[]{:S(2)}) %collective-permute-start) | collective-permute-done | bytes 294944 | tf_op jit(solution)/shard_map/ppermute | solution.py:283
  75.9 0.0 collective-permute-done.1
  75.9 0.0 copy-start.1
  75.9 6.6 %zonal.2 = (f32[4,72,32,128]{3,2,1,0:T(8,128)S(1)}, bf16[9,32,128]{2,1,0:T(8,128)(2,1)S(1)}, bf16[9,32,128]{2,1,0:T(8,128)(2,1)S(1)}) custom-call(f32[4,72,32,128]{3,2,1,0:T(8,128)S(1)} %bitcast.6, f32[72,32,128]{2,1,0:T(8,128)S(1)} %copy-done.2, bf16[4,4,72,128]{3,2,1,0:T(8,128)(2,1)S(1)} %bitcast.7, bf16[4,4,72,128]{3,2,1,0:T(8,128)(2,1)S(1)} %bitcast.9), custom_call_target="tpu_custom_call" | custom-call | flops 23592960 | bytes 9437184 | tf_op jit(solution)/shard_map/zonal/pallas_call | solution.py:342
  82.5 5.2 %collective-permute-start.2 = (bf16[9,32,128]{2,1,0:T(8,128)(2,1)S(1)}, bf16[9,32,128]{2,1,0:T(8,128)(2,1)S(1)}, u32[]{:S(2)}, u32[]{:S(2)}) collective-permute-start(bf16[9,32,128]{2,1,0:T(8,128)(2,1)S(1)} %get-tuple-element.23), channel_id=1, source_target_pairs={{0,1},{1,2},{2,3},{3,4},{4,5},{5,6},{6,7},{8,9},{9,10},{10,11},{11... | collective-permute-start | bytes 221192 | tf_op jit(solution)/shard_map/ppermute | solution.py:283
  87.7 1.9 collective-permute-start.3
  89.7 0.9 factor.1
  90.6 0.0 collective-permute-done.2.refs_5_
  90.6 7.0 %collective-permute-done.3.refs_6_ = bf16[9,32,128]{2,1,0:T(8,128)(2,1)S(1)} collective-permute-done((bf16[9,32,128]{2,1,0:T(8,128)(2,1)S(1)}, bf16[9,32,128]{2,1,0:T(8,128)(2,1)S(1)}, u32[]{:S(2)}, u32[]{:S(2)}) %collective-permute-start.3) | collective-permute-done | bytes 73760 | tf_op jit(solution)/shard_map/ppermute | solution.py:283
  97.6 34.6 %column.2 = (f32[4,72,32,128]{3,2,1,0:T(8,128)S(1)}, f32[4,32,128]{2,1,0:T(8,128)S(1)}, bf16[4,288,128]{2,1,0:T(8,128)(2,1)S(1)}, bf16[4,288,128]{2,1,0:T(8,128)(2,1)S(1)}) custom-call(f32[4,72,32,128]{3,2,1,0:T(8,128)S(1)} %get-tuple-element.20.refs_0_, f32[72,32,128]{2,1,0:T(8,128)S(1)} %copy-done.1, f32[71,32,128]{2,1,0:T(8,128)S(1)} %copy-done, ...), custom_call_target="tpu_custom_call" | custom-call | flops 47185920 | bytes 9437184 | tf_op jit(solution)/shard_map/column/pallas_call | solution.py:389
  132.2 0.1 collective-permute-start.4
  132.3 3.8 %collective-permute-start.5 = (bf16[4,288,128]{2,1,0:T(8,128)(2,1)S(1)}, bf16[4,288,128]{2,1,0:T(8,128)(2,1)S(1)}, u32[]{:S(2)}, u32[]{:S(2)}) collective-permute-start(bf16[4,288,128]{2,1,0:T(8,128)(2,1)S(1)} %get-tuple-element.27), channel_id=1, source_target_pairs={{8,0},{16,8},{24,16},{32,24},{40,32},{48,40},{56,48},{64,56},{72,6... | collective-permute-start | bytes 884744 | tf_op jit(solution)/shard_map/ppermute | solution.py:283
  136.1 4.4 %collective-permute-done.4 = bf16[4,288,128]{2,1,0:T(8,128)(2,1)S(1)} collective-permute-done((bf16[4,288,128]{2,1,0:T(8,128)(2,1)S(1)}, bf16[4,288,128]{2,1,0:T(8,128)(2,1)S(1)}, u32[]{:S(2)}, u32[]{:S(2)}) %collective-permute-start.4) | collective-permute-done | bytes 294944 | tf_op jit(solution)/shard_map/ppermute | solution.py:283
  140.5 0.0 collective-permute-done.5
  140.5 6.5 %zonal.3 = (f32[4,72,32,128]{3,2,1,0:T(8,128)S(1)}, bf16[9,32,128]{2,1,0:T(8,128)(2,1)S(1)}, bf16[9,32,128]{2,1,0:T(8,128)(2,1)S(1)}) custom-call(f32[4,72,32,128]{3,2,1,0:T(8,128)S(1)} %get-tuple-element.25.state, f32[72,32,128]{2,1,0:T(8,128)S(1)} %copy-done.2, bf16[4,4,72,128]{3,2,1,0:T(8,128)(2,1)S(1)} %bitcast.8, bf16[4,4,72,128]{3,2,1,0:T(8,128)(2,1)S(1)} %bitcast.10), custom_call_target="tpu_custom_call" | custom-call | flops 23592960 | bytes 9437184 | tf_op jit(solution)/shard_map/zonal/pallas_call | solution.py:342
  147.1 1.9 collective-permute-start.6
  149.0 3.9 %collective-permute-start.7 = (bf16[9,32,128]{2,1,0:T(8,128)(2,1)S(1)}, bf16[9,32,128]{2,1,0:T(8,128)(2,1)S(1)}, u32[]{:S(2)}, u32[]{:S(2)}) collective-permute-start(bf16[9,32,128]{2,1,0:T(8,128)(2,1)S(1)} %get-tuple-element.30), channel_id=1, source_target_pairs={{1,0},{2,1},{3,2},{4,3},{5,4},{6,5},{7,6},{9,8},{10,9},{11,10},{12... | collective-permute-start | bytes 221192 | tf_op jit(solution)/shard_map/ppermute | solution.py:283
  152.9 0.4 collective-permute-done.6.refs_5_
  153.3 5.5 %collective-permute-done.7.refs_6_ = bf16[9,32,128]{2,1,0:T(8,128)(2,1)S(1)} collective-permute-done((bf16[9,32,128]{2,1,0:T(8,128)(2,1)S(1)}, bf16[9,32,128]{2,1,0:T(8,128)(2,1)S(1)}, u32[]{:S(2)}, u32[]{:S(2)}) %collective-permute-start.7) | collective-permute-done | bytes 73760 | tf_op jit(solution)/shard_map/ppermute | solution.py:283
  158.9 33.7 %column.3 = (f32[4,72,32,128]{3,2,1,0:T(8,128)}, f32[4,32,128]{2,1,0:T(8,128)}) custom-call(f32[4,72,32,128]{3,2,1,0:T(8,128)S(1)} %get-tuple-element.28.refs_0_, f32[72,32,128]{2,1,0:T(8,128)S(1)} %copy-done.1, f32[71,32,128]{2,1,0:T(8,128)S(1)} %copy-done, f32[72,32,128]{2,1,0:T(8,128)S(1)} %get-tuple-element.21.refs_3_, ...), custom_call_target="tpu_custom_call" | custom-call | flops 47185920 | bytes 9437184 | tf_op jit(solution)/shard_map/column/pallas_call | solution.py:389
  (11 shorter events, 0.0 us)
Async XLA Ops:
  0.6 1.1 copy-start.3
  1.7 0.8 copy-start.4
  2.5 0.7 copy-start.5
  3.1 14.4 %copy-start.7 = (s32[4096]{0:T(1024)S(1)}, s32[4096]{0:T(1024)}, u32[]{:S(2)}) copy-start(s32[4096]{0:T(1024)} %param.14) | copy-start | bytes 49156
  7.2 25.1 %all-to-all-start = ((bf16[128,24,128]{2,1,0:T(8,128)(2,1)}), bf16[128,24,128]{2,1,0:T(8,128)(2,1)S(1)}, u32[]{:S(2)}, u32[]{:S(2)}) async-start(bf16[128,24,128]{2,1,0:T(8,128)(2,1)} %pack.1), calls=%async_computation | async-start | bytes 1572864 | tf_op jit(solution)/shard_map/all_to_all | solution.py:300
  32.3 2.3 %copy-start.6 = (f32[4,72,32,128]{3,2,1,0:T(8,128)S(1)}, f32[4,72,32,128]{3,2,1,0:T(8,128)}, u32[]{:S(2)}) copy-start(f32[4,72,32,128]{3,2,1,0:T(8,128)} %param.8) | copy-start | bytes 14155780
  34.7 41.2 %copy-start.2 = (f32[72,32,128]{2,1,0:T(8,128)S(1)}, f32[72,32,128]{2,1,0:T(8,128)}, u32[]{:S(2)}) copy-start(f32[72,32,128]{2,1,0:T(8,128)} %courant.3) | copy-start | bytes 3538948
  67.6 8.3 %collective-permute-start = (bf16[4,288,128]{2,1,0:T(8,128)(2,1)S(1)}, bf16[4,288,128]{2,1,0:T(8,128)(2,1)S(1)}, u32[]{:S(2)}, u32[]{:S(2)}) collective-permute-start(bf16[4,288,128]{2,1,0:T(8,128)(2,1)S(1)} %get-tuple-element.18), channel_id=1, source_target_pairs={{0,8},{8,16},{16,24},{24,32},{32,40},{40,48},{48,56},{56,64},{64,7... | collective-permute-start | bytes 884744 | tf_op jit(solution)/shard_map/ppermute | solution.py:283
  67.6 8.2 %collective-permute-start.1 = (bf16[4,288,128]{2,1,0:T(8,128)(2,1)S(1)}, bf16[4,288,128]{2,1,0:T(8,128)(2,1)S(1)}, u32[]{:S(2)}, u32[]{:S(2)}) collective-permute-start(bf16[4,288,128]{2,1,0:T(8,128)(2,1)S(1)} %get-tuple-element.19), channel_id=1, source_target_pairs={{8,0},{16,8},{24,16},{32,24},{40,32},{48,40},{56,48},{64,56},{72,6... | collective-permute-start | bytes 884744 | tf_op jit(solution)/shard_map/ppermute | solution.py:283
  75.9 13.8 %copy-start = (f32[71,32,128]{2,1,0:T(8,128)S(1)}, f32[71,32,128]{2,1,0:T(8,128)}, u32[]{:S(2)}) copy-start(f32[71,32,128]{2,1,0:T(8,128)} %refs_2_.3) | copy-start | bytes 3489796
  75.9 21.7 %copy-start.1 = (f32[72,32,128]{2,1,0:T(8,128)S(1)}, f32[72,32,128]{2,1,0:T(8,128)}, u32[]{:S(2)}) copy-start(f32[72,32,128]{2,1,0:T(8,128)} %refs_1_.3) | copy-start | bytes 3538948
  82.5 8.1 %collective-permute-start.2 = (bf16[9,32,128]{2,1,0:T(8,128)(2,1)S(1)}, bf16[9,32,128]{2,1,0:T(8,128)(2,1)S(1)}, u32[]{:S(2)}, u32[]{:S(2)}) collective-permute-start(bf16[9,32,128]{2,1,0:T(8,128)(2,1)S(1)} %get-tuple-element.23), channel_id=1, source_target_pairs={{0,1},{1,2},{2,3},{3,4},{4,5},{5,6},{6,7},{8,9},{9,10},{10,11},{11... | collective-permute-start | bytes 221192 | tf_op jit(solution)/shard_map/ppermute | solution.py:283
  87.7 9.9 %collective-permute-start.3 = (bf16[9,32,128]{2,1,0:T(8,128)(2,1)S(1)}, bf16[9,32,128]{2,1,0:T(8,128)(2,1)S(1)}, u32[]{:S(2)}, u32[]{:S(2)}) collective-permute-start(bf16[9,32,128]{2,1,0:T(8,128)(2,1)S(1)} %get-tuple-element.24), channel_id=1, source_target_pairs={{1,0},{2,1},{3,2},{4,3},{5,4},{6,5},{7,6},{9,8},{10,9},{11,10},{12... | collective-permute-start | bytes 221192 | tf_op jit(solution)/shard_map/ppermute | solution.py:283
  132.2 8.3 %collective-permute-start.4 = (bf16[4,288,128]{2,1,0:T(8,128)(2,1)S(1)}, bf16[4,288,128]{2,1,0:T(8,128)(2,1)S(1)}, u32[]{:S(2)}, u32[]{:S(2)}) collective-permute-start(bf16[4,288,128]{2,1,0:T(8,128)(2,1)S(1)} %get-tuple-element.26), channel_id=1, source_target_pairs={{0,8},{8,16},{16,24},{24,32},{32,40},{40,48},{48,56},{56,64},{64,7... | collective-permute-start | bytes 884744 | tf_op jit(solution)/shard_map/ppermute | solution.py:283
  132.3 8.2 %collective-permute-start.5 = (bf16[4,288,128]{2,1,0:T(8,128)(2,1)S(1)}, bf16[4,288,128]{2,1,0:T(8,128)(2,1)S(1)}, u32[]{:S(2)}, u32[]{:S(2)}) collective-permute-start(bf16[4,288,128]{2,1,0:T(8,128)(2,1)S(1)} %get-tuple-element.27), channel_id=1, source_target_pairs={{8,0},{16,8},{24,16},{32,24},{40,32},{48,40},{56,48},{64,56},{72,6... | collective-permute-start | bytes 884744 | tf_op jit(solution)/shard_map/ppermute | solution.py:283
  147.1 6.2 %collective-permute-start.6 = (bf16[9,32,128]{2,1,0:T(8,128)(2,1)S(1)}, bf16[9,32,128]{2,1,0:T(8,128)(2,1)S(1)}, u32[]{:S(2)}, u32[]{:S(2)}) collective-permute-start(bf16[9,32,128]{2,1,0:T(8,128)(2,1)S(1)} %get-tuple-element.29), channel_id=1, source_target_pairs={{0,1},{1,2},{2,3},{3,4},{4,5},{5,6},{6,7},{8,9},{9,10},{10,11},{11... | collective-permute-start | bytes 221192 | tf_op jit(solution)/shard_map/ppermute | solution.py:283
  149.0 9.9 %collective-permute-start.7 = (bf16[9,32,128]{2,1,0:T(8,128)(2,1)S(1)}, bf16[9,32,128]{2,1,0:T(8,128)(2,1)S(1)}, u32[]{:S(2)}, u32[]{:S(2)}) collective-permute-start(bf16[9,32,128]{2,1,0:T(8,128)(2,1)S(1)} %get-tuple-element.30), channel_id=1, source_target_pairs={{1,0},{2,1},{3,2},{4,3},{5,4},{6,5},{7,6},{9,8},{10,9},{11,10},{12... | collective-permute-start | bytes 221192 | tf_op jit(solution)/shard_map/ppermute | solution.py:283

commit v2 on v1

v2 whole, which is shorter than its diff:
```python
import jax
import jax.numpy as jnp
import numpy as np
from jax import lax
from jax.experimental import pallas as pl
from jax.experimental.pallas import tpu as pltpu
from jax.sharding import PartitionSpec as P

STEPS = 2
LB = 8
CHUNK = 1024

D1, D2, D3 = 0.75, -0.15, 1.0 / 60.0
E1, E2, E3 = 1.5, -0.15, 1.0 / 90.0
E0 = -49.0 / 18.0

f32 = jnp.float32
bf16 = jnp.bfloat16


def fill_swap(table):
    row = lax.broadcasted_iota(jnp.int32, table.shape, 0)
    col = lax.broadcasted_iota(jnp.int32, table.shape, 1)
    want = ((col >> 5) & 3) * 128 + (col >> 7) * 32 + (col & 31)
    table[...] = jnp.where(row == want, 1.0, 0.0).astype(bf16)


def split(value):
    hi = value.astype(bf16)
    return hi, (value - hi.astype(f32)).astype(bf16)


def pack_kernel(counts, rows, weights, out, swap):
    step = pl.program_id(0)
    groups = rows.shape[1] // 128

    @pl.when(step == 0)
    def _():
        fill_swap(swap)

    lane = lax.broadcasted_iota(jnp.int32, (24, 128), 1)
    block = lane >> 5
    columns = [[] for _ in range(4)]
    for g in range(groups):
        lanes = slice(g * 128, g * 128 + 128)
        first = 4 * (step * groups + g)
        limit = jnp.where(
            block < 2,
            jnp.where(block == 0, counts[0, first], counts[0, first + 1]),
            jnp.where(block == 2, counts[0, first + 2], counts[0, first + 3]),
        )
        live = (lane & 31) < limit
        for q in range(3):
            columns[q].append(jnp.where(live, rows[24 * q : 24 * q + 24, lanes].astype(f32), 0.0))
        columns[3].append(jnp.concatenate([weights[:, lanes].astype(f32), jnp.zeros((20, 128), f32)], axis=0))
    wide = jnp.concatenate([jnp.concatenate(c, axis=0).astype(bf16) for c in columns], axis=1)
    moved = jnp.dot(wide, swap[...], preferred_element_type=f32)
    for g in range(groups):
        for i in range(4):
            out[4 * g + i] = moved[24 * g : 24 * g + 24, 128 * i : 128 * i + 128].astype(bf16)


def factor_kernel(mixing, inv_out, q_out):
    levels = inv_out.shape[0]
    top = mixing[0]
    inv = 1.0 / (1.0 + top)
    q = top * inv
    inv_out[0] = inv
    q_out[0] = q

    def level(l, carry):
        below, q = carry
        above = mixing[l]
        inv = 1.0 / (1.0 + below + above - below * q)
        q = above * inv
        inv_out[l] = inv
        q_out[l] = q
        return above, q

    below, q = lax.fori_loop(1, levels - 1, level, (top, q))
    inv_out[levels - 1] = 1.0 / (1.0 + below - below * q)
    q_out[levels - 1] = jnp.zeros_like(q)


def rank_kernel(bins, code, starts):
    piece = 256
    lane = lax.broadcasted_iota(jnp.int32, (piece, 128), 1)
    lane_f = lane.astype(f32)
    upto = (lax.broadcasted_iota(jnp.int32, (piece, piece), 1) <= lax.broadcasted_iota(jnp.int32, (piece, piece), 0))
    upto = jnp.where(upto, 1.0, 0.0).astype(bf16)
    row2 = lax.broadcasted_iota(jnp.int32, (256, 256), 0)
    col2 = lax.broadcasted_iota(jnp.int32, (256, 256), 1)
    spread = jnp.where((row2 >> 7) == (col2 >> 7), 1.0, 0.0).astype(bf16)
    ones = jnp.ones((8, CHUNK), bf16)
    for h in range(bins.shape[0] // CHUNK):
        own = bins[h * CHUNK : (h + 1) * CHUNK, :].astype(f32)
        wide = lax.broadcasted_iota(jnp.int32, own.shape, 1).astype(f32)
        below = jnp.where(own < wide, 1.0, 0.0).astype(bf16)
        start = jnp.dot(ones, below, preferred_element_type=f32)
        starts[8 * h : 8 * h + 8, :] = start.astype(jnp.int32)
        running = start[0:1, :] - 1.0
        for p in range(CHUNK // piece):
            at = slice(p * piece, p * piece + piece)
            mine = own[at] == lane_f
            one_hot = jnp.where(mine, 1.0, 0.0)
            place = jnp.dot(upto, one_hot.astype(bf16), preferred_element_type=f32) + running
            running = place[piece - 1 : piece, :]
            place = jnp.where(mine, place, 0.0)
            high = jnp.floor(place * (1.0 / 128.0))
            low = place - 128.0 * high
            both = jnp.dot(
                jnp.concatenate([high.astype(bf16), low.astype(bf16)], axis=1), spread, preferred_element_type=f32
            )
            found = jnp.where(both[:, 128:] == lane_f, both[:, :128], -1.0)
            code[h * CHUNK + p * piece : h * CHUNK + (p + 1) * piece, :] = found.astype(bf16)


def order_kernel(got, ids, code, lhs, places, swap, raw):
    half = lhs.shape[0] // 2
    slots = lhs.shape[1]
    fill_swap(swap)
    batch = 8
    for first in range(0, slots // 128, batch):
        wide = jnp.concatenate(
            [
                jnp.concatenate([got[4 * (first + g) + i].astype(f32) for g in range(batch)], axis=0).astype(bf16)
                for i in range(4)
            ],
            axis=1,
        )
        moved = jnp.dot(wide, swap[...], preferred_element_type=f32)
        for g in range(batch):
            lanes = slice((first + g) * 128, (first + g) * 128 + 128)
            for q in range(4):
                count = 24 if q < 3 else 8
                raw[24 * q : 24 * q + count, lanes] = moved[24 * g : 24 * g + count, 128 * q : 128 * q + 128]
    cells = ids[...]
    raw[76:77, :] = (cells & 127).astype(f32)
    raw[77:78, :] = (cells >> 7).astype(f32)
    one, zero = jnp.ones((), bf16), jnp.zeros((), bf16)
    for h in range(slots // CHUNK):
        block = raw[:, h * CHUNK : (h + 1) * CHUNK].astype(bf16)
        part = code[h * CHUNK : (h + 1) * CHUNK, :]
        for p in range(CHUNK // 256):
            one_hot = jnp.concatenate(
                [jnp.where(part == jnp.asarray(2 * p + a, bf16), one, zero) for a in range(2)], axis=1
            )
            done = jnp.dot(block, one_hot, preferred_element_type=f32)
            lanes = slice(h * CHUNK + p * 256, h * CHUNK + (p + 1) * 256)
            places[:, lanes] = done[72:80, :]
            for t in range(4):
                hi, lo = split(done[:72] * done[72 + t : 73 + t, :])
                lhs[72 * t : 72 * t + 72, lanes] = hi
                lhs[half + 72 * t : half + 72 * t + 72, lanes] = lo


def forcing_kernel(starts, lhs, places, adjoint, state, x_low, x_high, total):
    step = pl.program_id(0)
    half = lhs.shape[0] // 2
    chunks = lhs.shape[1] // CHUNK
    row = lax.broadcasted_iota(jnp.int32, (128, 256), 0).astype(f32)

    def placed(at, lon):
        lat = places[4:5, pl.ds(at, 256)]
        slot_lon = places[5:6, pl.ds(at, 256)]
        return jnp.concatenate(
            [
                jnp.where(jnp.where(slot_lon == (lon + a).astype(f32), lat, -1.0) == row, 1.0, 0.0).astype(bf16)
                for a in range(2)
            ],
            axis=0,
        )

    def product(at, lon):
        return lax.dot_general(
            lhs[:, pl.ds(at, 256)], placed(at, lon), (((1,), (1,)), ((), ())), preferred_element_type=f32
        )

    for pair in range(4):
        lon = step * 8 + 2 * pair
        number = step * 4 + pair
        result = None
        limits = []
        for h in range(chunks):
            low = starts[8 * h, number]
            high = starts[8 * h, number + 1]
            first = jnp.minimum(low >> 7, CHUNK // 128 - 2)
            tiles = (high + 127) >> 7
            limits.append((first, tiles))
            at = pl.multiple_of(h * CHUNK + first * 128, 128)
            piece = product(at, lon)
            result = piece if result is None else result + piece
        total[...] = result
        for h, (first, tiles) in enumerate(limits):

            def more(j, _, h=h, first=first, lon=lon):
                at = first + 2 + 2 * j
                start = jnp.minimum(at, CHUNK // 128 - 2)
                fresh = lax.broadcasted_iota(jnp.int32, (1, 256), 1) >= (at - start) * 128
                base = pl.multiple_of(h * CHUNK + start * 128, 128)
                one_hot = jnp.where(fresh, placed(base, lon).astype(f32), 0.0).astype(bf16)
                total[...] += lax.dot_general(
                    lhs[:, pl.ds(base, 256)], one_hot, (((1,), (1,)), ((), ())), preferred_element_type=f32
                )
                return 0

            lax.fori_loop(0, jnp.maximum(tiles - first - 1, 0) >> 1, more, 0)
        for a in range(2):
            lanes = slice(128 * a, 128 * a + 128)
            state[:, 2 * pair + a, :] = adjoint[:, 2 * pair + a, :] + (total[:half, lanes] + total[half:, lanes])

    @pl.when(step == 0)
    def _():
        low_edge(state, x_low)

    @pl.when(step == pl.num_programs(0) - 1)
    def _():
        high_edge(state, x_high)


def low_edge(state, out):
    out[0], out[1] = split(state[:, 0, :])
    out[2] = state[:, 1, :].astype(bf16)
    out[3] = state[:, 2, :].astype(bf16)


def high_edge(state, out):
    out[0], out[1] = split(state[:, 7, :])
    out[2] = state[:, 6, :].astype(bf16)
    out[3] = state[:, 5, :].astype(bf16)


def zonal_kernel(state, courant, left, right, spread, zonal, to_left, to_right, pad, halves):
    lane = lax.broadcasted_iota(jnp.int32, (32, 128), 1)
    group = lane >> 2
    for t in range(4):
        base = t * LB * 48
        for where, halo in ((0, left), (1, right)):
            near = halo[0, t].astype(f32) + halo[1, t].astype(f32)
            for k, value in enumerate((near, halo[2, t].astype(f32), halo[3, t].astype(f32))):
                row = base + (7 - k if where == 0 else 40 + k)
                pad[pl.ds(row, LB, stride=48), :] = value
        for l in range(LB):
            pad[base + 48 * l + 8 : base + 48 * l + 40, :] = state[t, l]
    notes = [jnp.zeros((32, 128), f32)] * 2
    for t in range(4):
        for l in range(LB):
            c = courant[l]
            base = (t * LB + l) * 48 + 8
            out = stencil({k: pad[base + k : base + k + 32, :] for k in range(-3, 4)}, c, 0.5 * c * c)
            zonal[t, l] = out
            i = t * LB + l
            at = slice(32 * i, 32 * i + 32)
            halves[at, 0:128], halves[at, 128:256] = split(out)
        at = slice(32 * LB * t, 32 * LB * (t + 1))
        edges = jnp.dot(halves[at, :], spread[...], preferred_element_type=f32)
        for l in range(LB):
            mine = group == t * LB + l
            rows = slice(32 * l, 32 * l + 32)
            notes = [jnp.where(mine, edges[rows, 128 * n : 128 * n + 128], notes[n]) for n in range(2)]
    to_left[0] = notes[0].astype(bf16)
    to_right[0] = notes[1].astype(bf16)


def stencil(v, c, c2):
    slope = D1 * (v[1] - v[-1]) + D2 * (v[2] - v[-2]) + D3 * (v[3] - v[-3])
    curve = E0 * v[0] + E1 * (v[1] + v[-1]) + E2 * (v[2] + v[-2]) + E3 * (v[3] + v[-3])
    return v[0] + c * slope + c2 * curve


def column_kernel(first, zonal, courant, mixing, inv, q, left, right, weights, *rest):
    lhs = rest[-1]
    if first:
        state, gradient, x_low, x_high = rest[:-1]
    else:
        before, state, gradient = rest[:-1]
    step = pl.program_id(0)
    levels = inv.shape[0]
    rows = 32
    lane = lax.broadcasted_iota(jnp.int32, (rows, 128), 1)
    row = lax.broadcasted_iota(jnp.int32, (rows, 128), 0)
    owner = ((lane >> 2) - (row >> 3) * LB).astype(f32).astype(bf16)
    zero = jnp.zeros((), bf16)
    carry = None
    for b in range(levels // LB):
        notes = [jnp.concatenate([side[b].astype(f32)] * 4, axis=0).astype(bf16) for side in (left, right)]
        for l in range(LB):
            level = b * LB + l
            at = slice(level * rows, level * rows + rows)
            hi, lo = split(zonal[:, level].reshape(rows, 128))
            lhs[at, 0:128] = hi
            lhs[at, 128:256] = lo
            mine = owner == jnp.asarray(l, bf16)
            lhs[at, 256:384] = jnp.where(mine, notes[0], zero)
            lhs[at, 384:512] = jnp.where(mine, notes[1], zero)
        both = jnp.dot(
            lhs[b * LB * rows : (b + 1) * LB * rows, :], weights[...], preferred_element_type=f32
        )
        for l in range(LB):
            level = b * LB + l
            c = courant[level]
            c1 = c * (1.0 / 60.0)
            c2 = c * c * (1.0 / 360.0)
            part = both[l * rows : l * rows + rows].reshape(4, 8, 256)
            y = zonal[:, level] + c1 * part[:, :, :128] + c2 * part[:, :, 128:]
            if level > 0:
                y = y + mixing[level - 1] * carry
            carry = y * inv[level]
            state[:, level] = carry

    def back(j, carry):
        level = levels - 2 - j
        carry = state[:, level] + q[level] * carry
        state[:, level] = carry
        return carry

    carry = lax.fori_loop(0, levels - 1, back, carry, unroll=8)
    gradient[...] = carry if first else before[...] + carry
    if first:

        @pl.when(step == 0)
        def _():
            for t in range(4):
                rows = slice(72 * t, 72 * t + 72)
                x_low[0, rows], x_low[1, rows] = split(state[t, :, 0, :])
                x_low[2, rows] = state[t, :, 1, :].astype(bf16)
                x_low[3, rows] = state[t, :, 2, :].astype(bf16)

        @pl.when(step == pl.num_programs(0) - 1)
        def _():
            for t in range(4):
                rows = slice(72 * t, 72 * t + 72)
                x_high[0, rows], x_high[1, rows] = split(state[t, :, 7, :])
                x_high[2, rows] = state[t, :, 6, :].astype(bf16)
                x_high[3, rows] = state[t, :, 5, :].astype(bf16)


def edge_weights():
    table = np.zeros((256, 256), np.float32)
    for lane in range(128):
        part = lane % 4
        table[(128, part)[part < 3], lane] = 1
        table[(255, 125 + part)[part < 3], 128 + lane] = 1
    return table


def lat_weights():
    first = {1: 45, 2: -9, 3: 1}
    second = {0: -490, 1: 270, 2: -27, 3: 2}
    table = np.zeros((512, 256), np.float32)

    def fill(row, place):
        for out in range(128):
            k = place - out
            if abs(k) <= 3:
                table[row, out] = first.get(abs(k), 0) * (1 if k > 0 else -1)
                table[row, 128 + out] = second[abs(k)]

    for lane in range(128):
        fill(lane, lane)
        fill(128 + lane, lane)
        fill(256 + lane, (-3, -2, -1, -1)[lane % 4])
        fill(384 + lane, (128, 129, 130, 128)[lane % 4])
    return table


def cost(flops, size):
    return pl.CostEstimate(flops=flops, bytes_accessed=size, transcendentals=0)


def params(mib):
    return pltpu.CompilerParams(vmem_limit_bytes=mib * 2**20)


def shape(dims, kind=f32):
    return jax.ShapeDtypeStruct(dims, kind)


def whole(dims):
    return pl.BlockSpec(dims, lambda i: (0,) * len(dims))


def shift(value, axis, closed, forward):
    count = lax.axis_size(axis)
    ends = count if closed else count - 1
    pairs = [(i, (i + 1) % count) for i in range(ends)]
    if not forward:
        pairs = [(b, a) for a, b in pairs]
    return lax.ppermute(value, axis, pairs)


def local(adjoint_in, courant_x, courant_y, mixing, kernel_rows, tracer_weights, column_ids, counts):
    tracers, levels, lons, lats = adjoint_in.shape
    devices = lax.axis_size(("gx", "gy"))
    slots = kernel_rows.shape[1]
    fields = tracers * levels
    size = fields * lons * lats * 4

    packed = pl.pallas_call(
        pack_kernel,
        grid=(8,),
        in_specs=[
            pl.BlockSpec(memory_space=pltpu.SMEM),
            pl.BlockSpec((levels, slots // 8), lambda i: (0, i)),
            pl.BlockSpec((tracers, slots // 8), lambda i: (0, i)),
        ],
        out_specs=pl.BlockSpec((devices // 8, 24, 128), lambda i: (i, 0, 0)),
        out_shape=shape((devices, 24, 128), bf16),
        scratch_shapes=[pltpu.VMEM((512, 512), bf16)],
        compiler_params=params(60),
        name="pack",
    )(counts, kernel_rows, tracer_weights)
    got = lax.all_to_all(packed, ("gx", "gy"), split_axis=0, concat_axis=0, tiled=True)

    inv, q = pl.pallas_call(
        factor_kernel,
        out_shape=[shape((levels, lons, lats))] * 2,
        compiler_params=params(16),
        cost_estimate=cost(30 * levels * lons * lats, 3 * levels * lons * lats * 4),
        name="factor",
    )(mixing)
    bins = jnp.broadcast_to((column_ids // (2 * lats)).astype(bf16)[:, None], (slots, 128))
    code, starts = pl.pallas_call(
        rank_kernel,
        out_shape=[shape((slots, 128), bf16), shape((8 * (slots // CHUNK), 128), jnp.int32)],
        compiler_params=params(16),
        cost_estimate=cost(10**9, 2 * 10**6),
        name="rank",
    )(bins)
    lhs, places = pl.pallas_call(
        order_kernel,
        out_shape=[shape((2 * fields, slots), bf16), shape((8, slots))],
        scratch_shapes=[pltpu.VMEM((512, 512), bf16), pltpu.VMEM((80, slots), f32)],
        compiler_params=params(24),
        cost_estimate=cost(10**9, 8 * 10**6),
        name="order",
    )(got, column_ids.reshape(1, slots), code)

    edge = shape((4, fields, lats), bf16)
    state, x_low, x_high = pl.pallas_call(
        forcing_kernel,
        grid=(lons // 8,),
        in_specs=[
            pl.BlockSpec(memory_space=pltpu.SMEM),
            whole((2 * fields, slots)),
            whole((8, slots)),
            pl.BlockSpec((fields, 8, lats), lambda i: (0, i, 0)),
        ],
        out_specs=[
            pl.BlockSpec((fields, 8, lats), lambda i: (0, i, 0)),
            whole((4, fields, lats)),
            whole((4, fields, lats)),
        ],
        out_shape=[shape((fields, lons, lats)), edge, edge],
        scratch_shapes=[pltpu.VMEM((2 * fields, 2 * lats), f32)],
        compiler_params=params(32),
        cost_estimate=cost(10**10, 2 * size),
        name="forcing",
    )(starts, lhs, places, adjoint_in.reshape(fields, lons, lats))

    for step in range(STEPS):
        from_left = shift(x_high, "gx", True, True)
        from_right = shift(x_low, "gx", True, False)
        blocks = levels // LB
        halo_spec = pl.BlockSpec((4, tracers, LB, lats), lambda b: (0, 0, b, 0))
        field_spec = pl.BlockSpec((tracers, LB, lons, lats), lambda b: (0, b, 0, 0))
        note_spec = pl.BlockSpec((1, lons, 128), lambda b: (b, 0, 0))
        zonal, to_left, to_right = pl.pallas_call(
            zonal_kernel,
            grid=(blocks,),
            in_specs=[
                field_spec,
                pl.BlockSpec((LB, lons, lats), lambda b: (b, 0, 0)),
                halo_spec,
                halo_spec,
                whole((256, 256)),
            ],
            out_specs=[field_spec, note_spec, note_spec],
            out_shape=[
                shape((tracers, levels, lons, lats)),
                shape((blocks, lons, 128), bf16),
                shape((blocks, lons, 128), bf16),
            ],
            scratch_shapes=[
                pltpu.VMEM((tracers * LB * 48, lats), f32),
                pltpu.VMEM((tracers * LB * lons, 2 * lats), bf16),
            ],
            compiler_params=params(24),
            cost_estimate=cost(20 * size // 4, 2 * size),
            name="zonal",
        )(
            state.reshape(tracers, levels, lons, lats),
            courant_x,
            from_left.reshape(4, tracers, levels, lats),
            from_right.reshape(4, tracers, levels, lats),
            jnp.asarray(edge_weights(), bf16),
        )
        y_left = shift(to_right, "gy", False, True)
        y_right = shift(to_left, "gy", False, False)
        first = step == 0
        field_spec = pl.BlockSpec((tracers, levels, 8, lats), lambda r: (0, 0, r, 0))
        level_spec = pl.BlockSpec((levels, 8, lats), lambda r: (0, r, 0))
        note_spec = pl.BlockSpec((blocks, 8, 128), lambda r: (0, r, 0))
        gradient_spec = pl.BlockSpec((tracers, 8, lats), lambda r: (0, r, 0))
        mixing_spec = pl.BlockSpec((levels - 1, 8, lats), lambda r: (0, r, 0))
        operands = [zonal, courant_y, mixing, inv, q, y_left, y_right, jnp.asarray(lat_weights(), bf16)]
        in_specs = [field_spec, level_spec, mixing_spec, level_spec, level_spec, note_spec, note_spec, whole((512, 256))]
        out_specs = [field_spec, gradient_spec]
        out_shape = [shape((tracers, levels, lons, lats)), shape((tracers, lons, lats))]
        if first:
            out_specs += [whole((4, fields, lats))] * 2
            out_shape += [edge, edge]
        else:
            operands.append(gradient)
            in_specs.append(gradient_spec)

        def kernel(*refs, first=first):
            column_kernel(first, *refs)

        out = pl.pallas_call(
            kernel,
            grid=(lons // 8,),
            in_specs=in_specs,
            out_specs=out_specs,
            out_shape=out_shape,
            scratch_shapes=[pltpu.VMEM((levels * tracers * 8, 512), bf16)],
            compiler_params=params(32),
            cost_estimate=cost(40 * size // 4, 2 * size),
            name="column",
        )(*operands)
        if first:
            state, gradient, x_low, x_high = out
        else:
            state, gradient = out
    return state, gradient


def solution(mesh):
    in_specs = (
        P(None, None, "gx", "gy"),
        P(None, "gx", "gy"),
        P(None, "gx", "gy"),
        P(None, "gx", "gy"),
        P(None, ("gx", "gy")),
        P(None, ("gx", "gy")),
        P(("gx", "gy")),
        P(("gx", "gy"), None),
    )
    out_specs = (P(None, None, "gx", "gy"), P(None, "gx", "gy"))
    return jax.shard_map(local, mesh=mesh, in_specs=in_specs, out_specs=out_specs, check_vma=False)
```

time: 193 us -> 129 us (0.67)
  Pallas kernels: 119 us -> 59 us
    pallas_call x2, Pallas kernels: 68.2 us -> 15.7 us  [local(): pl.pallas_call(kernel, grid=(lons // 8,), in_specs=in_specs, out_specs=ou...]
    pallas_call x2 -> x4, Pallas kernels: 37 us -> 27.3 us  [the longest x1 15.8 us: local(): pl.pallas_call(forcing_kernel, grid=(lons // 8,), in_specs=[pl.BlockSpec(...]
    unnamed x16 -> x14, local copies, waits for them, and re-layouts: 4.82 us -> 2.37 us
    pallas_call x2, Pallas kernels: 13.1 us -> 15.1 us  [local(): pl.pallas_call(zonal_kernel, grid=(blocks,), in_specs=[field_spec, pl.Blo...]
  transfers between devices with their start and end apart: 9 -> 9, of which waited for: 6 -> 6; matrix products, arithmetic and copies ran while one was open for 1% -> 1% of each run, Pallas kernels for 0% -> 2%
where the time goes in v2:
time: 129 us; the launch traced here: 128 us
  Pallas kernels  59 us (46%)
  waiting for transfers between devices  33.3 us (26%)
  starting transfers between devices  31.1 us (24%)
  local copies, waits for them, and re-layouts  2.97 us (2%)
    ppermute x8, waiting for transfers between devices, shift(): return lax.ppermute(value, axis, pairs)  21.8 us
    ppermute x8, starting transfers between devices, shift(): return lax.ppermute(value, axis, pairs)  20.8 us
    pallas_call x1, Pallas kernels, local(): pl.pallas_call(forcing_kernel, grid=(lons // 8,), in_specs=[pl.BlockSpec(...  15.8 us
    pallas_call x2, Pallas kernels, local(): pl.pallas_call(kernel, grid=(lons // 8,), in_specs=in_specs, out_specs=ou...  15.7 us
    pallas_call x2, Pallas kernels, local(): pl.pallas_call(zonal_kernel, grid=(blocks,), in_specs=[field_spec, pl.Blo...  15.1 us
    all_to_all x1, waiting for transfers between devices, local(): lax.all_to_all(packed, ('gx', 'gy'), split_axis=0, concat_axis=0, tiled=T...  11.6 us
    all_to_all x1, starting transfers between devices, local(): lax.all_to_all(packed, ('gx', 'gy'), split_axis=0, concat_axis=0, tiled=T...  10.3 us
    pallas_call x1, Pallas kernels, local(): pl.pallas_call(pack_kernel, grid=(8,), in_specs=[pl.BlockSpec(memory_spac...  6.02 us
  transfers between devices with their start and end apart: 9, of which 6 were waited for; matrix products, arithmetic and copies ran while one was open for 1% of the time, Pallas kernels for 2%

profile of v2, /device:TPU:24, one launch (start us, length us, event | category | flops | bytes accessed | tf_op | source)
XLA Modules:
  0.0 128.0 jit_solution(2656826516698715977)
XLA Ops:
  0.6 0.0 copy-start.5
  0.6 6.0 %pack.1 = bf16[128,24,128]{2,1,0:T(8,128)(2,1)} custom-call(s32[1,128]{1,0:T(1,128)} %counts.1, bf16[72,4096]{1,0:T(8,128)(2,1)} %rows.1, bf16[4,4096]{1,0:T(4,128)(2,1)} %weights.1), custom_call_target="tpu_custom_call" | custom-call | tf_op jit(solution)/shard_map/pack/pallas_call | solution.py:399
  6.7 10.3 %all-to-all-start = ((bf16[128,24,128]{2,1,0:T(8,128)(2,1)}), bf16[128,24,128]{2,1,0:T(8,128)(2,1)S(1)}, u32[]{:S(2)}, u32[]{:S(2)}) async-start(bf16[128,24,128]{2,1,0:T(8,128)(2,1)} %pack.1), calls=%async_computation | async-start | bytes 1572864 | tf_op jit(solution)/shard_map/all_to_all | solution.py:413
  16.9 0.7 fusion.1
  17.7 0.6 broadcast_in_dim.2.bins
  18.3 1.9 %rank.1 = (bf16[4096,128]{1,0:T(8,128)(2,1)S(1)}, s32[32,128]{1,0:T(8,128)S(1)}) custom-call(bf16[4096,128]{1,0:T(8,128)(2,1)S(1)} %broadcast_in_dim.2.bins), custom_call_target="tpu_custom_call" | custom-call | flops 1000000000 | bytes 2000000 | tf_op jit(solution)/shard_map/rank/pallas_call | solution.py:423
  20.2 11.6 %all-to-all-done.got = bf16[128,24,128]{2,1,0:T(8,128)(2,1)S(1)} async-done(((bf16[128,24,128]{2,1,0:T(8,128)(2,1)}), bf16[128,24,128]{2,1,0:T(8,128)(2,1)S(1)}, u32[]{:S(2)}, u32[]{:S(2)}) %all-to-all-start) | async-done | bytes 786464 | tf_op jit(solution)/shard_map/all_to_all | solution.py:413
  31.8 3.5 %order.1 = (bf16[576,4096]{1,0:T(8,128)(2,1)S(1)}, f32[8,4096]{1,0:T(8,128)S(1)}) custom-call(bf16[128,24,128]{2,1,0:T(8,128)(2,1)S(1)} %all-to-all-done.got, s32[1,4096]{1,0:T(1,128)S(1)} %bitcast.12, bf16[4096,128]{1,0:T(8,128)(2,1)S(1)} %get-tuple-element.22.code), custom_call_target="tpu_custom_call" | custom-call | flops 1000000000 | bytes 8000000 | tf_op jit(solution)/shard_map/order/pallas_call | solution.py:430
  35.3 0.0 copy-start.6
  35.3 2.3 %copy-done.6 = f32[4,72,32,128]{3,2,1,0:T(8,128)S(1)} copy-done((f32[4,72,32,128]{3,2,1,0:T(8,128)S(1)}, f32[4,72,32,128]{3,2,1,0:T(8,128)}, u32[]{:S(2)}) %copy-start.6) | copy-done | bytes 4718616
  37.7 15.8 %forcing.1 = (f32[288,32,128]{2,1,0:T(8,128)S(1)}, bf16[4,288,128]{2,1,0:T(8,128)(2,1)S(1)}, bf16[4,288,128]{2,1,0:T(8,128)(2,1)S(1)}) custom-call(s32[32,128]{1,0:T(8,128)S(1)} %get-tuple-element.21.starts, bf16[576,4096]{1,0:T(8,128)(2,1)S(1)} %get-tuple-element.23.lhs, f32[8,4096]{1,0:T(8,128)S(1)} %get-tuple-element.24.places, f32[288,32,128]{2,1,0:T(8,128)S(1)} %bitcast.13), custom_call_target="tpu_custom_call" | custom-call | flops 10000000000 | bytes 9437184 | tf_op jit(solution)/shard_map/forcing/pallas_call | solution.py:440
  53.5 0.0 copy-start
  53.5 0.0 copy-start.1
  53.5 0.0 copy-start.3
  53.5 0.1 collective-permute-start
  53.6 3.8 %collective-permute-start.1 = (bf16[4,288,128]{2,1,0:T(8,128)(2,1)S(1)}, bf16[4,288,128]{2,1,0:T(8,128)(2,1)S(1)}, u32[]{:S(2)}, u32[]{:S(2)}) collective-permute-start(bf16[4,288,128]{2,1,0:T(8,128)(2,1)S(1)} %get-tuple-element.27), channel_id=1, source_target_pairs={{8,0},{16,8},{24,16},{32,24},{40,32},{48,40},{56,48},{64,56},{72,6... | collective-permute-start | bytes 884744 | tf_op jit(solution)/shard_map/ppermute | solution.py:389
  57.5 4.4 %collective-permute-done = bf16[4,288,128]{2,1,0:T(8,128)(2,1)S(1)} collective-permute-done((bf16[4,288,128]{2,1,0:T(8,128)(2,1)S(1)}, bf16[4,288,128]{2,1,0:T(8,128)(2,1)S(1)}, u32[]{:S(2)}, u32[]{:S(2)}) %collective-permute-start) | collective-permute-done | bytes 294944 | tf_op jit(solution)/shard_map/ppermute | solution.py:389
  61.9 7.6 %zonal.2 = (f32[4,72,32,128]{3,2,1,0:T(8,128)S(1)}, bf16[9,32,128]{2,1,0:T(8,128)(2,1)S(1)}, bf16[9,32,128]{2,1,0:T(8,128)(2,1)S(1)}) custom-call(f32[4,72,32,128]{3,2,1,0:T(8,128)S(1)} %bitcast.7, f32[72,32,128]{2,1,0:T(8,128)S(1)} %copy-done.2, bf16[4,4,72,128]{3,2,1,0:T(8,128)(2,1)S(1)} %bitcast.8, bf16[4,4,72,128]{3,2,1,0:T(8,128)(2,1)S(1)} %bitcast.10, ...), custom_call_target="tpu_custom_call" | custom-call | flops 23592960 | bytes 9437184 | tf_op jit(solution)/shard_map/zonal/pallas_call | solution.py:468
  69.5 5.2 %collective-permute-start.2 = (bf16[9,32,128]{2,1,0:T(8,128)(2,1)S(1)}, bf16[9,32,128]{2,1,0:T(8,128)(2,1)S(1)}, u32[]{:S(2)}, u32[]{:S(2)}) collective-permute-start(bf16[9,32,128]{2,1,0:T(8,128)(2,1)S(1)} %get-tuple-element.31), channel_id=1, source_target_pairs={{0,1},{1,2},{2,3},{3,4},{4,5},{5,6},{6,7},{8,9},{9,10},{10,11},{11... | collective-permute-start | bytes 221192 | tf_op jit(solution)/shard_map/ppermute | solution.py:389
  74.7 1.9 %collective-permute-start.3 = (bf16[9,32,128]{2,1,0:T(8,128)(2,1)S(1)}, bf16[9,32,128]{2,1,0:T(8,128)(2,1)S(1)}, u32[]{:S(2)}, u32[]{:S(2)}) collective-permute-start(bf16[9,32,128]{2,1,0:T(8,128)(2,1)S(1)} %get-tuple-element.32), channel_id=1, source_target_pairs={{1,0},{2,1},{3,2},{4,3},{5,4},{6,5},{7,6},{9,8},{10,9},{11,10},{12... | collective-permute-start | bytes 221192 | tf_op jit(solution)/shard_map/ppermute | solution.py:389
  76.6 0.9 factor.1
  77.6 7.0 %collective-permute-done.3.refs_6_ = bf16[9,32,128]{2,1,0:T(8,128)(2,1)S(1)} collective-permute-done((bf16[9,32,128]{2,1,0:T(8,128)(2,1)S(1)}, bf16[9,32,128]{2,1,0:T(8,128)(2,1)S(1)}, u32[]{:S(2)}, u32[]{:S(2)}) %collective-permute-start.3) | collective-permute-done | bytes 73760 | tf_op jit(solution)/shard_map/ppermute | solution.py:389
  84.6 8.3 %column.2 = (f32[4,72,32,128]{3,2,1,0:T(8,128)S(1)}, f32[4,32,128]{2,1,0:T(8,128)S(1)}, bf16[4,288,128]{2,1,0:T(8,128)(2,1)S(1)}, bf16[4,288,128]{2,1,0:T(8,128)(2,1)S(1)}) custom-call(f32[4,72,32,128]{3,2,1,0:T(8,128)S(1)} %get-tuple-element.28.refs_0_, f32[72,32,128]{2,1,0:T(8,128)S(1)} %copy-done.1, f32[71,32,128]{2,1,0:T(8,128)S(1)} %copy-done, ...), custom_call_target="tpu_custom_call" | custom-call | flops 47185920 | bytes 9437184 | tf_op jit(solution)/shard_map/column/pallas_call | solution.py:520
  92.8 0.1 collective-permute-start.4
  92.9 3.8 %collective-permute-start.5 = (bf16[4,288,128]{2,1,0:T(8,128)(2,1)S(1)}, bf16[4,288,128]{2,1,0:T(8,128)(2,1)S(1)}, u32[]{:S(2)}, u32[]{:S(2)}) collective-permute-start(bf16[4,288,128]{2,1,0:T(8,128)(2,1)S(1)} %get-tuple-element.35), channel_id=1, source_target_pairs={{8,0},{16,8},{24,16},{32,24},{40,32},{48,40},{56,48},{64,56},{72,6... | collective-permute-start | bytes 884744 | tf_op jit(solution)/shard_map/ppermute | solution.py:389
  96.8 4.4 %collective-permute-done.4 = bf16[4,288,128]{2,1,0:T(8,128)(2,1)S(1)} collective-permute-done((bf16[4,288,128]{2,1,0:T(8,128)(2,1)S(1)}, bf16[4,288,128]{2,1,0:T(8,128)(2,1)S(1)}, u32[]{:S(2)}, u32[]{:S(2)}) %collective-permute-start.4) | collective-permute-done | bytes 294944 | tf_op jit(solution)/shard_map/ppermute | solution.py:389
  101.2 7.6 %zonal.3 = (f32[4,72,32,128]{3,2,1,0:T(8,128)S(1)}, bf16[9,32,128]{2,1,0:T(8,128)(2,1)S(1)}, bf16[9,32,128]{2,1,0:T(8,128)(2,1)S(1)}) custom-call(f32[4,72,32,128]{3,2,1,0:T(8,128)S(1)} %get-tuple-element.33.state, f32[72,32,128]{2,1,0:T(8,128)S(1)} %copy-done.2, bf16[4,4,72,128]{3,2,1,0:T(8,128)(2,1)S(1)} %bitcast.9, bf16[4,4,72,128]{3,2,1,0:T(8,128)(2,1)S(1)} %bitcast.11, ...), custom_call_target="tpu_custom_call" | custom-call | flops 23592960 | bytes 9437184 | tf_op jit(solution)/shard_map/zonal/pallas_call | solution.py:468
  108.7 1.9 %collective-permute-start.6 = (bf16[9,32,128]{2,1,0:T(8,128)(2,1)S(1)}, bf16[9,32,128]{2,1,0:T(8,128)(2,1)S(1)}, u32[]{:S(2)}, u32[]{:S(2)}) collective-permute-start(bf16[9,32,128]{2,1,0:T(8,128)(2,1)S(1)} %get-tuple-element.37), channel_id=1, source_target_pairs={{0,1},{1,2},{2,3},{3,4},{4,5},{5,6},{6,7},{8,9},{9,10},{10,11},{11... | collective-permute-start | bytes 221192 | tf_op jit(solution)/shard_map/ppermute | solution.py:389
  110.7 3.9 %collective-permute-start.7 = (bf16[9,32,128]{2,1,0:T(8,128)(2,1)S(1)}, bf16[9,32,128]{2,1,0:T(8,128)(2,1)S(1)}, u32[]{:S(2)}, u32[]{:S(2)}) collective-permute-start(bf16[9,32,128]{2,1,0:T(8,128)(2,1)S(1)} %get-tuple-element.38), channel_id=1, source_target_pairs={{1,0},{2,1},{3,2},{4,3},{5,4},{6,5},{7,6},{9,8},{10,9},{11,10},{12... | collective-permute-start | bytes 221192 | tf_op jit(solution)/shard_map/ppermute | solution.py:389
  114.6 0.4 collective-permute-done.6.refs_5_
  115.0 5.5 %collective-permute-done.7.refs_6_ = bf16[9,32,128]{2,1,0:T(8,128)(2,1)S(1)} collective-permute-done((bf16[9,32,128]{2,1,0:T(8,128)(2,1)S(1)}, bf16[9,32,128]{2,1,0:T(8,128)(2,1)S(1)}, u32[]{:S(2)}, u32[]{:S(2)}) %collective-permute-start.7) | collective-permute-done | bytes 73760 | tf_op jit(solution)/shard_map/ppermute | solution.py:389
  120.5 7.4 %column.3 = (f32[4,72,32,128]{3,2,1,0:T(8,128)}, f32[4,32,128]{2,1,0:T(8,128)}) custom-call(f32[4,72,32,128]{3,2,1,0:T(8,128)S(1)} %get-tuple-element.36.refs_0_, f32[72,32,128]{2,1,0:T(8,128)S(1)} %copy-done.1, f32[71,32,128]{2,1,0:T(8,128)S(1)} %copy-done, f32[72,32,128]{2,1,0:T(8,128)S(1)} %get-tuple-element.29.refs_3_, ...), custom_call_target="tpu_custom_call" | custom-call | flops 47185920 | bytes 9437184 | tf_op jit(solution)/shard_map/column/pallas_call | solution.py:520
  (11 shorter events, 0.0 us)
Async XLA Ops:
  0.6 31.1 %copy-start.5 = (s32[4096]{0:T(1024)S(1)}, s32[4096]{0:T(1024)}, u32[]{:S(2)}) copy-start(s32[4096]{0:T(1024)} %param.18) | copy-start | bytes 49156
  6.7 25.1 %all-to-all-start = ((bf16[128,24,128]{2,1,0:T(8,128)(2,1)}), bf16[128,24,128]{2,1,0:T(8,128)(2,1)S(1)}, u32[]{:S(2)}, u32[]{:S(2)}) async-start(bf16[128,24,128]{2,1,0:T(8,128)(2,1)} %pack.1), calls=%async_computation | async-start | bytes 1572864 | tf_op jit(solution)/shard_map/all_to_all | solution.py:413
  35.3 2.3 %copy-start.6 = (f32[4,72,32,128]{3,2,1,0:T(8,128)S(1)}, f32[4,72,32,128]{3,2,1,0:T(8,128)}, u32[]{:S(2)}) copy-start(f32[4,72,32,128]{3,2,1,0:T(8,128)} %param.12) | copy-start | bytes 14155780
  37.7 24.2 %copy-start.2 = (f32[72,32,128]{2,1,0:T(8,128)S(1)}, f32[72,32,128]{2,1,0:T(8,128)}, u32[]{:S(2)}) copy-start(f32[72,32,128]{2,1,0:T(8,128)} %courant.3) | copy-start | bytes 3538948
  37.7 24.2 %copy-start.4 = (bf16[256,256]{1,0:T(8,128)(2,1)S(1)}, bf16[256,256]{1,0:T(8,128)(2,1)}, u32[]{:S(2)}) copy-start(bf16[256,256]{1,0:T(8,128)(2,1)} %constant.20.clone.spread) | copy-start | bytes 393220
  53.5 23.1 %copy-start = (f32[71,32,128]{2,1,0:T(8,128)S(1)}, f32[71,32,128]{2,1,0:T(8,128)}, u32[]{:S(2)}) copy-start(f32[71,32,128]{2,1,0:T(8,128)} %refs_2_.3) | copy-start | bytes 3489796
  53.5 31.0 %copy-start.1 = (f32[72,32,128]{2,1,0:T(8,128)S(1)}, f32[72,32,128]{2,1,0:T(8,128)}, u32[]{:S(2)}) copy-start(f32[72,32,128]{2,1,0:T(8,128)} %refs_1_.3) | copy-start | bytes 3538948
  53.5 31.0 %copy-start.3 = (bf16[512,256]{1,0:T(8,128)(2,1)S(1)}, bf16[512,256]{1,0:T(8,128)(2,1)}, u32[]{:S(2)}) copy-start(bf16[512,256]{1,0:T(8,128)(2,1)} %constant.21.clone.refs_7_) | copy-start | bytes 786436
  53.5 8.3 %collective-permute-start = (bf16[4,288,128]{2,1,0:T(8,128)(2,1)S(1)}, bf16[4,288,128]{2,1,0:T(8,128)(2,1)S(1)}, u32[]{:S(2)}, u32[]{:S(2)}) collective-permute-start(bf16[4,288,128]{2,1,0:T(8,128)(2,1)S(1)} %get-tuple-element.26), channel_id=1, source_target_pairs={{0,8},{8,16},{16,24},{24,32},{32,40},{40,48},{48,56},{56,64},{64,7... | collective-permute-start | bytes 884744 | tf_op jit(solution)/shard_map/ppermute | solution.py:389
  53.6 8.2 %collective-permute-start.1 = (bf16[4,288,128]{2,1,0:T(8,128)(2,1)S(1)}, bf16[4,288,128]{2,1,0:T(8,128)(2,1)S(1)}, u32[]{:S(2)}, u32[]{:S(2)}) collective-permute-start(bf16[4,288,128]{2,1,0:T(8,128)(2,1)S(1)} %get-tuple-element.27), channel_id=1, source_target_pairs={{8,0},{16,8},{24,16},{32,24},{40,32},{48,40},{56,48},{64,56},{72,6... | collective-permute-start | bytes 884744 | tf_op jit(solution)/shard_map/ppermute | solution.py:389
  69.5 8.1 %collective-permute-start.2 = (bf16[9,32,128]{2,1,0:T(8,128)(2,1)S(1)}, bf16[9,32,128]{2,1,0:T(8,128)(2,1)S(1)}, u32[]{:S(2)}, u32[]{:S(2)}) collective-permute-start(bf16[9,32,128]{2,1,0:T(8,128)(2,1)S(1)} %get-tuple-element.31), channel_id=1, source_target_pairs={{0,1},{1,2},{2,3},{3,4},{4,5},{5,6},{6,7},{8,9},{9,10},{10,11},{11... | collective-permute-start | bytes 221192 | tf_op jit(solution)/shard_map/ppermute | solution.py:389
  74.7 9.9 %collective-permute-start.3 = (bf16[9,32,128]{2,1,0:T(8,128)(2,1)S(1)}, bf16[9,32,128]{2,1,0:T(8,128)(2,1)S(1)}, u32[]{:S(2)}, u32[]{:S(2)}) collective-permute-start(bf16[9,32,128]{2,1,0:T(8,128)(2,1)S(1)} %get-tuple-element.32), channel_id=1, source_target_pairs={{1,0},{2,1},{3,2},{4,3},{5,4},{6,5},{7,6},{9,8},{10,9},{11,10},{12... | collective-permute-start | bytes 221192 | tf_op jit(solution)/shard_map/ppermute | solution.py:389
  92.8 8.3 %collective-permute-start.4 = (bf16[4,288,128]{2,1,0:T(8,128)(2,1)S(1)}, bf16[4,288,128]{2,1,0:T(8,128)(2,1)S(1)}, u32[]{:S(2)}, u32[]{:S(2)}) collective-permute-start(bf16[4,288,128]{2,1,0:T(8,128)(2,1)S(1)} %get-tuple-element.34), channel_id=1, source_target_pairs={{0,8},{8,16},{16,24},{24,32},{32,40},{40,48},{48,56},{56,64},{64,7... | collective-permute-start | bytes 884744 | tf_op jit(solution)/shard_map/ppermute | solution.py:389
  92.9 8.2 %collective-permute-start.5 = (bf16[4,288,128]{2,1,0:T(8,128)(2,1)S(1)}, bf16[4,288,128]{2,1,0:T(8,128)(2,1)S(1)}, u32[]{:S(2)}, u32[]{:S(2)}) collective-permute-start(bf16[4,288,128]{2,1,0:T(8,128)(2,1)S(1)} %get-tuple-element.35), channel_id=1, source_target_pairs={{8,0},{16,8},{24,16},{32,24},{40,32},{48,40},{56,48},{64,56},{72,6... | collective-permute-start | bytes 884744 | tf_op jit(solution)/shard_map/ppermute | solution.py:389
  108.7 6.2 %collective-permute-start.6 = (bf16[9,32,128]{2,1,0:T(8,128)(2,1)S(1)}, bf16[9,32,128]{2,1,0:T(8,128)(2,1)S(1)}, u32[]{:S(2)}, u32[]{:S(2)}) collective-permute-start(bf16[9,32,128]{2,1,0:T(8,128)(2,1)S(1)} %get-tuple-element.37), channel_id=1, source_target_pairs={{0,1},{1,2},{2,3},{3,4},{4,5},{5,6},{6,7},{8,9},{9,10},{10,11},{11... | collective-permute-start | bytes 221192 | tf_op jit(solution)/shard_map/ppermute | solution.py:389
  110.7 9.9 %collective-permute-start.7 = (bf16[9,32,128]{2,1,0:T(8,128)(2,1)S(1)}, bf16[9,32,128]{2,1,0:T(8,128)(2,1)S(1)}, u32[]{:S(2)}, u32[]{:S(2)}) collective-permute-start(bf16[9,32,128]{2,1,0:T(8,128)(2,1)S(1)} %get-tuple-element.38), channel_id=1, source_target_pairs={{1,0},{2,1},{3,2},{4,3},{5,4},{6,5},{7,6},{9,8},{10,9},{11,10},{12... | collective-permute-start | bytes 221192 | tf_op jit(solution)/shard_map/ppermute | solution.py:389

commit v3 on v2

v3 whole, which is shorter than its diff:
```python
import jax
import jax.numpy as jnp
import numpy as np
from jax import lax
from jax.experimental import pallas as pl
from jax.experimental.pallas import tpu as pltpu
from jax.sharding import PartitionSpec as P

STEPS = 2
LB = 8
CHUNK = 1024

D1, D2, D3 = 0.75, -0.15, 1.0 / 60.0
E1, E2, E3 = 1.5, -0.15, 1.0 / 90.0
E0 = -49.0 / 18.0

f32 = jnp.float32
bf16 = jnp.bfloat16


def fill_swap(table):
    row = lax.broadcasted_iota(jnp.int32, table.shape, 0)
    col = lax.broadcasted_iota(jnp.int32, table.shape, 1)
    want = ((col >> 5) & 3) * 128 + (col >> 7) * 32 + (col & 31)
    table[...] = jnp.where(row == want, 1.0, 0.0).astype(bf16)


def split(value):
    hi = value.astype(bf16)
    return hi, (value - hi.astype(f32)).astype(bf16)


def pack_kernel(counts, rows, weights, out, swap):
    step = pl.program_id(0)
    groups = rows.shape[1] // 128

    @pl.when(step == 0)
    def _():
        fill_swap(swap)

    lane = lax.broadcasted_iota(jnp.int32, (24, 128), 1)
    block = lane >> 5
    columns = [[] for _ in range(4)]
    for g in range(groups):
        lanes = slice(g * 128, g * 128 + 128)
        first = 4 * (step * groups + g)
        limit = jnp.where(
            block < 2,
            jnp.where(block == 0, counts[0, first], counts[0, first + 1]),
            jnp.where(block == 2, counts[0, first + 2], counts[0, first + 3]),
        )
        live = (lane & 31) < limit
        for q in range(3):
            columns[q].append(jnp.where(live, rows[24 * q : 24 * q + 24, lanes].astype(f32), 0.0))
        columns[3].append(jnp.concatenate([weights[:, lanes].astype(f32), jnp.zeros((20, 128), f32)], axis=0))
    wide = jnp.concatenate([jnp.concatenate(c, axis=0).astype(bf16) for c in columns], axis=1)
    moved = jnp.dot(wide, swap[...], preferred_element_type=f32)
    for g in range(groups):
        for i in range(4):
            out[4 * g + i] = moved[24 * g : 24 * g + 24, 128 * i : 128 * i + 128].astype(bf16)


def factor_kernel(mixing, inv_out, q_out):
    levels = inv_out.shape[0]
    top = mixing[0]
    inv = 1.0 / (1.0 + top)
    q = top * inv
    inv_out[0] = inv
    q_out[0] = q

    def level(l, carry):
        below, q = carry
        above = mixing[l]
        inv = 1.0 / (1.0 + below + above - below * q)
        q = above * inv
        inv_out[l] = inv
        q_out[l] = q
        return above, q

    below, q = lax.fori_loop(1, levels - 1, level, (top, q))
    inv_out[levels - 1] = 1.0 / (1.0 + below - below * q)
    q_out[levels - 1] = jnp.zeros_like(q)


def rank_kernel(bins, code, starts):
    piece = 256
    lane = lax.broadcasted_iota(jnp.int32, (piece, 128), 1)
    lane_f = lane.astype(f32)
    upto = (lax.broadcasted_iota(jnp.int32, (piece, piece), 1) <= lax.broadcasted_iota(jnp.int32, (piece, piece), 0))
    upto = jnp.where(upto, 1.0, 0.0).astype(bf16)
    row2 = lax.broadcasted_iota(jnp.int32, (256, 256), 0)
    col2 = lax.broadcasted_iota(jnp.int32, (256, 256), 1)
    spread = jnp.where((row2 >> 7) == (col2 >> 7), 1.0, 0.0).astype(bf16)
    ones = jnp.ones((8, CHUNK), bf16)
    for h in range(bins.shape[0] // CHUNK):
        own = bins[h * CHUNK : (h + 1) * CHUNK, :].astype(f32)
        wide = lax.broadcasted_iota(jnp.int32, own.shape, 1).astype(f32)
        below = jnp.where(own < wide, 1.0, 0.0).astype(bf16)
        start = jnp.dot(ones, below, preferred_element_type=f32)
        starts[8 * h : 8 * h + 8, :] = start.astype(jnp.int32)
        running = start[0:1, :] - 1.0
        for p in range(CHUNK // piece):
            at = slice(p * piece, p * piece + piece)
            mine = own[at] == lane_f
            one_hot = jnp.where(mine, 1.0, 0.0)
            place = jnp.dot(upto, one_hot.astype(bf16), preferred_element_type=f32) + running
            running = place[piece - 1 : piece, :]
            place = jnp.where(mine, place, 0.0)
            high = jnp.floor(place * (1.0 / 128.0))
            low = place - 128.0 * high
            both = jnp.dot(
                jnp.concatenate([high.astype(bf16), low.astype(bf16)], axis=1), spread, preferred_element_type=f32
            )
            found = jnp.where(both[:, 128:] == lane_f, both[:, :128], -1.0)
            code[h * CHUNK + p * piece : h * CHUNK + (p + 1) * piece, :] = found.astype(bf16)


def order_kernel(got, ids, code, lhs, places, swap, raw):
    half = lhs.shape[0] // 2
    slots = lhs.shape[1]
    fill_swap(swap)
    batch = 8
    for first in range(0, slots // 128, batch):
        wide = jnp.concatenate(
            [
                jnp.concatenate([got[4 * (first + g) + i].astype(f32) for g in range(batch)], axis=0).astype(bf16)
                for i in range(4)
            ],
            axis=1,
        )
        moved = jnp.dot(wide, swap[...], preferred_element_type=f32)
        for g in range(batch):
            lanes = slice((first + g) * 128, (first + g) * 128 + 128)
            for q in range(4):
                count = 24 if q < 3 else 8
                raw[24 * q : 24 * q + count, lanes] = moved[24 * g : 24 * g + count, 128 * q : 128 * q + 128]
    cells = ids[...]
    raw[76:77, :] = (cells & 127).astype(f32)
    raw[77:78, :] = (cells >> 7).astype(f32)
    one, zero = jnp.ones((), bf16), jnp.zeros((), bf16)
    for h in range(slots // CHUNK):
        block = raw[:, h * CHUNK : (h + 1) * CHUNK].astype(bf16)
        part = code[h * CHUNK : (h + 1) * CHUNK, :]
        for p in range(CHUNK // 256):
            one_hot = jnp.concatenate(
                [jnp.where(part == jnp.asarray(2 * p + a, bf16), one, zero) for a in range(2)], axis=1
            )
            done = jnp.dot(block, one_hot, preferred_element_type=f32)
            lanes = slice(h * CHUNK + p * 256, h * CHUNK + (p + 1) * 256)
            places[:, lanes] = done[72:80, :]
            for t in range(4):
                hi, lo = split(done[:72] * done[72 + t : 73 + t, :])
                lhs[72 * t : 72 * t + 72, lanes] = hi
                lhs[half + 72 * t : half + 72 * t + 72, lanes] = lo


def forcing_kernel(starts, lhs, places, adjoint_hbm, state, x_low, x_high, adjoint, turned, arrived):
    copy = pltpu.make_async_copy(adjoint_hbm, adjoint, arrived)
    copy.start()
    fields = state.shape[0]
    chunks = lhs.shape[1] // CHUNK
    last = CHUNK // 128 - 2
    steps = state.shape[1] // 8
    row = lax.broadcasted_iota(jnp.int32, (128, 256), 0).astype(f32)
    window = lax.broadcasted_iota(jnp.int32, (1, 256), 1)

    def product(base, lon, skip):
        lat = places[4:5, pl.ds(base, 256)]
        slot_lon = places[5:6, pl.ds(base, 256)]
        if skip is not None:
            slot_lon = jnp.where(window >= skip, slot_lon, -1.0)
        one_hot = jnp.concatenate(
            [
                jnp.where(jnp.where(slot_lon == (lon + a).astype(f32), lat, -1.0) == row, 1.0, 0.0).astype(bf16)
                for a in range(2)
            ],
            axis=0,
        )
        both = lax.dot_general(
            lhs[:, pl.ds(base, 256)], one_hot, (((1,), (1,)), ((), ())), preferred_element_type=f32
        )
        return both

    def extent(h, number):
        low = starts[8 * h, number]
        high = starts[8 * h, number + 1]
        first = jnp.minimum(low >> 7, last)
        return first, jnp.maximum(((high + 127) >> 7) - first - 1, 0) >> 1

    def eight(step, _):
        rest = jnp.int32(0)
        for pair in range(4):
            number = step * 4 + pair
            total = None
            for h in range(chunks):
                first, visits = extent(h, number)
                rest = rest + visits
                piece = product(pl.multiple_of(h * CHUNK + first * 128, 128), 2 * number, None)
                total = piece if total is None else total + piece
            total = total[:fields] + total[fields:]
            for a in range(2):
                turned[pl.ds(2 * pair + a, fields, stride=9), :] = total[:, 128 * a : 128 * a + 128]

        @pl.when(rest > 0)
        def _():
            def each(n, _):
                pair, h = n // chunks, n % chunks
                number = step * 4 + pair
                first, visits = extent(h, number)

                def more(j, _):
                    at = first + 2 + 2 * j
                    start = jnp.minimum(at, last)
                    base = pl.multiple_of(h * CHUNK + start * 128, 128)
                    both = product(base, 2 * number, (at - start) * 128)
                    both = both[:fields] + both[fields:]
                    for a in range(2):
                        place = pl.ds(2 * pair + a, fields, stride=9)
                        turned[place, :] = turned[place, :] + both[:, 128 * a : 128 * a + 128]
                    return 0

                lax.fori_loop(0, visits, more, 0)
                return 0

            lax.fori_loop(0, 4 * chunks, each, 0)

        @pl.when(step == 0)
        def _():
            copy.wait()

        rows = pl.ds(pl.multiple_of(8 * step, 8), 8)
        for f in range(fields):
            cell = adjoint[f, rows, :] + turned[9 * f : 9 * f + 8, :]
            state[f, rows, :] = cell
            turned[9 * f : 9 * f + 8, :] = cell

        def edge(out, order):
            near, second, third = (turned[pl.ds(j, fields, stride=9), :] for j in order)
            out[0], out[1] = split(near)
            out[2] = second.astype(bf16)
            out[3] = third.astype(bf16)

        @pl.when(step == 0)
        def _():
            edge(x_low, (0, 1, 2))

        @pl.when(step == steps - 1)
        def _():
            edge(x_high, (7, 6, 5))

        return 0

    lax.fori_loop(0, steps, eight, 0)


def zonal_rows(outer, state, courant, spread, halos, zonal, to_left, to_right, halves, pad):
    lane = lax.broadcasted_iota(jnp.int32, (16, 128), 1)
    group = lane >> 2
    note_rows = slice(16, 32) if outer else slice(0, 16)

    def block(b, _):
        levels = pl.ds(pl.multiple_of(b * LB, LB), LB)
        if outer:
            for t in range(4):
                for side, halo in enumerate(halos):
                    near = halo[0, t, levels, :].astype(f32) + halo[1, t, levels, :].astype(f32)
                    far = (halo[2, t, levels, :].astype(f32), halo[3, t, levels, :].astype(f32))
                    for k, value in enumerate((near, *far)):
                        pad[pl.ds(t * LB * 33 + (24 + k if side else 7 - k), LB, stride=33), :] = value
        notes = [jnp.zeros((16, 128), f32)] * 2
        for t in range(4):
            for l in range(LB):
                level = b * LB + l
                i = t * LB + l
                if outer:
                    c = jnp.concatenate([courant[level, 0:8, :], courant[level, 24:32, :]], axis=0)
                    low = state[t, level, 0:8, :]
                    high = state[t, level, 24:32, :]
                    base = 33 * i
                    pad[base + 8 : base + 16, :] = low
                    pad[base + 16 : base + 24, :] = high
                    v = {0: jnp.concatenate([low, high], axis=0)}
                    for k in (1, 2, 3):
                        v[-k] = jnp.concatenate(
                            [pad[base + 8 - k : base + 16 - k, :], state[t, level, 24 - k : 32 - k, :]], axis=0
                        )
                        v[k] = jnp.concatenate(
                            [state[t, level, k : 8 + k, :], pad[base + 16 + k : base + 24 + k, :]], axis=0
                        )
                else:
                    c = courant[level, 8:24, :]
                    v = {k: state[t, level, 8 + k : 24 + k, :] for k in range(-3, 4)}
                out = stencil(v, c, 0.5 * c * c)
                if outer:
                    zonal[t, level, 0:8, :] = out[:8]
                    zonal[t, level, 24:32, :] = out[8:]
                else:
                    zonal[t, level, 8:24, :] = out
                at = slice(16 * i, 16 * i + 16)
                halves[at, 0:128], halves[at, 128:256] = split(out)
            at = slice(16 * LB * t, 16 * LB * (t + 1))
            edges = jnp.dot(halves[at, :], spread[...], preferred_element_type=f32)
            for l in range(LB):
                mine = group == t * LB + l
                rows = slice(16 * l, 16 * l + 16)
                notes = [jnp.where(mine, edges[rows, 128 * n : 128 * n + 128], notes[n]) for n in range(2)]
        to_left[b, note_rows] = notes[0].astype(bf16)
        to_right[b, note_rows] = notes[1].astype(bf16)
        return 0

    lax.fori_loop(0, courant.shape[0] // LB, block, 0)


def inner_kernel(state, courant, spread, zonal, to_left, to_right, halves):
    zonal_rows(False, state, courant, spread, None, zonal, to_left, to_right, halves, None)


def outer_kernel(state, courant, spread, left, right, _z, _l, _r, zonal, to_left, to_right, halves, pad):
    zonal_rows(True, state, courant, spread, (left, right), zonal, to_left, to_right, halves, pad)


def stencil(v, c, c2):
    slope = D1 * (v[1] - v[-1]) + D2 * (v[2] - v[-2]) + D3 * (v[3] - v[-3])
    curve = E0 * v[0] + E1 * (v[1] + v[-1]) + E2 * (v[2] + v[-2]) + E3 * (v[3] + v[-3])
    return v[0] + c * slope + c2 * curve


def lat_kernel(zonal, courant, weights, result, halves):
    tracers, levels, lons, lats = zonal.shape
    rows = tracers * lons

    def block(b, _):
        for l in range(LB):
            level = b * LB + l
            at = slice(l * rows, (l + 1) * rows)
            halves[at, 0:128], halves[at, 128:256] = split(zonal[:, level].reshape(rows, lats))
        for l in range(LB):
            level = b * LB + l
            at = slice(l * rows, (l + 1) * rows)
            both = jnp.dot(halves[at, :], weights[...], preferred_element_type=f32).reshape(tracers, lons, 256)
            c = courant[level]
            result[:, level] = (
                zonal[:, level] + (c * (1.0 / 60.0)) * both[:, :, :128] + (c * c * (1.0 / 360.0)) * both[:, :, 128:]
            )
        return 0

    lax.fori_loop(0, levels // LB, block, 0)


def column_kernel(first, inner, courant, mixing, inv, q, left, right, weights, *rest):
    lhs = rest[-1]
    if first:
        state, gradient, x_low, x_high = rest[:-1]
    else:
        before, state, gradient = rest[:-1]
    levels = inv.shape[0]
    rows = 32
    lane = lax.broadcasted_iota(jnp.int32, (rows, 128), 1)
    row = lax.broadcasted_iota(jnp.int32, (rows, 128), 0)
    owner = ((lane >> 2) - (row >> 3) * LB).astype(f32).astype(bf16)
    zero = jnp.zeros((), bf16)

    def tile(r, _):
        here = pl.ds(pl.multiple_of(8 * r, 8), 8)
        slot = jnp.where(r == 0, 2, jnp.where(r == 3, 3, r - 1))
        there = pl.ds(pl.multiple_of(8 * slot, 8), 8)
        carry = None
        for b in range(levels // LB):
            notes = [
                jnp.concatenate([side[b, there, :].astype(f32)] * 4, axis=0).astype(bf16) for side in (left, right)
            ]
            for l in range(LB):
                at = slice((b * LB + l) * rows, (b * LB + l + 1) * rows)
                mine = owner == jnp.asarray(l, bf16)
                lhs[at, 0:128] = jnp.where(mine, notes[0], zero)
                lhs[at, 128:256] = jnp.where(mine, notes[1], zero)
            both = jnp.dot(
                lhs[b * LB * rows : (b + 1) * LB * rows, :], weights[...], preferred_element_type=f32
            )
            for l in range(LB):
                level = b * LB + l
                c = courant[level, here, :]
                part = both[l * rows : l * rows + rows].reshape(4, 8, 256)
                y = inner[:, level, here, :]
                y = y + (c * (1.0 / 60.0)) * part[:, :, :128] + (c * c * (1.0 / 360.0)) * part[:, :, 128:]
                if level > 0:
                    y = y + mixing[level - 1, here, :] * carry
                carry = y * inv[level, here, :]
                state[:, level, here, :] = carry

        def back(j, carry):
            level = levels - 2 - j
            carry = state[:, level, here, :] + q[level, here, :] * carry
            state[:, level, here, :] = carry
            return carry

        carry = lax.fori_loop(0, levels - 1, back, carry, unroll=8)
        gradient[:, here, :] = carry if first else before[:, here, :] + carry
        return 0

    lax.fori_loop(0, inner.shape[2] // 8, tile, 0)
    if first:
        for out, order in ((x_low, (0, 1, 2)), (x_high, (31, 30, 29))):
            for t in range(4):
                rows = slice(levels * t, levels * t + levels)
                near, second, third = (state[t, :, j, :] for j in order)
                out[0, rows], out[1, rows] = split(near)
                out[2, rows] = second.astype(bf16)
                out[3, rows] = third.astype(bf16)


def edge_weights():
    table = np.zeros((256, 256), np.float32)
    for lane in range(128):
        part = lane % 4
        table[(128, part)[part < 3], lane] = 1
        table[(255, 125 + part)[part < 3], 128 + lane] = 1
    return table


def lat_weights():
    first = {1: 45, 2: -9, 3: 1}
    second = {0: -490, 1: 270, 2: -27, 3: 2}
    table = np.zeros((512, 256), np.float32)

    def fill(row, place):
        for out in range(128):
            k = place - out
            if abs(k) <= 3:
                table[row, out] = first.get(abs(k), 0) * (1 if k > 0 else -1)
                table[row, 128 + out] = second[abs(k)]

    for lane in range(128):
        fill(lane, lane)
        fill(128 + lane, lane)
        fill(256 + lane, (-3, -2, -1, -1)[lane % 4])
        fill(384 + lane, (128, 129, 130, 128)[lane % 4])
    return table


def cost(flops, size):
    return pl.CostEstimate(flops=flops, bytes_accessed=size, transcendentals=0)


def params(mib):
    return pltpu.CompilerParams(vmem_limit_bytes=mib * 2**20)


def shape(dims, kind=f32):
    return jax.ShapeDtypeStruct(dims, kind)


def shift(value, axis, closed, forward):
    count = lax.axis_size(axis)
    ends = count if closed else count - 1
    pairs = [(i, (i + 1) % count) for i in range(ends)]
    if not forward:
        pairs = [(b, a) for a, b in pairs]
    return lax.ppermute(value, axis, pairs)


def local(adjoint_in, courant_x, courant_y, mixing, kernel_rows, tracer_weights, column_ids, counts):
    tracers, levels, lons, lats = adjoint_in.shape
    devices = lax.axis_size(("gx", "gy"))
    slots = kernel_rows.shape[1]
    fields = tracers * levels
    size = fields * lons * lats * 4

    packed = pl.pallas_call(
        pack_kernel,
        grid=(2,),
        in_specs=[
            pl.BlockSpec(memory_space=pltpu.SMEM),
            pl.BlockSpec((levels, slots // 2), lambda i: (0, i)),
            pl.BlockSpec((tracers, slots // 2), lambda i: (0, i)),
        ],
        out_specs=pl.BlockSpec((devices // 2, 24, 128), lambda i: (i, 0, 0)),
        out_shape=shape((devices, 24, 128), bf16),
        scratch_shapes=[pltpu.VMEM((512, 512), bf16)],
        compiler_params=params(60),
        name="pack",
    )(counts, kernel_rows, tracer_weights)
    got = lax.all_to_all(packed, ("gx", "gy"), split_axis=0, concat_axis=0, tiled=True)

    inv, q = pl.pallas_call(
        factor_kernel,
        out_shape=[shape((levels, lons, lats))] * 2,
        compiler_params=params(16),
        cost_estimate=cost(30 * levels * lons * lats, 3 * levels * lons * lats * 4),
        name="factor",
    )(mixing)
    bins = jnp.broadcast_to((column_ids // (2 * lats)).astype(bf16)[:, None], (slots, 128))
    code, starts = pl.pallas_call(
        rank_kernel,
        out_shape=[shape((slots, 128), bf16), shape((8 * (slots // CHUNK), 128), jnp.int32)],
        compiler_params=params(16),
        cost_estimate=cost(10**9, 2 * 10**6),
        name="rank",
    )(bins)
    lhs, places = pl.pallas_call(
        order_kernel,
        out_shape=[shape((2 * fields, slots), bf16), shape((8, slots))],
        scratch_shapes=[pltpu.VMEM((512, 512), bf16), pltpu.VMEM((80, slots), f32)],
        compiler_params=params(24),
        cost_estimate=cost(10**9, 8 * 10**6),
        name="order",
    )(got, column_ids.reshape(1, slots), code)

    vmem = pl.BlockSpec(memory_space=pltpu.VMEM)
    edge = shape((4, fields, lats), bf16)
    state, x_low, x_high = pl.pallas_call(
        forcing_kernel,
        in_specs=[pl.BlockSpec(memory_space=pltpu.SMEM), vmem, vmem, pl.BlockSpec(memory_space=pl.ANY)],
        out_specs=[vmem] * 3,
        out_shape=[shape((fields, lons, lats)), edge, edge],
        scratch_shapes=[
            pltpu.VMEM((fields, lons, lats), f32),
            pltpu.VMEM((fields * 9, lats), f32),
            pltpu.SemaphoreType.DMA,
        ],
        compiler_params=params(40),
        cost_estimate=cost(10**10, 2 * size),
        name="forcing",
    )(starts, lhs, places, adjoint_in.reshape(fields, lons, lats))

    whole_field = shape((tracers, levels, lons, lats))
    blocks = levels // LB
    note = shape((blocks, lons, 128), bf16)
    spread = jnp.asarray(edge_weights(), bf16)
    table = lat_weights()
    for step in range(STEPS):
        from_left = shift(x_high, "gx", True, True)
        from_right = shift(x_low, "gx", True, False)
        halves = pltpu.VMEM((tracers * LB * 16, 2 * lats), bf16)
        state = state.reshape(tracers, levels, lons, lats)
        partial = pl.pallas_call(
            inner_kernel,
            in_specs=[vmem] * 3,
            out_specs=[vmem] * 3,
            out_shape=[whole_field, note, note],
            scratch_shapes=[halves],
            compiler_params=params(24),
            cost_estimate=cost(5 * size, 2 * size),
            name="inner",
        )(state, courant_x, spread)
        zonal, to_left, to_right = pl.pallas_call(
            outer_kernel,
            in_specs=[vmem] * 8,
            out_specs=[vmem] * 3,
            out_shape=[whole_field, note, note],
            input_output_aliases={5: 0, 6: 1, 7: 2},
            scratch_shapes=[halves, pltpu.VMEM((tracers * LB * 33, lats), f32)],
            compiler_params=params(24),
            cost_estimate=cost(5 * size, 2 * size),
            name="outer",
        )(
            state,
            courant_x,
            spread,
            from_left.reshape(4, tracers, levels, lats),
            from_right.reshape(4, tracers, levels, lats),
            *partial,
        )
        y_left = shift(to_right, "gy", False, True)
        y_right = shift(to_left, "gy", False, False)
        inner = pl.pallas_call(
            lat_kernel,
            in_specs=[vmem] * 3,
            out_specs=vmem,
            out_shape=whole_field,
            scratch_shapes=[pltpu.VMEM((LB * tracers * lons, 2 * lats), bf16)],
            compiler_params=params(24),
            cost_estimate=cost(5 * size, 2 * size),
            name="lat",
        )(zonal, courant_y, jnp.asarray(table[:256], bf16))
        first = step == 0
        operands = [inner, courant_y, mixing, inv, q, y_left, y_right, jnp.asarray(table[256:], bf16)]
        out_shape = [whole_field, shape((tracers, lons, lats))]
        if first:
            out_shape += [edge, edge]
        else:
            operands.append(gradient)

        def kernel(*refs, first=first):
            column_kernel(first, *refs)

        out = pl.pallas_call(
            kernel,
            in_specs=[vmem] * len(operands),
            out_specs=[vmem] * len(out_shape),
            out_shape=out_shape,
            scratch_shapes=[pltpu.VMEM((levels * tracers * 8, 2 * lats), bf16)],
            compiler_params=params(24),
            cost_estimate=cost(5 * size, 2 * size),
            name="column",
        )(*operands)
        if first:
            state, gradient, x_low, x_high = out
        else:
            state, gradient = out
    return state, gradient


def solution(mesh):
    in_specs = (
        P(None, None, "gx", "gy"),
        P(None, "gx", "gy"),
        P(None, "gx", "gy"),
        P(None, "gx", "gy"),
        P(None, ("gx", "gy")),
        P(None, ("gx", "gy")),
        P(("gx", "gy")),
        P(("gx", "gy"), None),
    )
    out_specs = (P(None, None, "gx", "gy"), P(None, "gx", "gy"))
    return jax.shard_map(local, mesh=mesh, in_specs=in_specs, out_specs=out_specs, check_vma=False)
```

time: 129 us -> 105 us (0.81)
  Pallas kernels: 59 us -> 48.3 us
  waiting for transfers between devices: 33.3 us -> 22.6 us
  local copies, waits for them, and re-layouts: 2.97 us -> 0.64 us
    ppermute x8, waiting for transfers between devices: 21.8 us -> 11 us  [shift(): return lax.ppermute(value, axis, pairs)]
    pallas_call x6 -> x10, Pallas kernels: 52.7 us -> 42 us  [the longest x2 11.9 us: local(): pl.pallas_call(kernel, in_specs=[vmem] * len(operands), out_specs=[vmem]...]
    unnamed x14, local copies, waits for them, and re-layouts: 2.37 us -> 0.04 us
  transfers between devices with their start and end apart: 9 -> 9, of which waited for: 6 -> 5; matrix products, arithmetic and copies ran while one was open for 1% -> 1% of each run, Pallas kernels for 2% -> 14%
where the time goes in v3:
time: 105 us; the launch traced here: 104 us
  Pallas kernels  48.3 us (46%)
  starting transfers between devices  31.3 us (30%)
  waiting for transfers between devices  22.6 us (22%)
    ppermute x8, starting transfers between devices, shift(): return lax.ppermute(value, axis, pairs)  21 us
    pallas_call x2, Pallas kernels, local(): pl.pallas_call(kernel, in_specs=[vmem] * len(operands), out_specs=[vmem]...  11.9 us
    all_to_all x1, waiting for transfers between devices, local(): lax.all_to_all(packed, ('gx', 'gy'), split_axis=0, concat_axis=0, tiled=T...  11.6 us
    ppermute x8, waiting for transfers between devices, shift(): return lax.ppermute(value, axis, pairs)  11 us
    all_to_all x1, starting transfers between devices, local(): lax.all_to_all(packed, ('gx', 'gy'), split_axis=0, concat_axis=0, tiled=T...  10.3 us
    pallas_call x1, Pallas kernels, local(): pl.pallas_call(forcing_kernel, in_specs=[pl.BlockSpec(memory_space=pltpu....  8.66 us
    pallas_call x2, Pallas kernels, local(): pl.pallas_call(outer_kernel, in_specs=[vmem] * 8, out_specs=[vmem] * 3, o...  6.66 us
    pallas_call x2, Pallas kernels, local(): pl.pallas_call(inner_kernel, in_specs=[vmem] * 3, out_specs=[vmem] * 3, o...  6.46 us
  transfers between devices with their start and end apart: 9, of which 5 were waited for; matrix products, arithmetic and copies ran while one was open for 1% of the time, Pallas kernels for 14%

profile of v3, /device:TPU:24, one launch (start us, length us, event | category | flops | bytes accessed | tf_op | source)
XLA Modules:
  0.0 104.5 jit_solution(12007137941913048591)
XLA Ops:
  0.6 0.0 copy-start.6
  0.6 2.6 %pack.1 = bf16[128,24,128]{2,1,0:T(8,128)(2,1)} custom-call(s32[1,128]{1,0:T(1,128)} %counts.1, bf16[72,4096]{1,0:T(8,128)(2,1)} %rows.1, bf16[4,4096]{1,0:T(4,128)(2,1)} %weights.3), custom_call_target="tpu_custom_call" | custom-call | tf_op jit(solution)/shard_map/pack/pallas_call | solution.py:469
  3.3 10.3 %all-to-all-start = ((bf16[128,24,128]{2,1,0:T(8,128)(2,1)}), bf16[128,24,128]{2,1,0:T(8,128)(2,1)S(1)}, u32[]{:S(2)}, u32[]{:S(2)}) async-start(bf16[128,24,128]{2,1,0:T(8,128)(2,1)} %pack.1), calls=%async_computation | async-start | bytes 1572864 | tf_op jit(solution)/shard_map/all_to_all | solution.py:483
  13.5 0.7 fusion.1
  14.3 0.6 broadcast_in_dim.2.bins
  14.9 1.9 %rank.1 = (bf16[4096,128]{1,0:T(8,128)(2,1)S(1)}, s32[32,128]{1,0:T(8,128)S(1)}) custom-call(bf16[4096,128]{1,0:T(8,128)(2,1)S(1)} %broadcast_in_dim.2.bins), custom_call_target="tpu_custom_call" | custom-call | flops 1000000000 | bytes 2000000 | tf_op jit(solution)/shard_map/rank/pallas_call | solution.py:493
  16.8 11.6 %all-to-all-done.got = bf16[128,24,128]{2,1,0:T(8,128)(2,1)S(1)} async-done(((bf16[128,24,128]{2,1,0:T(8,128)(2,1)}), bf16[128,24,128]{2,1,0:T(8,128)(2,1)S(1)}, u32[]{:S(2)}, u32[]{:S(2)}) %all-to-all-start) | async-done | bytes 786464 | tf_op jit(solution)/shard_map/all_to_all | solution.py:483
  28.4 3.5 %order.1 = (bf16[576,4096]{1,0:T(8,128)(2,1)S(1)}, f32[8,4096]{1,0:T(8,128)S(1)}) custom-call(bf16[128,24,128]{2,1,0:T(8,128)(2,1)S(1)} %all-to-all-done.got, s32[1,4096]{1,0:T(1,128)S(1)} %bitcast.13, bf16[4096,128]{1,0:T(8,128)(2,1)S(1)} %get-tuple-element.28.code), custom_call_target="tpu_custom_call" | custom-call | flops 1000000000 | bytes 8000000 | tf_op jit(solution)/shard_map/order/pallas_call | solution.py:500
  32.0 0.0 copy-start.3
  32.0 8.7 %forcing.1 = (f32[288,32,128]{2,1,0:T(8,128)S(1)}, bf16[4,288,128]{2,1,0:T(8,128)(2,1)S(1)}, bf16[4,288,128]{2,1,0:T(8,128)(2,1)S(1)}) custom-call(s32[32,128]{1,0:T(8,128)S(1)} %get-tuple-element.27.starts, bf16[576,4096]{1,0:T(8,128)(2,1)S(1)} %get-tuple-element.29.lhs, f32[8,4096]{1,0:T(8,128)S(1)} %get-tuple-element.30.places, f32[288,32,128]{2,1,0:T(8,128)} %bitcast.14), custom_call_target="tpu_custom_call" | custom-call | flops 10000000000 | bytes 9437184 | tf_op jit(solution)/shard_map/forcing/pallas_call | solution.py:511
  40.6 0.1 collective-permute-start
  40.7 3.8 %collective-permute-start.1 = (bf16[4,288,128]{2,1,0:T(8,128)(2,1)S(1)}, bf16[4,288,128]{2,1,0:T(8,128)(2,1)S(1)}, u32[]{:S(2)}, u32[]{:S(2)}) collective-permute-start(bf16[4,288,128]{2,1,0:T(8,128)(2,1)S(1)} %get-tuple-element.33), channel_id=1, source_target_pairs={{8,0},{16,8},{24,16},{32,24},{40,32},{48,40},{56,48},{64,56},{72,6... | collective-permute-start | bytes 884744 | tf_op jit(solution)/shard_map/ppermute | solution.py:459
  44.6 3.2 %inner.2 = (f32[4,72,32,128]{3,2,1,0:T(8,128)S(1)}, bf16[9,32,128]{2,1,0:T(8,128)(2,1)S(1)}, bf16[9,32,128]{2,1,0:T(8,128)(2,1)S(1)}) custom-call(f32[4,72,32,128]{3,2,1,0:T(8,128)S(1)} %bitcast.7, f32[72,32,128]{2,1,0:T(8,128)S(1)} %copy-done.1, bf16[256,256]{1,0:T(8,128)(2,1)S(1)} %copy-done.3), custom_call_target="tpu_custom_call" | custom-call | flops 23592960 | bytes 9437184 | tf_op jit(solution)/shard_map/inner/pallas_call | solution.py:536
  47.8 1.2 %collective-permute-done = bf16[4,288,128]{2,1,0:T(8,128)(2,1)S(1)} collective-permute-done((bf16[4,288,128]{2,1,0:T(8,128)(2,1)S(1)}, bf16[4,288,128]{2,1,0:T(8,128)(2,1)S(1)}, u32[]{:S(2)}, u32[]{:S(2)}) %collective-permute-start) | collective-permute-done | bytes 294944 | tf_op jit(solution)/shard_map/ppermute | solution.py:459
  49.0 3.3 %outer.2 = (f32[4,72,32,128]{3,2,1,0:T(8,128)S(1)}, bf16[9,32,128]{2,1,0:T(8,128)(2,1)S(1)}, bf16[9,32,128]{2,1,0:T(8,128)(2,1)S(1)}) custom-call(f32[4,72,32,128]{3,2,1,0:T(8,128)S(1)} %bitcast.8, f32[72,32,128]{2,1,0:T(8,128)S(1)} %copy-done.1, bf16[256,256]{1,0:T(8,128)(2,1)S(1)} %copy-done.3, ...), custom_call_target="tpu_custom_call", output_to_operand_aliasing={{0}: (5, {}), {1}: (6, {}), {2}: (7, {})} | custom-call | flops 23592960 | bytes 9437184 | tf_op jit(solution)/shard_map/outer/pallas_call | solution.py:546
  52.3 5.2 %collective-permute-start.2 = (bf16[9,32,128]{2,1,0:T(8,128)(2,1)S(1)}, bf16[9,32,128]{2,1,0:T(8,128)(2,1)S(1)}, u32[]{:S(2)}, u32[]{:S(2)}) collective-permute-start(bf16[9,32,128]{2,1,0:T(8,128)(2,1)S(1)} %get-tuple-element.40), channel_id=1, source_target_pairs={{0,1},{1,2},{2,3},{3,4},{4,5},{5,6},{6,7},{8,9},{9,10},{10,11},{11... | collective-permute-start | bytes 221192 | tf_op jit(solution)/shard_map/ppermute | solution.py:459
  57.6 2.1 %collective-permute-start.3 = (bf16[9,32,128]{2,1,0:T(8,128)(2,1)S(1)}, bf16[9,32,128]{2,1,0:T(8,128)(2,1)S(1)}, u32[]{:S(2)}, u32[]{:S(2)}) collective-permute-start(bf16[9,32,128]{2,1,0:T(8,128)(2,1)S(1)} %get-tuple-element.41), channel_id=1, source_target_pairs={{1,0},{2,1},{3,2},{4,3},{5,4},{6,5},{7,6},{9,8},{10,9},{11,10},{12... | collective-permute-start | bytes 221192 | tf_op jit(solution)/shard_map/ppermute | solution.py:459
  59.7 0.9 factor.1
  60.6 0.0 copy-start.4
  60.6 2.9 %lat.2.refs_0_ = f32[4,72,32,128]{3,2,1,0:T(8,128)S(1)} custom-call(f32[4,72,32,128]{3,2,1,0:T(8,128)S(1)} %get-tuple-element.37.zonal, f32[72,32,128]{2,1,0:T(8,128)S(1)} %copy-done, bf16[256,256]{1,0:T(8,128)(2,1)S(1)} %copy-done.5), custom_call_target="tpu_custom_call" | custom-call | flops 23592960 | bytes 9437184 | tf_op jit(solution)/shard_map/lat/pallas_call | solution.py:566
  63.5 3.9 %collective-permute-done.3.refs_6_ = bf16[9,32,128]{2,1,0:T(8,128)(2,1)S(1)} collective-permute-done((bf16[9,32,128]{2,1,0:T(8,128)(2,1)S(1)}, bf16[9,32,128]{2,1,0:T(8,128)(2,1)S(1)}, u32[]{:S(2)}, u32[]{:S(2)}) %collective-permute-start.3) | collective-permute-done | bytes 73760 | tf_op jit(solution)/shard_map/ppermute | solution.py:459
  67.4 5.5 %column.2 = (f32[4,72,32,128]{3,2,1,0:T(8,128)S(1)}, f32[4,32,128]{2,1,0:T(8,128)S(1)}, bf16[4,288,128]{2,1,0:T(8,128)(2,1)S(1)}, bf16[4,288,128]{2,1,0:T(8,128)(2,1)S(1)}) custom-call(f32[4,72,32,128]{3,2,1,0:T(8,128)S(1)} %lat.2.refs_0_, f32[72,32,128]{2,1,0:T(8,128)S(1)} %copy-done, f32[71,32,128]{2,1,0:T(8,128)S(1)} %copy-done.2, ...), custom_call_target="tpu_custom_call" | custom-call | flops 23592960 | bytes 9437184 | tf_op jit(solution)/shard_map/column/pallas_call | solution.py:587
  72.9 0.1 collective-permute-start.4
  73.0 3.8 %collective-permute-start.5 = (bf16[4,288,128]{2,1,0:T(8,128)(2,1)S(1)}, bf16[4,288,128]{2,1,0:T(8,128)(2,1)S(1)}, u32[]{:S(2)}, u32[]{:S(2)}) collective-permute-start(bf16[4,288,128]{2,1,0:T(8,128)(2,1)S(1)} %get-tuple-element.44), channel_id=1, source_target_pairs={{8,0},{16,8},{24,16},{32,24},{40,32},{48,40},{56,48},{64,56},{72,6... | collective-permute-start | bytes 884744 | tf_op jit(solution)/shard_map/ppermute | solution.py:459
  76.9 3.2 %inner.3 = (f32[4,72,32,128]{3,2,1,0:T(8,128)S(1)}, bf16[9,32,128]{2,1,0:T(8,128)(2,1)S(1)}, bf16[9,32,128]{2,1,0:T(8,128)(2,1)S(1)}) custom-call(f32[4,72,32,128]{3,2,1,0:T(8,128)S(1)} %get-tuple-element.42.state, f32[72,32,128]{2,1,0:T(8,128)S(1)} %copy-done.1, bf16[256,256]{1,0:T(8,128)(2,1)S(1)} %copy-done.3), custom_call_target="tpu_custom_call" | custom-call | flops 23592960 | bytes 9437184 | tf_op jit(solution)/shard_map/inner/pallas_call | solution.py:536
  80.1 1.2 %collective-permute-done.4 = bf16[4,288,128]{2,1,0:T(8,128)(2,1)S(1)} collective-permute-done((bf16[4,288,128]{2,1,0:T(8,128)(2,1)S(1)}, bf16[4,288,128]{2,1,0:T(8,128)(2,1)S(1)}, u32[]{:S(2)}, u32[]{:S(2)}) %collective-permute-start.4) | collective-permute-done | bytes 294944 | tf_op jit(solution)/shard_map/ppermute | solution.py:459
  81.3 3.3 %outer.3 = (f32[4,72,32,128]{3,2,1,0:T(8,128)S(1)}, bf16[9,32,128]{2,1,0:T(8,128)(2,1)S(1)}, bf16[9,32,128]{2,1,0:T(8,128)(2,1)S(1)}) custom-call(f32[4,72,32,128]{3,2,1,0:T(8,128)S(1)} %get-tuple-element.42.state, f32[72,32,128]{2,1,0:T(8,128)S(1)} %copy-done.1, ...), custom_call_target="tpu_custom_call", output_to_operand_aliasing={{0}: (5, {}), {1}: (6, {}), {2}: (7, {})} | custom-call | flops 23592960 | bytes 9437184 | tf_op jit(solution)/shard_map/outer/pallas_call | solution.py:546
  84.6 3.6 %collective-permute-start.6 = (bf16[9,32,128]{2,1,0:T(8,128)(2,1)S(1)}, bf16[9,32,128]{2,1,0:T(8,128)(2,1)S(1)}, u32[]{:S(2)}, u32[]{:S(2)}) collective-permute-start(bf16[9,32,128]{2,1,0:T(8,128)(2,1)S(1)} %get-tuple-element.49), channel_id=1, source_target_pairs={{0,1},{1,2},{2,3},{3,4},{4,5},{5,6},{6,7},{8,9},{9,10},{10,11},{11... | collective-permute-start | bytes 221192 | tf_op jit(solution)/shard_map/ppermute | solution.py:459
  88.2 2.2 %collective-permute-start.7 = (bf16[9,32,128]{2,1,0:T(8,128)(2,1)S(1)}, bf16[9,32,128]{2,1,0:T(8,128)(2,1)S(1)}, u32[]{:S(2)}, u32[]{:S(2)}) collective-permute-start(bf16[9,32,128]{2,1,0:T(8,128)(2,1)S(1)} %get-tuple-element.50), channel_id=1, source_target_pairs={{1,0},{2,1},{3,2},{4,3},{5,4},{6,5},{7,6},{9,8},{10,9},{11,10},{12... | collective-permute-start | bytes 221192 | tf_op jit(solution)/shard_map/ppermute | solution.py:459
  90.5 2.9 %lat.3.refs_0_ = f32[4,72,32,128]{3,2,1,0:T(8,128)S(1)} custom-call(f32[4,72,32,128]{3,2,1,0:T(8,128)S(1)} %get-tuple-element.48.zonal, f32[72,32,128]{2,1,0:T(8,128)S(1)} %copy-done, bf16[256,256]{1,0:T(8,128)(2,1)S(1)} %copy-done.5), custom_call_target="tpu_custom_call" | custom-call | flops 23592960 | bytes 9437184 | tf_op jit(solution)/shard_map/lat/pallas_call | solution.py:566
  93.3 4.8 %collective-permute-done.7.refs_6_ = bf16[9,32,128]{2,1,0:T(8,128)(2,1)S(1)} collective-permute-done((bf16[9,32,128]{2,1,0:T(8,128)(2,1)S(1)}, bf16[9,32,128]{2,1,0:T(8,128)(2,1)S(1)}, u32[]{:S(2)}, u32[]{:S(2)}) %collective-permute-start.7) | collective-permute-done | bytes 73760 | tf_op jit(solution)/shard_map/ppermute | solution.py:459
  98.1 6.4 %column.3 = (f32[4,72,32,128]{3,2,1,0:T(8,128)}, f32[4,32,128]{2,1,0:T(8,128)}) custom-call(f32[4,72,32,128]{3,2,1,0:T(8,128)S(1)} %lat.3.refs_0_, f32[72,32,128]{2,1,0:T(8,128)S(1)} %copy-done, f32[71,32,128]{2,1,0:T(8,128)S(1)} %copy-done.2, f32[72,32,128]{2,1,0:T(8,128)S(1)} %get-tuple-element.38.refs_3_, f32[72,32,128]{2,1,0:T(8,128)S(1)} %get-tuple-element.39.refs_4_, ...), custom_call_target="tpu_custom_call" | custom-call | flops 23592960 | bytes 9437184 | tf_op jit(solution)/shard_map/column/pallas_call | solution.py:587
  (15 shorter events, 0.0 us)
Async XLA Ops:
  0.6 27.8 %copy-start.6 = (s32[4096]{0:T(1024)S(1)}, s32[4096]{0:T(1024)}, u32[]{:S(2)}) copy-start(s32[4096]{0:T(1024)} %param.19) | copy-start | bytes 49156
  3.3 25.1 %all-to-all-start = ((bf16[128,24,128]{2,1,0:T(8,128)(2,1)}), bf16[128,24,128]{2,1,0:T(8,128)(2,1)S(1)}, u32[]{:S(2)}, u32[]{:S(2)}) async-start(bf16[128,24,128]{2,1,0:T(8,128)(2,1)} %pack.1), calls=%async_computation | async-start | bytes 1572864 | tf_op jit(solution)/shard_map/all_to_all | solution.py:483
  31.9 12.6 %copy-start.1 = (f32[72,32,128]{2,1,0:T(8,128)S(1)}, f32[72,32,128]{2,1,0:T(8,128)}, u32[]{:S(2)}) copy-start(f32[72,32,128]{2,1,0:T(8,128)} %courant.10) | copy-start | bytes 3538948
  32.0 12.6 %copy-start.3 = (bf16[256,256]{1,0:T(8,128)(2,1)S(1)}, bf16[256,256]{1,0:T(8,128)(2,1)}, u32[]{:S(2)}) copy-start(bf16[256,256]{1,0:T(8,128)(2,1)} %constant.22.clone.spread) | copy-start | bytes 393220
  40.6 8.3 %collective-permute-start = (bf16[4,288,128]{2,1,0:T(8,128)(2,1)S(1)}, bf16[4,288,128]{2,1,0:T(8,128)(2,1)S(1)}, u32[]{:S(2)}, u32[]{:S(2)}) collective-permute-start(bf16[4,288,128]{2,1,0:T(8,128)(2,1)S(1)} %get-tuple-element.32), channel_id=1, source_target_pairs={{0,8},{8,16},{16,24},{24,32},{32,40},{40,48},{48,56},{56,64},{64,7... | collective-permute-start | bytes 884744 | tf_op jit(solution)/shard_map/ppermute | solution.py:459
  40.7 8.2 %collective-permute-start.1 = (bf16[4,288,128]{2,1,0:T(8,128)(2,1)S(1)}, bf16[4,288,128]{2,1,0:T(8,128)(2,1)S(1)}, u32[]{:S(2)}, u32[]{:S(2)}) collective-permute-start(bf16[4,288,128]{2,1,0:T(8,128)(2,1)S(1)} %get-tuple-element.33), channel_id=1, source_target_pairs={{8,0},{16,8},{24,16},{32,24},{40,32},{48,40},{56,48},{64,56},{72,6... | collective-permute-start | bytes 884744 | tf_op jit(solution)/shard_map/ppermute | solution.py:459
  49.0 10.7 %copy-start.2 = (f32[71,32,128]{2,1,0:T(8,128)S(1)}, f32[71,32,128]{2,1,0:T(8,128)}, u32[]{:S(2)}) copy-start(f32[71,32,128]{2,1,0:T(8,128)} %refs_2_.3) | copy-start | bytes 3489796
  49.0 11.6 %copy-start = (f32[72,32,128]{2,1,0:T(8,128)S(1)}, f32[72,32,128]{2,1,0:T(8,128)}, u32[]{:S(2)}) copy-start(f32[72,32,128]{2,1,0:T(8,128)} %refs_1_.3) | copy-start | bytes 3538948
  49.0 11.6 %copy-start.5 = (bf16[256,256]{1,0:T(8,128)(2,1)S(1)}, bf16[256,256]{1,0:T(8,128)(2,1)}, u32[]{:S(2)}) copy-start(bf16[256,256]{1,0:T(8,128)(2,1)} %constant.23.clone.weights) | copy-start | bytes 393220
  52.3 11.2 %collective-permute-start.2 = (bf16[9,32,128]{2,1,0:T(8,128)(2,1)S(1)}, bf16[9,32,128]{2,1,0:T(8,128)(2,1)S(1)}, u32[]{:S(2)}, u32[]{:S(2)}) collective-permute-start(bf16[9,32,128]{2,1,0:T(8,128)(2,1)S(1)} %get-tuple-element.40), channel_id=1, source_target_pairs={{0,1},{1,2},{2,3},{3,4},{4,5},{5,6},{6,7},{8,9},{9,10},{10,11},{11... | collective-permute-start | bytes 221192 | tf_op jit(solution)/shard_map/ppermute | solution.py:459
  57.6 9.9 %collective-permute-start.3 = (bf16[9,32,128]{2,1,0:T(8,128)(2,1)S(1)}, bf16[9,32,128]{2,1,0:T(8,128)(2,1)S(1)}, u32[]{:S(2)}, u32[]{:S(2)}) collective-permute-start(bf16[9,32,128]{2,1,0:T(8,128)(2,1)S(1)} %get-tuple-element.41), channel_id=1, source_target_pairs={{1,0},{2,1},{3,2},{4,3},{5,4},{6,5},{7,6},{9,8},{10,9},{11,10},{12... | collective-permute-start | bytes 221192 | tf_op jit(solution)/shard_map/ppermute | solution.py:459
  60.6 6.8 %copy-start.4 = (bf16[256,256]{1,0:T(8,128)(2,1)S(1)}, bf16[256,256]{1,0:T(8,128)(2,1)}, u32[]{:S(2)}) copy-start(bf16[256,256]{1,0:T(8,128)(2,1)} %constant.24.clone.refs_7_) | copy-start | bytes 393220
  72.9 8.3 %collective-permute-start.4 = (bf16[4,288,128]{2,1,0:T(8,128)(2,1)S(1)}, bf16[4,288,128]{2,1,0:T(8,128)(2,1)S(1)}, u32[]{:S(2)}, u32[]{:S(2)}) collective-permute-start(bf16[4,288,128]{2,1,0:T(8,128)(2,1)S(1)} %get-tuple-element.43), channel_id=1, source_target_pairs={{0,8},{8,16},{16,24},{24,32},{32,40},{40,48},{48,56},{56,64},{64,7... | collective-permute-start | bytes 884744 | tf_op jit(solution)/shard_map/ppermute | solution.py:459
  73.0 8.2 %collective-permute-start.5 = (bf16[4,288,128]{2,1,0:T(8,128)(2,1)S(1)}, bf16[4,288,128]{2,1,0:T(8,128)(2,1)S(1)}, u32[]{:S(2)}, u32[]{:S(2)}) collective-permute-start(bf16[4,288,128]{2,1,0:T(8,128)(2,1)S(1)} %get-tuple-element.44), channel_id=1, source_target_pairs={{8,0},{16,8},{24,16},{32,24},{40,32},{48,40},{56,48},{64,56},{72,6... | collective-permute-start | bytes 884744 | tf_op jit(solution)/shard_map/ppermute | solution.py:459
  84.6 8.7 %collective-permute-start.6 = (bf16[9,32,128]{2,1,0:T(8,128)(2,1)S(1)}, bf16[9,32,128]{2,1,0:T(8,128)(2,1)S(1)}, u32[]{:S(2)}, u32[]{:S(2)}) collective-permute-start(bf16[9,32,128]{2,1,0:T(8,128)(2,1)S(1)} %get-tuple-element.49), channel_id=1, source_target_pairs={{0,1},{1,2},{2,3},{3,4},{4,5},{5,6},{6,7},{8,9},{9,10},{10,11},{11... | collective-permute-start | bytes 221192 | tf_op jit(solution)/shard_map/ppermute | solution.py:459
  88.2 9.9 %collective-permute-start.7 = (bf16[9,32,128]{2,1,0:T(8,128)(2,1)S(1)}, bf16[9,32,128]{2,1,0:T(8,128)(2,1)S(1)}, u32[]{:S(2)}, u32[]{:S(2)}) collective-permute-start(bf16[9,32,128]{2,1,0:T(8,128)(2,1)S(1)} %get-tuple-element.50), channel_id=1, source_target_pairs={{1,0},{2,1},{3,2},{4,3},{5,4},{6,5},{7,6},{9,8},{10,9},{11,10},{12... | collective-permute-start | bytes 221192 | tf_op jit(solution)/shard_map/ppermute | solution.py:459

commit v4 on v3

--- a/solution.py
+++ b/solution.py
@@ -23,6 +23,10 @@
     col = lax.broadcasted_iota(jnp.int32, table.shape, 1)
     want = ((col >> 5) & 3) * 128 + (col >> 7) * 32 + (col & 31)
     table[...] = jnp.where(row == want, 1.0, 0.0).astype(bf16)
+
+
+def is_odd(axis):
+    return (lax.axis_index(axis) & 1) == 1
 
 
 def split(value):
@@ -154,7 +158,7 @@
                 lhs[half + 72 * t : half + 72 * t + 72, lanes] = lo
 
 
-def forcing_kernel(starts, lhs, places, adjoint_hbm, state, x_low, x_high, adjoint, turned, arrived):
+def forcing_kernel(starts, lhs, places, adjoint_hbm, state, x_a, x_b, adjoint, turned, arrived):
     copy = pltpu.make_async_copy(adjoint_hbm, adjoint, arrived)
     copy.start()
     fields = state.shape[0]
@@ -164,22 +168,27 @@
     row = lax.broadcasted_iota(jnp.int32, (128, 256), 0).astype(f32)
     window = lax.broadcasted_iota(jnp.int32, (1, 256), 1)
 
-    def product(base, lon, skip):
+    def placed(base, lon, skip):
         lat = places[4:5, pl.ds(base, 256)]
         slot_lon = places[5:6, pl.ds(base, 256)]
         if skip is not None:
             slot_lon = jnp.where(window >= skip, slot_lon, -1.0)
-        one_hot = jnp.concatenate(
+        return jnp.concatenate(
             [
                 jnp.where(jnp.where(slot_lon == (lon + a).astype(f32), lat, -1.0) == row, 1.0, 0.0).astype(bf16)
                 for a in range(2)
             ],
             axis=0,
         )
-        both = lax.dot_general(
-            lhs[:, pl.ds(base, 256)], one_hot, (((1,), (1,)), ((), ())), preferred_element_type=f32
+
+    def product(bases, one_hots):
+        values = [lhs[at, pl.ds(base, 256)] for at in (slice(0, fields), slice(fields, 2 * fields)) for base in bases]
+        return lax.dot_general(
+            jnp.concatenate(values, axis=1),
+            jnp.concatenate(one_hots * 2, axis=1),
+            (((1,), (1,)), ((), ())),
+            preferred_element_type=f32,
         )
-        return both
 
     def extent(h, number):
         low = starts[8 * h, number]
@@ -191,13 +200,12 @@
         rest = jnp.int32(0)
         for pair in range(4):
             number = step * 4 + pair
-            total = None
+            bases = []
             for h in range(chunks):
                 first, visits = extent(h, number)
                 rest = rest + visits
-                piece = product(pl.multiple_of(h * CHUNK + first * 128, 128), 2 * number, None)
-                total = piece if total is None else total + piece
-            total = total[:fields] + total[fields:]
+                bases.append(pl.multiple_of(h * CHUNK + first * 128, 128))
+            total = product(bases, [placed(base, 2 * number, None) for base in bases])
             for a in range(2):
                 turned[pl.ds(2 * pair + a, fields, stride=9), :] = total[:, 128 * a : 128 * a + 128]
 
@@ -212,8 +220,7 @@
                     at = first + 2 + 2 * j
                     start = jnp.minimum(at, last)
                     base = pl.multiple_of(h * CHUNK + start * 128, 128)
-                    both = product(base, 2 * number, (at - start) * 128)
-                    both = both[:fields] + both[fields:]
+                    both = product([base], [placed(base, 2 * number, (at - start) * 128)])
                     for a in range(2):
                         place = pl.ds(2 * pair + a, fields, stride=9)
                         turned[place, :] = turned[place, :] + both[:, 128 * a : 128 * a + 128]
@@ -240,32 +247,37 @@
             out[2] = second.astype(bf16)
             out[3] = third.astype(bf16)
 
-        @pl.when(step == 0)
-        def _():
-            edge(x_low, (0, 1, 2))
-
-        @pl.when(step == steps - 1)
-        def _():
-            edge(x_high, (7, 6, 5))
+        odd = is_odd("gx")
+        for when, order, swapped in ((0, (0, 1, 2), odd), (steps - 1, (7, 6, 5), jnp.logical_not(odd))):
+            for out, mine in ((x_a, swapped), (x_b, jnp.logical_not(swapped))):
+
+                @pl.when((step == when) & mine)
+                def _(out=out, order=order):
+                    edge(out, order)
 
         return 0
 
     lax.fori_loop(0, steps, eight, 0)
 
 
-def zonal_rows(outer, state, courant, spread, halos, zonal, to_left, to_right, halves, pad):
+def zonal_rows(outer, state, courant, spread, halos, zonal, to_a, to_b, halves, pad):
     lane = lax.broadcasted_iota(jnp.int32, (16, 128), 1)
     group = lane >> 2
     note_rows = slice(16, 32) if outer else slice(0, 16)
+    odd_x = is_odd("gx")
+    odd_y = is_odd("gy")
 
     def block(b, _):
         levels = pl.ds(pl.multiple_of(b * LB, LB), LB)
         if outer:
             for t in range(4):
-                for side, halo in enumerate(halos):
-                    near = halo[0, t, levels, :].astype(f32) + halo[1, t, levels, :].astype(f32)
-                    far = (halo[2, t, levels, :].astype(f32), halo[3, t, levels, :].astype(f32))
-                    for k, value in enumerate((near, *far)):
+                parts = []
+                for halo in halos:
+                    part = [halo[n, t, levels, :].astype(f32) for n in range(4)]
+                    parts.append((part[0] + part[1], part[2], part[3]))
+                for side in range(2):
+                    for k in range(3):
+                        value = jnp.where(odd_x, parts[side][k], parts[1 - side][k])
                         pad[pl.ds(t * LB * 33 + (24 + k if side else 7 - k), LB, stride=33), :] = value
         notes = [jnp.zeros((16, 128), f32)] * 2
         for t in range(4):
@@ -304,19 +316,19 @@
                 mine = group == t * LB + l
                 rows = slice(16 * l, 16 * l + 16)
                 notes = [jnp.where(mine, edges[rows, 128 * n : 128 * n + 128], notes[n]) for n in range(2)]
-        to_left[b, note_rows] = notes[0].astype(bf16)
-        to_right[b, note_rows] = notes[1].astype(bf16)
+        to_a[b, note_rows] = jnp.where(odd_y, notes[0], notes[1]).astype(bf16)
+        to_b[b, note_rows] = jnp.where(odd_y, notes[1], notes[0]).astype(bf16)
         return 0
 
     lax.fori_loop(0, courant.shape[0] // LB, block, 0)
 
 
-def inner_kernel(state, courant, spread, zonal, to_left, to_right, halves):
-    zonal_rows(False, state, courant, spread, None, zonal, to_left, to_right, halves, None)
-
-
-def outer_kernel(state, courant, spread, left, right, _z, _l, _r, zonal, to_left, to_right, halves, pad):
-    zonal_rows(True, state, courant, spread, (left, right), zonal, to_left, to_right, halves, pad)
+def inner_kernel(state, courant, spread, zonal, to_a, to_b, halves):
+    zonal_rows(False, state, courant, spread, None, zonal, to_a, to_b, halves, None)
+
+
+def outer_kernel(state, courant, spread, from_a, from_b, _z, _a, _b, zonal, to_a, to_b, halves, pad):
+    zonal_rows(True, state, courant, spread, (from_a, from_b), zonal, to_a, to_b, halves, pad)
 
 
 def stencil(v, c, c2):
@@ -347,10 +359,10 @@
     lax.fori_loop(0, levels // LB, block, 0)
 
 
-def column_kernel(first, inner, courant, mixing, inv, q, left, right, weights, *rest):
+def column_kernel(first, inner, courant, mixing, inv, q, from_a, from_b, weights, *rest):
     lhs = rest[-1]
     if first:
-        state, gradient, x_low, x_high = rest[:-1]
+        state, gradient, x_a, x_b = rest[:-1]
     else:
         before, state, gradient = rest[:-1]
     levels = inv.shape[0]
@@ -359,6 +371,7 @@
     row = lax.broadcasted_iota(jnp.int32, (rows, 128), 0)
     owner = ((lane >> 2) - (row >> 3) * LB).astype(f32).astype(bf16)
     zero = jnp.zeros((), bf16)
+    odd_y = is_odd("gy")
 
     def tile(r, _):
         here = pl.ds(pl.multiple_of(8 * r, 8), 8)
@@ -366,8 +379,10 @@
         there = pl.ds(pl.multiple_of(8 * slot, 8), 8)
         carry = None
         for b in range(levels // LB):
+            a, z = from_a[b, there, :].astype(f32), from_b[b, there, :].astype(f32)
             notes = [
-                jnp.concatenate([side[b, there, :].astype(f32)] * 4, axis=0).astype(bf16) for side in (left, right)
+                jnp.concatenate([note] * 4, axis=0).astype(bf16)
+                for note in (jnp.where(odd_y, a, z), jnp.where(odd_y, z, a))
             ]
             for l in range(LB):
                 at = slice((b * LB + l) * rows, (b * LB + l + 1) * rows)
@@ -400,13 +415,26 @@
 
     lax.fori_loop(0, inner.shape[2] // 8, tile, 0)
     if first:
-        for out, order in ((x_low, (0, 1, 2)), (x_high, (31, 30, 29))):
+
+        def edge(out, order):
             for t in range(4):
                 rows = slice(levels * t, levels * t + levels)
                 near, second, third = (state[t, :, j, :] for j in order)
                 out[0, rows], out[1, rows] = split(near)
                 out[2, rows] = second.astype(bf16)
                 out[3, rows] = third.astype(bf16)
+
+        low, high = (0, 1, 2), (31, 30, 29)
+
+        @pl.when(is_odd("gx"))
+        def _():
+            edge(x_a, low)
+            edge(x_b, high)
+
+        @pl.when(jnp.logical_not(is_odd("gx")))
+        def _():
+            edge(x_a, high)
+            edge(x_b, low)
 
 
 def edge_weights():
@@ -450,12 +478,13 @@
     return jax.ShapeDtypeStruct(dims, kind)
 
 
-def shift(value, axis, closed, forward):
+def swap(value, axis, first, closed):
     count = lax.axis_size(axis)
-    ends = count if closed else count - 1
-    pairs = [(i, (i + 1) % count) for i in range(ends)]
-    if not forward:
-        pairs = [(b, a) for a, b in pairs]
+    pairs = []
+    for low in range(0 if first else 1, count, 2):
+        if low + 1 < count or closed:
+            high = (low + 1) % count
+            pairs += [(low, high), (high, low)]
     return lax.ppermute(value, axis, pairs)
 
 
@@ -508,7 +537,7 @@
 
     vmem = pl.BlockSpec(memory_space=pltpu.VMEM)
     edge = shape((4, fields, lats), bf16)
-    state, x_low, x_high = pl.pallas_call(
+    state, x_a, x_b = pl.pallas_call(
         forcing_kernel,
         in_specs=[pl.BlockSpec(memory_space=pltpu.SMEM), vmem, vmem, pl.BlockSpec(memory_space=pl.ANY)],
         out_specs=[vmem] * 3,
@@ -529,8 +558,8 @@
     spread = jnp.asarray(edge_weights(), bf16)
     table = lat_weights()
     for step in range(STEPS):
-        from_left = shift(x_high, "gx", True, True)
-        from_right = shift(x_low, "gx", True, False)
+        got_b = swap(x_b, "gx", False, True)
+        got_a = swap(x_a, "gx", True, True)
         halves = pltpu.VMEM((tracers * LB * 16, 2 * lats), bf16)
         state = state.reshape(tracers, levels, lons, lats)
         partial = pl.pallas_call(
@@ -543,7 +572,7 @@
             cost_estimate=cost(5 * size, 2 * size),
             name="inner",
         )(state, courant_x, spread)
-        zonal, to_left, to_right = pl.pallas_call(
+        zonal, to_a, to_b = pl.pallas_call(
             outer_kernel,
             in_specs=[vmem] * 8,
             out_specs=[vmem] * 3,
@@ -557,12 +586,12 @@
             state,
             courant_x,
             spread,
-            from_left.reshape(4, tracers, levels, lats),
-            from_right.reshape(4, tracers, levels, lats),
+            got_a.reshape(4, tracers, levels, lats),
+            got_b.reshape(4, tracers, levels, lats),
             *partial,
         )
-        y_left = shift(to_right, "gy", False, True)
-        y_right = shift(to_left, "gy", False, False)
+        y_b = swap(to_b, "gy", False, False)
+        y_a = swap(to_a, "gy", True, False)
         inner = pl.pallas_call(
             lat_kernel,
             in_specs=[vmem] * 3,
@@ -574,7 +603,7 @@
             name="lat",
         )(zonal, courant_y, jnp.asarray(table[:256], bf16))
         first = step == 0
-        operands = [inner, courant_y, mixing, inv, q, y_left, y_right, jnp.asarray(table[256:], bf16)]
+        operands = [inner, courant_y, mixing, inv, q, y_a, y_b, jnp.asarray(table[256:], bf16)]
         out_shape = [whole_field, shape((tracers, lons, lats))]
         if first:
             out_shape += [edge, edge]
@@ -595,7 +624,7 @@
             name="column",
         )(*operands)
         if first:
-            state, gradient, x_low, x_high = out
+            state, gradient, x_a, x_b = out
         else:
             state, gradient = out
     return state, gradient

time: 105 us -> 97.2 us (0.926)
  starting transfers between devices: 31.3 us -> 22 us
  waiting for transfers between devices: 22.6 us -> 24.1 us
    ppermute x8, starting transfers between devices: 21 us -> 11.7 us  [swap(): return lax.ppermute(value, axis, pairs)]
    ppermute x8, waiting for transfers between devices: 11 us -> 12.5 us  [swap(): return lax.ppermute(value, axis, pairs)]
  transfers between devices with their start and end apart: 9 -> 9, of which waited for: 5 -> 5; matrix products, arithmetic and copies ran while one was open for 1% -> 1% of each run, Pallas kernels for 14% -> 15%
where the time goes in v4:
time: 97.2 us; the launch traced here: 96.9 us
  Pallas kernels  48.6 us (50%)
  waiting for transfers between devices  24.1 us (25%)
  starting transfers between devices  22 us (23%)
    ppermute x8, waiting for transfers between devices, swap(): return lax.ppermute(value, axis, pairs)  12.5 us
    pallas_call x2, Pallas kernels, local(): pl.pallas_call(kernel, in_specs=[vmem] * len(operands), out_specs=[vmem]...  12 us
    ppermute x8, starting transfers between devices, swap(): return lax.ppermute(value, axis, pairs)  11.7 us
    all_to_all x1, waiting for transfers between devices, local(): lax.all_to_all(packed, ('gx', 'gy'), split_axis=0, concat_axis=0, tiled=T...  11.6 us
    all_to_all x1, starting transfers between devices, local(): lax.all_to_all(packed, ('gx', 'gy'), split_axis=0, concat_axis=0, tiled=T...  10.3 us
    pallas_call x1, Pallas kernels, local(): pl.pallas_call(forcing_kernel, in_specs=[pl.BlockSpec(memory_space=pltpu....  8.71 us
    pallas_call x2, Pallas kernels, local(): pl.pallas_call(outer_kernel, in_specs=[vmem] * 8, out_specs=[vmem] * 3, o...  6.74 us
    pallas_call x2, Pallas kernels, local(): pl.pallas_call(inner_kernel, in_specs=[vmem] * 3, out_specs=[vmem] * 3, o...  6.48 us
  transfers between devices with their start and end apart: 9, of which 5 were waited for; matrix products, arithmetic and copies ran while one was open for 1% of the time, Pallas kernels for 15%

profile of v4, /device:TPU:24, one launch (start us, length us, event | category | flops | bytes accessed | tf_op | source)
XLA Modules:
  0.0 96.9 jit_solution(15933607968396732200)
XLA Ops:
  0.6 0.0 copy-start.6
  0.6 2.6 %pack.1 = bf16[128,24,128]{2,1,0:T(8,128)(2,1)} custom-call(s32[1,128]{1,0:T(1,128)} %counts.1, bf16[72,4096]{1,0:T(8,128)(2,1)} %rows.1, bf16[4,4096]{1,0:T(4,128)(2,1)} %weights.3), custom_call_target="tpu_custom_call" | custom-call | tf_op jit(solution)/shard_map/pack/pallas_call | solution.py:498
  3.3 10.3 %all-to-all-start = ((bf16[128,24,128]{2,1,0:T(8,128)(2,1)}), bf16[128,24,128]{2,1,0:T(8,128)(2,1)S(1)}, u32[]{:S(2)}, u32[]{:S(2)}) async-start(bf16[128,24,128]{2,1,0:T(8,128)(2,1)} %pack.1), calls=%async_computation | async-start | bytes 1572864 | tf_op jit(solution)/shard_map/all_to_all | solution.py:512
  13.5 0.7 fusion.1
  14.3 0.6 broadcast_in_dim.2.bins
  14.9 1.9 %rank.1 = (bf16[4096,128]{1,0:T(8,128)(2,1)S(1)}, s32[32,128]{1,0:T(8,128)S(1)}) custom-call(bf16[4096,128]{1,0:T(8,128)(2,1)S(1)} %broadcast_in_dim.2.bins), custom_call_target="tpu_custom_call" | custom-call | flops 1000000000 | bytes 2000000 | tf_op jit(solution)/shard_map/rank/pallas_call | solution.py:522
  16.8 11.6 %all-to-all-done.got = bf16[128,24,128]{2,1,0:T(8,128)(2,1)S(1)} async-done(((bf16[128,24,128]{2,1,0:T(8,128)(2,1)}), bf16[128,24,128]{2,1,0:T(8,128)(2,1)S(1)}, u32[]{:S(2)}, u32[]{:S(2)}) %all-to-all-start) | async-done | bytes 786464 | tf_op jit(solution)/shard_map/all_to_all | solution.py:512
  28.4 3.5 %order.1 = (bf16[576,4096]{1,0:T(8,128)(2,1)S(1)}, f32[8,4096]{1,0:T(8,128)S(1)}) custom-call(bf16[128,24,128]{2,1,0:T(8,128)(2,1)S(1)} %all-to-all-done.got, s32[1,4096]{1,0:T(1,128)S(1)} %bitcast.13, bf16[4096,128]{1,0:T(8,128)(2,1)S(1)} %get-tuple-element.28.code), custom_call_target="tpu_custom_call" | custom-call | flops 1000000000 | bytes 8000000 | tf_op jit(solution)/shard_map/order/pallas_call | solution.py:529
  32.0 0.0 copy-start.3
  32.0 8.7 %forcing.1 = (f32[288,32,128]{2,1,0:T(8,128)S(1)}, bf16[4,288,128]{2,1,0:T(8,128)(2,1)S(1)}, bf16[4,288,128]{2,1,0:T(8,128)(2,1)S(1)}) custom-call(s32[32,128]{1,0:T(8,128)S(1)} %get-tuple-element.27.starts, bf16[576,4096]{1,0:T(8,128)(2,1)S(1)} %get-tuple-element.29.lhs, f32[8,4096]{1,0:T(8,128)S(1)} %get-tuple-element.30.places, f32[288,32,128]{2,1,0:T(8,128)} %bitcast.14), custom_call_target="tpu_custom_call" | custom-call | flops 10000000000 | bytes 9437184 | tf_op jit(solution)/shard_map/forcing/pallas_call | solution.py:540
  40.7 0.1 collective-permute-start
  40.8 1.5 %collective-permute-start.1 = (bf16[4,288,128]{2,1,0:T(8,128)(2,1)S(1)}, bf16[4,288,128]{2,1,0:T(8,128)(2,1)S(1)}, u32[]{:S(2)}, u32[]{:S(2)}) collective-permute-start(bf16[4,288,128]{2,1,0:T(8,128)(2,1)S(1)} %get-tuple-element.33), channel_id=1, source_target_pairs={{8,16},{16,8},{24,32},{32,24},{40,48},{48,40},{56,64},{64,56},{72,... | collective-permute-start | bytes 884744 | tf_op jit(solution)/shard_map/ppermute | solution.py:488
  42.3 3.2 %inner.2 = (f32[4,72,32,128]{3,2,1,0:T(8,128)S(1)}, bf16[9,32,128]{2,1,0:T(8,128)(2,1)S(1)}, bf16[9,32,128]{2,1,0:T(8,128)(2,1)S(1)}) custom-call(f32[4,72,32,128]{3,2,1,0:T(8,128)S(1)} %bitcast.7, f32[72,32,128]{2,1,0:T(8,128)S(1)} %copy-done.1, bf16[256,256]{1,0:T(8,128)(2,1)S(1)} %copy-done.3), custom_call_target="tpu_custom_call" | custom-call | flops 23592960 | bytes 9437184 | tf_op jit(solution)/shard_map/inner/pallas_call | solution.py:565
  45.5 3.6 %collective-permute-done.1 = bf16[4,288,128]{2,1,0:T(8,128)(2,1)S(1)} collective-permute-done((bf16[4,288,128]{2,1,0:T(8,128)(2,1)S(1)}, bf16[4,288,128]{2,1,0:T(8,128)(2,1)S(1)}, u32[]{:S(2)}, u32[]{:S(2)}) %collective-permute-start.1) | collective-permute-done | bytes 294944 | tf_op jit(solution)/shard_map/ppermute | solution.py:488
  49.1 3.4 %outer.2 = (f32[4,72,32,128]{3,2,1,0:T(8,128)S(1)}, bf16[9,32,128]{2,1,0:T(8,128)(2,1)S(1)}, bf16[9,32,128]{2,1,0:T(8,128)(2,1)S(1)}) custom-call(f32[4,72,32,128]{3,2,1,0:T(8,128)S(1)} %bitcast.8, f32[72,32,128]{2,1,0:T(8,128)S(1)} %copy-done.1, bf16[256,256]{1,0:T(8,128)(2,1)S(1)} %copy-done.3, ...), custom_call_target="tpu_custom_call", output_to_operand_aliasing={{0}: (5, {}), {1}: (6, {}), {2}: (7, {})} | custom-call | flops 23592960 | bytes 9437184 | tf_op jit(solution)/shard_map/outer/pallas_call | solution.py:575
  52.5 0.8 collective-permute-start.2
  53.3 4.5 %collective-permute-start.3 = (bf16[9,32,128]{2,1,0:T(8,128)(2,1)S(1)}, bf16[9,32,128]{2,1,0:T(8,128)(2,1)S(1)}, u32[]{:S(2)}, u32[]{:S(2)}) collective-permute-start(bf16[9,32,128]{2,1,0:T(8,128)(2,1)S(1)} %get-tuple-element.41), channel_id=1, source_target_pairs={{1,2},{2,1},{3,4},{4,3},{5,6},{6,5},{9,10},{10,9},{11,12},{12,11},... | collective-permute-start | bytes 221192 | tf_op jit(solution)/shard_map/ppermute | solution.py:488
  57.9 0.9 factor.1
  58.8 0.0 copy-start.4
  58.8 2.9 %lat.2.refs_0_ = f32[4,72,32,128]{3,2,1,0:T(8,128)S(1)} custom-call(f32[4,72,32,128]{3,2,1,0:T(8,128)S(1)} %get-tuple-element.37.zonal, f32[72,32,128]{2,1,0:T(8,128)S(1)} %copy-done, bf16[256,256]{1,0:T(8,128)(2,1)S(1)} %copy-done.5), custom_call_target="tpu_custom_call" | custom-call | flops 23592960 | bytes 9437184 | tf_op jit(solution)/shard_map/lat/pallas_call | solution.py:595
  61.7 1.5 %collective-permute-done.3.refs_6_ = bf16[9,32,128]{2,1,0:T(8,128)(2,1)S(1)} collective-permute-done((bf16[9,32,128]{2,1,0:T(8,128)(2,1)S(1)}, bf16[9,32,128]{2,1,0:T(8,128)(2,1)S(1)}, u32[]{:S(2)}, u32[]{:S(2)}) %collective-permute-start.3) | collective-permute-done | bytes 73760 | tf_op jit(solution)/shard_map/ppermute | solution.py:488
  63.2 5.7 %column.2 = (f32[4,72,32,128]{3,2,1,0:T(8,128)S(1)}, f32[4,32,128]{2,1,0:T(8,128)S(1)}, bf16[4,288,128]{2,1,0:T(8,128)(2,1)S(1)}, bf16[4,288,128]{2,1,0:T(8,128)(2,1)S(1)}) custom-call(f32[4,72,32,128]{3,2,1,0:T(8,128)S(1)} %lat.2.refs_0_, f32[72,32,128]{2,1,0:T(8,128)S(1)} %copy-done, f32[71,32,128]{2,1,0:T(8,128)S(1)} %copy-done.2, ...), custom_call_target="tpu_custom_call" | custom-call | flops 23592960 | bytes 9437184 | tf_op jit(solution)/shard_map/column/pallas_call | solution.py:616
  68.9 0.1 collective-permute-start.4
  69.0 0.1 collective-permute-start.5
  69.0 3.2 %inner.3 = (f32[4,72,32,128]{3,2,1,0:T(8,128)S(1)}, bf16[9,32,128]{2,1,0:T(8,128)(2,1)S(1)}, bf16[9,32,128]{2,1,0:T(8,128)(2,1)S(1)}) custom-call(f32[4,72,32,128]{3,2,1,0:T(8,128)S(1)} %get-tuple-element.42.state, f32[72,32,128]{2,1,0:T(8,128)S(1)} %copy-done.1, bf16[256,256]{1,0:T(8,128)(2,1)S(1)} %copy-done.3), custom_call_target="tpu_custom_call" | custom-call | flops 23592960 | bytes 9437184 | tf_op jit(solution)/shard_map/inner/pallas_call | solution.py:565
  72.3 5.0 %collective-permute-done.5 = bf16[4,288,128]{2,1,0:T(8,128)(2,1)S(1)} collective-permute-done((bf16[4,288,128]{2,1,0:T(8,128)(2,1)S(1)}, bf16[4,288,128]{2,1,0:T(8,128)(2,1)S(1)}, u32[]{:S(2)}, u32[]{:S(2)}) %collective-permute-start.5) | collective-permute-done | bytes 294944 | tf_op jit(solution)/shard_map/ppermute | solution.py:488
  77.3 3.4 %outer.3 = (f32[4,72,32,128]{3,2,1,0:T(8,128)S(1)}, bf16[9,32,128]{2,1,0:T(8,128)(2,1)S(1)}, bf16[9,32,128]{2,1,0:T(8,128)(2,1)S(1)}) custom-call(f32[4,72,32,128]{3,2,1,0:T(8,128)S(1)} %get-tuple-element.42.state, f32[72,32,128]{2,1,0:T(8,128)S(1)} %copy-done.1, ...), custom_call_target="tpu_custom_call", output_to_operand_aliasing={{0}: (5, {}), {1}: (6, {}), {2}: (7, {})} | custom-call | flops 23592960 | bytes 9437184 | tf_op jit(solution)/shard_map/outer/pallas_call | solution.py:575
  80.7 0.1 collective-permute-start.6
  80.8 4.5 %collective-permute-start.7 = (bf16[9,32,128]{2,1,0:T(8,128)(2,1)S(1)}, bf16[9,32,128]{2,1,0:T(8,128)(2,1)S(1)}, u32[]{:S(2)}, u32[]{:S(2)}) collective-permute-start(bf16[9,32,128]{2,1,0:T(8,128)(2,1)S(1)} %get-tuple-element.50), channel_id=1, source_target_pairs={{1,2},{2,1},{3,4},{4,3},{5,6},{6,5},{9,10},{10,9},{11,12},{12,11},... | collective-permute-start | bytes 221192 | tf_op jit(solution)/shard_map/ppermute | solution.py:488
  85.3 2.9 %lat.3.refs_0_ = f32[4,72,32,128]{3,2,1,0:T(8,128)S(1)} custom-call(f32[4,72,32,128]{3,2,1,0:T(8,128)S(1)} %get-tuple-element.48.zonal, f32[72,32,128]{2,1,0:T(8,128)S(1)} %copy-done, bf16[256,256]{1,0:T(8,128)(2,1)S(1)} %copy-done.5), custom_call_target="tpu_custom_call" | custom-call | flops 23592960 | bytes 9437184 | tf_op jit(solution)/shard_map/lat/pallas_call | solution.py:595
  88.2 2.4 %collective-permute-done.7.refs_6_ = bf16[9,32,128]{2,1,0:T(8,128)(2,1)S(1)} collective-permute-done((bf16[9,32,128]{2,1,0:T(8,128)(2,1)S(1)}, bf16[9,32,128]{2,1,0:T(8,128)(2,1)S(1)}, u32[]{:S(2)}, u32[]{:S(2)}) %collective-permute-start.7) | collective-permute-done | bytes 73760 | tf_op jit(solution)/shard_map/ppermute | solution.py:488
  90.6 6.3 %column.3 = (f32[4,72,32,128]{3,2,1,0:T(8,128)}, f32[4,32,128]{2,1,0:T(8,128)}) custom-call(f32[4,72,32,128]{3,2,1,0:T(8,128)S(1)} %lat.3.refs_0_, f32[72,32,128]{2,1,0:T(8,128)S(1)} %copy-done, f32[71,32,128]{2,1,0:T(8,128)S(1)} %copy-done.2, f32[72,32,128]{2,1,0:T(8,128)S(1)} %get-tuple-element.38.refs_3_, f32[72,32,128]{2,1,0:T(8,128)S(1)} %get-tuple-element.39.refs_4_, ...), custom_call_target="tpu_custom_call" | custom-call | flops 23592960 | bytes 9437184 | tf_op jit(solution)/shard_map/column/pallas_call | solution.py:616
  (15 shorter events, 0.0 us)
Async XLA Ops:
  0.6 27.8 %copy-start.6 = (s32[4096]{0:T(1024)S(1)}, s32[4096]{0:T(1024)}, u32[]{:S(2)}) copy-start(s32[4096]{0:T(1024)} %param.19) | copy-start | bytes 49156
  3.3 25.1 %all-to-all-start = ((bf16[128,24,128]{2,1,0:T(8,128)(2,1)}), bf16[128,24,128]{2,1,0:T(8,128)(2,1)S(1)}, u32[]{:S(2)}, u32[]{:S(2)}) async-start(bf16[128,24,128]{2,1,0:T(8,128)(2,1)} %pack.1), calls=%async_computation | async-start | bytes 1572864 | tf_op jit(solution)/shard_map/all_to_all | solution.py:512
  31.9 10.3 %copy-start.1 = (f32[72,32,128]{2,1,0:T(8,128)S(1)}, f32[72,32,128]{2,1,0:T(8,128)}, u32[]{:S(2)}) copy-start(f32[72,32,128]{2,1,0:T(8,128)} %courant.10) | copy-start | bytes 3538948
  32.0 10.3 %copy-start.3 = (bf16[256,256]{1,0:T(8,128)(2,1)S(1)}, bf16[256,256]{1,0:T(8,128)(2,1)}, u32[]{:S(2)}) copy-start(bf16[256,256]{1,0:T(8,128)(2,1)} %constant.22.clone.spread) | copy-start | bytes 393220
  40.7 4.8 %collective-permute-start = (bf16[4,288,128]{2,1,0:T(8,128)(2,1)S(1)}, bf16[4,288,128]{2,1,0:T(8,128)(2,1)S(1)}, u32[]{:S(2)}, u32[]{:S(2)}) collective-permute-start(bf16[4,288,128]{2,1,0:T(8,128)(2,1)S(1)} %get-tuple-element.32), channel_id=1, source_target_pairs={{0,8},{8,0},{16,24},{24,16},{32,40},{40,32},{48,56},{56,48},{64,72... | collective-permute-start | bytes 884744 | tf_op jit(solution)/shard_map/ppermute | solution.py:488
  40.8 8.3 %collective-permute-start.1 = (bf16[4,288,128]{2,1,0:T(8,128)(2,1)S(1)}, bf16[4,288,128]{2,1,0:T(8,128)(2,1)S(1)}, u32[]{:S(2)}, u32[]{:S(2)}) collective-permute-start(bf16[4,288,128]{2,1,0:T(8,128)(2,1)S(1)} %get-tuple-element.33), channel_id=1, source_target_pairs={{8,16},{16,8},{24,32},{32,24},{40,48},{48,40},{56,64},{64,56},{72,... | collective-permute-start | bytes 884744 | tf_op jit(solution)/shard_map/ppermute | solution.py:488
  49.1 8.7 %copy-start.2 = (f32[71,32,128]{2,1,0:T(8,128)S(1)}, f32[71,32,128]{2,1,0:T(8,128)}, u32[]{:S(2)}) copy-start(f32[71,32,128]{2,1,0:T(8,128)} %refs_2_.3) | copy-start | bytes 3489796
  49.1 9.7 %copy-start = (f32[72,32,128]{2,1,0:T(8,128)S(1)}, f32[72,32,128]{2,1,0:T(8,128)}, u32[]{:S(2)}) copy-start(f32[72,32,128]{2,1,0:T(8,128)} %refs_1_.3) | copy-start | bytes 3538948
  49.1 9.7 %copy-start.5 = (bf16[256,256]{1,0:T(8,128)(2,1)S(1)}, bf16[256,256]{1,0:T(8,128)(2,1)}, u32[]{:S(2)}) copy-start(bf16[256,256]{1,0:T(8,128)(2,1)} %constant.23.clone.weights) | copy-start | bytes 393220
  52.5 9.2 %collective-permute-start.2 = (bf16[9,32,128]{2,1,0:T(8,128)(2,1)S(1)}, bf16[9,32,128]{2,1,0:T(8,128)(2,1)S(1)}, u32[]{:S(2)}, u32[]{:S(2)}) collective-permute-start(bf16[9,32,128]{2,1,0:T(8,128)(2,1)S(1)} %get-tuple-element.40), channel_id=1, source_target_pairs={{0,1},{1,0},{2,3},{3,2},{4,5},{5,4},{6,7},{7,6},{8,9},{9,8},{10,11... | collective-permute-start | bytes 221192 | tf_op jit(solution)/shard_map/ppermute | solution.py:488
  53.3 9.8 %collective-permute-start.3 = (bf16[9,32,128]{2,1,0:T(8,128)(2,1)S(1)}, bf16[9,32,128]{2,1,0:T(8,128)(2,1)S(1)}, u32[]{:S(2)}, u32[]{:S(2)}) collective-permute-start(bf16[9,32,128]{2,1,0:T(8,128)(2,1)S(1)} %get-tuple-element.41), channel_id=1, source_target_pairs={{1,2},{2,1},{3,4},{4,3},{5,6},{6,5},{9,10},{10,9},{11,12},{12,11},... | collective-permute-start | bytes 221192 | tf_op jit(solution)/shard_map/ppermute | solution.py:488
  58.8 4.4 %copy-start.4 = (bf16[256,256]{1,0:T(8,128)(2,1)S(1)}, bf16[256,256]{1,0:T(8,128)(2,1)}, u32[]{:S(2)}) copy-start(bf16[256,256]{1,0:T(8,128)(2,1)} %constant.24.clone.refs_7_) | copy-start | bytes 393220
  68.9 3.4 %collective-permute-start.4 = (bf16[4,288,128]{2,1,0:T(8,128)(2,1)S(1)}, bf16[4,288,128]{2,1,0:T(8,128)(2,1)S(1)}, u32[]{:S(2)}, u32[]{:S(2)}) collective-permute-start(bf16[4,288,128]{2,1,0:T(8,128)(2,1)S(1)} %get-tuple-element.43), channel_id=1, source_target_pairs={{0,8},{8,0},{16,24},{24,16},{32,40},{40,32},{48,56},{56,48},{64,72... | collective-permute-start | bytes 884744 | tf_op jit(solution)/shard_map/ppermute | solution.py:488
  69.0 8.3 %collective-permute-start.5 = (bf16[4,288,128]{2,1,0:T(8,128)(2,1)S(1)}, bf16[4,288,128]{2,1,0:T(8,128)(2,1)S(1)}, u32[]{:S(2)}, u32[]{:S(2)}) collective-permute-start(bf16[4,288,128]{2,1,0:T(8,128)(2,1)S(1)} %get-tuple-element.44), channel_id=1, source_target_pairs={{8,16},{16,8},{24,32},{32,24},{40,48},{48,40},{56,64},{64,56},{72,... | collective-permute-start | bytes 884744 | tf_op jit(solution)/shard_map/ppermute | solution.py:488
  80.7 7.5 %collective-permute-start.6 = (bf16[9,32,128]{2,1,0:T(8,128)(2,1)S(1)}, bf16[9,32,128]{2,1,0:T(8,128)(2,1)S(1)}, u32[]{:S(2)}, u32[]{:S(2)}) collective-permute-start(bf16[9,32,128]{2,1,0:T(8,128)(2,1)S(1)} %get-tuple-element.49), channel_id=1, source_target_pairs={{0,1},{1,0},{2,3},{3,2},{4,5},{5,4},{6,7},{7,6},{8,9},{9,8},{10,11... | collective-permute-start | bytes 221192 | tf_op jit(solution)/shard_map/ppermute | solution.py:488
  80.8 9.9 %collective-permute-start.7 = (bf16[9,32,128]{2,1,0:T(8,128)(2,1)S(1)}, bf16[9,32,128]{2,1,0:T(8,128)(2,1)S(1)}, u32[]{:S(2)}, u32[]{:S(2)}) collective-permute-start(bf16[9,32,128]{2,1,0:T(8,128)(2,1)S(1)} %get-tuple-element.50), channel_id=1, source_target_pairs={{1,2},{2,1},{3,4},{4,3},{5,6},{6,5},{9,10},{10,9},{11,12},{12,11},... | collective-permute-start | bytes 221192 | tf_op jit(solution)/shard_map/ppermute | solution.py:488

commit v5 on v4

--- a/solution.py
+++ b/solution.py
@@ -260,10 +260,9 @@
     lax.fori_loop(0, steps, eight, 0)
 
 
-def zonal_rows(outer, state, courant, spread, halos, zonal, to_a, to_b, halves, pad):
+def zonal_rows(outer, state, courant, courant_y, weights, halos, result, to_a, to_b, halves, kept, pad):
     lane = lax.broadcasted_iota(jnp.int32, (16, 128), 1)
     group = lane >> 2
-    note_rows = slice(16, 32) if outer else slice(0, 16)
     odd_x = is_odd("gx")
     odd_y = is_odd("gy")
 
@@ -280,64 +279,91 @@
                         value = jnp.where(odd_x, parts[side][k], parts[1 - side][k])
                         pad[pl.ds(t * LB * 33 + (24 + k if side else 7 - k), LB, stride=33), :] = value
         notes = [jnp.zeros((16, 128), f32)] * 2
-        for t in range(4):
-            for l in range(LB):
+        for first in range(0, LB, 4):
+            for l in range(first, first + 4):
                 level = b * LB + l
-                i = t * LB + l
                 if outer:
                     c = jnp.concatenate([courant[level, 0:8, :], courant[level, 24:32, :]], axis=0)
-                    low = state[t, level, 0:8, :]
-                    high = state[t, level, 24:32, :]
-                    base = 33 * i
-                    pad[base + 8 : base + 16, :] = low
-                    pad[base + 16 : base + 24, :] = high
-                    v = {0: jnp.concatenate([low, high], axis=0)}
-                    for k in (1, 2, 3):
-                        v[-k] = jnp.concatenate(
-                            [pad[base + 8 - k : base + 16 - k, :], state[t, level, 24 - k : 32 - k, :]], axis=0
-                        )
-                        v[k] = jnp.concatenate(
-                            [state[t, level, k : 8 + k, :], pad[base + 16 + k : base + 24 + k, :]], axis=0
-                        )
                 else:
                     c = courant[level, 8:24, :]
-                    v = {k: state[t, level, 8 + k : 24 + k, :] for k in range(-3, 4)}
-                out = stencil(v, c, 0.5 * c * c)
-                if outer:
-                    zonal[t, level, 0:8, :] = out[:8]
-                    zonal[t, level, 24:32, :] = out[8:]
-                else:
-                    zonal[t, level, 8:24, :] = out
-                at = slice(16 * i, 16 * i + 16)
-                halves[at, 0:128], halves[at, 128:256] = split(out)
-            at = slice(16 * LB * t, 16 * LB * (t + 1))
-            edges = jnp.dot(halves[at, :], spread[...], preferred_element_type=f32)
-            for l in range(LB):
-                mine = group == t * LB + l
-                rows = slice(16 * l, 16 * l + 16)
-                notes = [jnp.where(mine, edges[rows, 128 * n : 128 * n + 128], notes[n]) for n in range(2)]
-        to_a[b, note_rows] = jnp.where(odd_y, notes[0], notes[1]).astype(bf16)
-        to_b[b, note_rows] = jnp.where(odd_y, notes[1], notes[0]).astype(bf16)
+                factors = stencil_factors(c)
+                for t in range(4):
+                    if outer:
+                        low = state[t, level, 0:8, :]
+                        high = state[t, level, 24:32, :]
+                        base = 33 * (t * LB + l)
+                        pad[base + 8 : base + 16, :] = low
+                        pad[base + 16 : base + 24, :] = high
+                        v = {0: jnp.concatenate([low, high], axis=0)}
+                        for k in (1, 2, 3):
+                            v[-k] = jnp.concatenate(
+                                [pad[base + 8 - k : base + 16 - k, :], state[t, level, 24 - k : 32 - k, :]], axis=0
+                            )
+                            v[k] = jnp.concatenate(
+                                [state[t, level, k : 8 + k, :], pad[base + 16 + k : base + 24 + k, :]], axis=0
+                            )
+                    else:
+                        v = {k: state[t, level, 8 + k : 24 + k, :] for k in range(-3, 4)}
+                    out = v[0] * factors[0]
+                    for k in (-1, 1, -2, 2, -3, 3):
+                        out = out + v[k] * factors[k]
+                    at = slice(16 * (4 * l + t), 16 * (4 * l + t) + 16)
+                    if outer:
+                        result[t, level] = out
+                    else:
+                        kept[at, :] = out
+                    halves[at, 0:128], halves[at, 128:256] = split(out)
+            at = slice(64 * first, 64 * first + 256)
+            edges = jnp.dot(halves[at, :], weights[...], preferred_element_type=f32)
+            for l in range(4):
+                if not outer:
+                    level = b * LB + first + l
+                    rows = slice(64 * l, 64 * l + 64)
+                    kept_rows = slice(64 * (first + l), 64 * (first + l) + 64)
+                    part = edges[rows, 256:512].reshape(4, 16, 256)
+                    c = courant_y[level, 8:24, :]
+                    result[:, level, 8:24, :] = (
+                        kept[kept_rows, :].reshape(4, 16, 128)
+                        + (c * (1.0 / 60.0)) * part[:, :, :128]
+                        + (c * c * (1.0 / 360.0)) * part[:, :, 128:]
+                    )
+                for t in range(4):
+                    mine = group == t * LB + first + l
+                    rows = slice(16 * (4 * l + t), 16 * (4 * l + t) + 16)
+                    notes = [jnp.where(mine, edges[rows, 128 * n : 128 * n + 128], notes[n]) for n in range(2)]
+        for out, note in (
+            (to_a, jnp.where(odd_y, notes[0], notes[1]).astype(bf16)),
+            (to_b, jnp.where(odd_y, notes[1], notes[0]).astype(bf16)),
+        ):
+            if outer:
+                out[b, 0:8] = note[:8]
+                out[b, 24:32] = note[8:]
+            else:
+                out[b, 8:24] = note
         return 0
 
     lax.fori_loop(0, courant.shape[0] // LB, block, 0)
 
 
-def inner_kernel(state, courant, spread, zonal, to_a, to_b, halves):
-    zonal_rows(False, state, courant, spread, None, zonal, to_a, to_b, halves, None)
-
-
-def outer_kernel(state, courant, spread, from_a, from_b, _z, _a, _b, zonal, to_a, to_b, halves, pad):
-    zonal_rows(True, state, courant, spread, (from_a, from_b), zonal, to_a, to_b, halves, pad)
-
-
-def stencil(v, c, c2):
-    slope = D1 * (v[1] - v[-1]) + D2 * (v[2] - v[-2]) + D3 * (v[3] - v[-3])
-    curve = E0 * v[0] + E1 * (v[1] + v[-1]) + E2 * (v[2] + v[-2]) + E3 * (v[3] + v[-3])
-    return v[0] + c * slope + c2 * curve
-
-
-def lat_kernel(zonal, courant, weights, result, halves):
+def inner_kernel(state, courant, courant_y, weights, result, to_a, to_b, halves, kept):
+    zonal_rows(False, state, courant, courant_y, weights, None, result, to_a, to_b, halves, kept, None)
+
+
+def outer_kernel(state, courant, weights, from_a, from_b, _a, _b, zonal, to_a, to_b, halves, pad):
+    zonal_rows(True, state, courant, None, weights, (from_a, from_b), zonal, to_a, to_b, halves, None, pad)
+
+
+def stencil_factors(c):
+    c2 = 0.5 * c * c
+    factors = {0: 1.0 + E0 * c2}
+    for k, d, e in ((1, D1, E1), (2, D2, E2), (3, D3, E3)):
+        slope, curve = d * c, e * c2
+        factors[k] = curve + slope
+        factors[-k] = curve - slope
+    return factors
+
+
+def lat_kernel(zonal, courant, weights, _result, result, halves):
     tracers, levels, lons, lats = zonal.shape
     rows = tracers * lons
 
@@ -346,14 +372,20 @@
             level = b * LB + l
             at = slice(l * rows, (l + 1) * rows)
             halves[at, 0:128], halves[at, 128:256] = split(zonal[:, level].reshape(rows, lats))
-        for l in range(LB):
-            level = b * LB + l
-            at = slice(l * rows, (l + 1) * rows)
-            both = jnp.dot(halves[at, :], weights[...], preferred_element_type=f32).reshape(tracers, lons, 256)
-            c = courant[level]
-            result[:, level] = (
-                zonal[:, level] + (c * (1.0 / 60.0)) * both[:, :, :128] + (c * c * (1.0 / 360.0)) * both[:, :, 128:]
-            )
+        for l in range(0, LB, 4):
+            at = slice(l * rows, (l + 4) * rows)
+            several = jnp.dot(halves[at, :], weights[...], preferred_element_type=f32)
+            for n in range(4):
+                level = b * LB + l + n
+                both = several[n * rows : (n + 1) * rows].reshape(tracers, lons, 256)
+                c = jnp.concatenate([courant[level, 0:8, :], courant[level, 24:32, :]], axis=0)
+                out = (
+                    zonal[:, level]
+                    + (c * (1.0 / 60.0)) * both[:, :, :128]
+                    + (c * c * (1.0 / 360.0)) * both[:, :, 128:]
+                )
+                result[:, level, 0:8, :] = out[:, :8]
+                result[:, level, 24:32, :] = out[:, 8:]
         return 0
 
     lax.fori_loop(0, levels // LB, block, 0)
@@ -366,20 +398,19 @@
     else:
         before, state, gradient = rest[:-1]
     levels = inv.shape[0]
-    rows = 32
+    lons = 32
+    rows = 4 * lons
     lane = lax.broadcasted_iota(jnp.int32, (rows, 128), 1)
     row = lax.broadcasted_iota(jnp.int32, (rows, 128), 0)
-    owner = ((lane >> 2) - (row >> 3) * LB).astype(f32).astype(bf16)
+    owner = ((lane >> 2) - (row >> 5) * LB).astype(f32).astype(bf16)
     zero = jnp.zeros((), bf16)
     odd_y = is_odd("gy")
 
     def tile(r, _):
-        here = pl.ds(pl.multiple_of(8 * r, 8), 8)
-        slot = jnp.where(r == 0, 2, jnp.where(r == 3, 3, r - 1))
-        there = pl.ds(pl.multiple_of(8 * slot, 8), 8)
+        here = pl.ds(pl.multiple_of(lons * r, lons), lons)
         carry = None
         for b in range(levels // LB):
-            a, z = from_a[b, there, :].astype(f32), from_b[b, there, :].astype(f32)
+            a, z = from_a[b, here, :].astype(f32), from_b[b, here, :].astype(f32)
             notes = [
                 jnp.concatenate([note] * 4, axis=0).astype(bf16)
                 for note in (jnp.where(odd_y, a, z), jnp.where(odd_y, z, a))
@@ -395,7 +426,7 @@
             for l in range(LB):
                 level = b * LB + l
                 c = courant[level, here, :]
-                part = both[l * rows : l * rows + rows].reshape(4, 8, 256)
+                part = both[l * rows : l * rows + rows].reshape(4, lons, 256)
                 y = inner[:, level, here, :]
                 y = y + (c * (1.0 / 60.0)) * part[:, :, :128] + (c * c * (1.0 / 360.0)) * part[:, :, 128:]
                 if level > 0:
@@ -413,7 +444,7 @@
         gradient[:, here, :] = carry if first else before[:, here, :] + carry
         return 0
 
-    lax.fori_loop(0, inner.shape[2] // 8, tile, 0)
+    lax.fori_loop(0, inner.shape[2] // lons, tile, 0)
     if first:
 
         def edge(out, order):
@@ -555,29 +586,29 @@
     whole_field = shape((tracers, levels, lons, lats))
     blocks = levels // LB
     note = shape((blocks, lons, 128), bf16)
-    spread = jnp.asarray(edge_weights(), bf16)
+    spread = edge_weights()
     table = lat_weights()
     for step in range(STEPS):
         got_b = swap(x_b, "gx", False, True)
         got_a = swap(x_a, "gx", True, True)
         halves = pltpu.VMEM((tracers * LB * 16, 2 * lats), bf16)
         state = state.reshape(tracers, levels, lons, lats)
-        partial = pl.pallas_call(
+        result, to_a, to_b = pl.pallas_call(
             inner_kernel,
-            in_specs=[vmem] * 3,
+            in_specs=[vmem] * 4,
             out_specs=[vmem] * 3,
             out_shape=[whole_field, note, note],
-            scratch_shapes=[halves],
+            scratch_shapes=[halves, pltpu.VMEM((tracers * LB * 16, lats), f32)],
             compiler_params=params(24),
             cost_estimate=cost(5 * size, 2 * size),
             name="inner",
-        )(state, courant_x, spread)
+        )(state, courant_x, courant_y, jnp.asarray(np.concatenate([spread, table[:256]], axis=1), bf16))
         zonal, to_a, to_b = pl.pallas_call(
             outer_kernel,
-            in_specs=[vmem] * 8,
+            in_specs=[vmem] * 7,
             out_specs=[vmem] * 3,
-            out_shape=[whole_field, note, note],
-            input_output_aliases={5: 0, 6: 1, 7: 2},
+            out_shape=[shape((tracers, levels, 16, lats)), note, note],
+            input_output_aliases={5: 1, 6: 2},
             scratch_shapes=[halves, pltpu.VMEM((tracers * LB * 33, lats), f32)],
             compiler_params=params(24),
             cost_estimate=cost(5 * size, 2 * size),
@@ -585,23 +616,25 @@
         )(
             state,
             courant_x,
-            spread,
+            jnp.asarray(spread, bf16),
             got_a.reshape(4, tracers, levels, lats),
             got_b.reshape(4, tracers, levels, lats),
-            *partial,
+            to_a,
+            to_b,
         )
         y_b = swap(to_b, "gy", False, False)
         y_a = swap(to_a, "gy", True, False)
         inner = pl.pallas_call(
             lat_kernel,
-            in_specs=[vmem] * 3,
+            in_specs=[vmem] * 4,
             out_specs=vmem,
             out_shape=whole_field,
-            scratch_shapes=[pltpu.VMEM((LB * tracers * lons, 2 * lats), bf16)],
+            input_output_aliases={3: 0},
+            scratch_shapes=[halves],
             compiler_params=params(24),
             cost_estimate=cost(5 * size, 2 * size),
             name="lat",
-        )(zonal, courant_y, jnp.asarray(table[:256], bf16))
+        )(zonal, courant_y, jnp.asarray(table[:256], bf16), result)
         first = step == 0
         operands = [inner, courant_y, mixing, inv, q, y_a, y_b, jnp.asarray(table[256:], bf16)]
         out_shape = [whole_field, shape((tracers, lons, lats))]
@@ -618,7 +651,7 @@
             in_specs=[vmem] * len(operands),
             out_specs=[vmem] * len(out_shape),
             out_shape=out_shape,
-            scratch_shapes=[pltpu.VMEM((levels * tracers * 8, 2 * lats), bf16)],
+            scratch_shapes=[pltpu.VMEM((levels * tracers * 32, 2 * lats), bf16)],
             compiler_params=params(24),
             cost_estimate=cost(5 * size, 2 * size),
             name="column",

time: 97.2 us -> 94.4 us (0.971)
  Pallas kernels: 48.6 us -> 45 us
    pallas_call x2, Pallas kernels: 12 us -> 9.97 us  [local(): pl.pallas_call(kernel, in_specs=[vmem] * len(operands), out_specs=[vmem]...]
    pallas_call x6, Pallas kernels: 18.9 us -> 17.3 us  [the longest x2 7.18 us: local(): pl.pallas_call(inner_kernel, in_specs=[vmem] * 4, out_specs=[vmem] * 3, o...]
where the time goes in v5:
time: 94.4 us; the launch traced here: 94.1 us
  Pallas kernels  45 us (48%)
  waiting for transfers between devices  24.8 us (26%)
  starting transfers between devices  22.1 us (23%)
    ppermute x8, waiting for transfers between devices, swap(): return lax.ppermute(value, axis, pairs)  13.2 us
    ppermute x8, starting transfers between devices, swap(): return lax.ppermute(value, axis, pairs)  11.9 us
    all_to_all x1, waiting for transfers between devices, local(): lax.all_to_all(packed, ('gx', 'gy'), split_axis=0, concat_axis=0, tiled=T...  11.6 us
    all_to_all x1, starting transfers between devices, local(): lax.all_to_all(packed, ('gx', 'gy'), split_axis=0, concat_axis=0, tiled=T...  10.3 us
    pallas_call x2, Pallas kernels, local(): pl.pallas_call(kernel, in_specs=[vmem] * len(operands), out_specs=[vmem]...  9.97 us
    pallas_call x1, Pallas kernels, local(): pl.pallas_call(forcing_kernel, in_specs=[pl.BlockSpec(memory_space=pltpu....  8.71 us
    pallas_call x2, Pallas kernels, local(): pl.pallas_call(inner_kernel, in_specs=[vmem] * 4, out_specs=[vmem] * 3, o...  7.18 us
    pallas_call x2, Pallas kernels, local(): pl.pallas_call(outer_kernel, in_specs=[vmem] * 7, out_specs=[vmem] * 3, o...  5.92 us
  transfers between devices with their start and end apart: 9, of which 5 were waited for; matrix products, arithmetic and copies ran while one was open for 1% of the time, Pallas kernels for 15%

profile of v5, /device:TPU:24, one launch (start us, length us, event | category | flops | bytes accessed | tf_op | source)
XLA Modules:
  0.0 94.1 jit_solution(10716313570068820579)
XLA Ops:
  0.6 2.6 %pack.1 = bf16[128,24,128]{2,1,0:T(8,128)(2,1)} custom-call(s32[1,128]{1,0:T(1,128)} %counts.1, bf16[72,4096]{1,0:T(8,128)(2,1)} %rows.1, bf16[4,4096]{1,0:T(4,128)(2,1)} %weights.7), custom_call_target="tpu_custom_call" | custom-call | tf_op jit(solution)/shard_map/pack/pallas_call | solution.py:529
  3.3 10.3 %all-to-all-start = ((bf16[128,24,128]{2,1,0:T(8,128)(2,1)}), bf16[128,24,128]{2,1,0:T(8,128)(2,1)S(1)}, u32[]{:S(2)}, u32[]{:S(2)}) async-start(bf16[128,24,128]{2,1,0:T(8,128)(2,1)} %pack.1), calls=%async_computation | async-start | bytes 1572864 | tf_op jit(solution)/shard_map/all_to_all | solution.py:543
  13.5 0.7 fusion.1
  14.3 0.6 broadcast_in_dim.2.bins
  14.9 1.9 %rank.1 = (bf16[4096,128]{1,0:T(8,128)(2,1)S(1)}, s32[32,128]{1,0:T(8,128)S(1)}) custom-call(bf16[4096,128]{1,0:T(8,128)(2,1)S(1)} %broadcast_in_dim.2.bins), custom_call_target="tpu_custom_call" | custom-call | flops 1000000000 | bytes 2000000 | tf_op jit(solution)/shard_map/rank/pallas_call | solution.py:553
  16.8 11.6 %all-to-all-done.got = bf16[128,24,128]{2,1,0:T(8,128)(2,1)S(1)} async-done(((bf16[128,24,128]{2,1,0:T(8,128)(2,1)}), bf16[128,24,128]{2,1,0:T(8,128)(2,1)S(1)}, u32[]{:S(2)}, u32[]{:S(2)}) %all-to-all-start) | async-done | bytes 786464 | tf_op jit(solution)/shard_map/all_to_all | solution.py:543
  28.4 3.5 %order.1 = (bf16[576,4096]{1,0:T(8,128)(2,1)S(1)}, f32[8,4096]{1,0:T(8,128)S(1)}) custom-call(bf16[128,24,128]{2,1,0:T(8,128)(2,1)S(1)} %all-to-all-done.got, s32[1,4096]{1,0:T(1,128)S(1)} %bitcast.13, bf16[4096,128]{1,0:T(8,128)(2,1)S(1)} %get-tuple-element.28.code), custom_call_target="tpu_custom_call" | custom-call | flops 1000000000 | bytes 8000000 | tf_op jit(solution)/shard_map/order/pallas_call | solution.py:560
  32.0 0.0 copy-start.3
  32.0 8.7 %forcing.1 = (f32[288,32,128]{2,1,0:T(8,128)S(1)}, bf16[4,288,128]{2,1,0:T(8,128)(2,1)S(1)}, bf16[4,288,128]{2,1,0:T(8,128)(2,1)S(1)}) custom-call(s32[32,128]{1,0:T(8,128)S(1)} %get-tuple-element.27.starts, bf16[576,4096]{1,0:T(8,128)(2,1)S(1)} %get-tuple-element.29.lhs, f32[8,4096]{1,0:T(8,128)S(1)} %get-tuple-element.30.places, f32[288,32,128]{2,1,0:T(8,128)} %bitcast.14), custom_call_target="tpu_custom_call" | custom-call | flops 10000000000 | bytes 9437184 | tf_op jit(solution)/shard_map/forcing/pallas_call | solution.py:571
  40.7 0.0 copy-start.6
  40.7 0.1 collective-permute-start
  40.8 1.5 %collective-permute-start.1 = (bf16[4,288,128]{2,1,0:T(8,128)(2,1)S(1)}, bf16[4,288,128]{2,1,0:T(8,128)(2,1)S(1)}, u32[]{:S(2)}, u32[]{:S(2)}) collective-permute-start(bf16[4,288,128]{2,1,0:T(8,128)(2,1)S(1)} %get-tuple-element.33), channel_id=1, source_target_pairs={{8,16},{16,8},{24,32},{32,24},{40,48},{48,40},{56,64},{64,56},{72,... | collective-permute-start | bytes 884744 | tf_op jit(solution)/shard_map/ppermute | solution.py:519
  42.3 3.6 %inner.2 = (f32[4,72,32,128]{3,2,1,0:T(8,128)S(1)}, bf16[9,32,128]{2,1,0:T(8,128)(2,1)S(1)}, bf16[9,32,128]{2,1,0:T(8,128)(2,1)S(1)}) custom-call(f32[4,72,32,128]{3,2,1,0:T(8,128)S(1)} %bitcast.7, f32[72,32,128]{2,1,0:T(8,128)S(1)} %copy-done.1, f32[72,32,128]{2,1,0:T(8,128)S(1)} %copy-done, bf16[256,512]{1,0:T(8,128)(2,1)S(1)} %copy-done.3), custom_call_target="tpu_custom_call" | custom-call | flops 23592960 | bytes 9437184 | tf_op jit(solution)/shard_map/inner/pallas_call | solution.py:596
  45.9 3.2 %collective-permute-done.1 = bf16[4,288,128]{2,1,0:T(8,128)(2,1)S(1)} collective-permute-done((bf16[4,288,128]{2,1,0:T(8,128)(2,1)S(1)}, bf16[4,288,128]{2,1,0:T(8,128)(2,1)S(1)}, u32[]{:S(2)}, u32[]{:S(2)}) %collective-permute-start.1) | collective-permute-done | bytes 294944 | tf_op jit(solution)/shard_map/ppermute | solution.py:519
  49.1 3.0 %outer.2 = (f32[4,72,16,128]{3,2,1,0:T(8,128)S(1)}, bf16[9,32,128]{2,1,0:T(8,128)(2,1)S(1)}, bf16[9,32,128]{2,1,0:T(8,128)(2,1)S(1)}) custom-call(f32[4,72,32,128]{3,2,1,0:T(8,128)S(1)} %bitcast.8, f32[72,32,128]{2,1,0:T(8,128)S(1)} %copy-done.1, bf16[256,256]{1,0:T(8,128)(2,1)S(1)} %copy-done.6, ...), custom_call_target="tpu_custom_call", output_to_operand_aliasing={{1}: (5, {}), {2}: (6, {})} | custom-call | flops 23592960 | bytes 9437184 | tf_op jit(solution)/shard_map/outer/pallas_call | solution.py:606
  52.1 0.8 collective-permute-start.2
  52.9 4.7 %collective-permute-start.3 = (bf16[9,32,128]{2,1,0:T(8,128)(2,1)S(1)}, bf16[9,32,128]{2,1,0:T(8,128)(2,1)S(1)}, u32[]{:S(2)}, u32[]{:S(2)}) collective-permute-start(bf16[9,32,128]{2,1,0:T(8,128)(2,1)S(1)} %get-tuple-element.41), channel_id=1, source_target_pairs={{1,2},{2,1},{3,4},{4,3},{5,6},{6,5},{9,10},{10,9},{11,12},{12,11},... | collective-permute-start | bytes 221192 | tf_op jit(solution)/shard_map/ppermute | solution.py:519
  57.7 0.9 factor.1
  58.6 0.0 copy-start.4
  58.6 2.1 %lat.2.refs_0_ = f32[4,72,32,128]{3,2,1,0:T(8,128)S(1)} custom-call(f32[4,72,16,128]{3,2,1,0:T(8,128)S(1)} %get-tuple-element.36.zonal, f32[72,32,128]{2,1,0:T(8,128)S(1)} %copy-done, bf16[256,256]{1,0:T(8,128)(2,1)S(1)} %copy-done.5, f32[4,72,32,128]{3,2,1,0:T(8,128)S(1)} %get-tuple-element.37._result), custom_call_target="tpu_custom_call", output_to_operand_aliasing={{}: (3, {})} | custom-call | flops 23592960 | bytes 9437184 | tf_op jit(solution)/shard_map/lat/pallas_call | solution.py:627
  60.7 2.1 %collective-permute-done.3.refs_6_ = bf16[9,32,128]{2,1,0:T(8,128)(2,1)S(1)} collective-permute-done((bf16[9,32,128]{2,1,0:T(8,128)(2,1)S(1)}, bf16[9,32,128]{2,1,0:T(8,128)(2,1)S(1)}, u32[]{:S(2)}, u32[]{:S(2)}) %collective-permute-start.3) | collective-permute-done | bytes 73760 | tf_op jit(solution)/shard_map/ppermute | solution.py:519
  62.8 4.6 %column.2 = (f32[4,72,32,128]{3,2,1,0:T(8,128)S(1)}, f32[4,32,128]{2,1,0:T(8,128)S(1)}, bf16[4,288,128]{2,1,0:T(8,128)(2,1)S(1)}, bf16[4,288,128]{2,1,0:T(8,128)(2,1)S(1)}) custom-call(f32[4,72,32,128]{3,2,1,0:T(8,128)S(1)} %lat.2.refs_0_, f32[72,32,128]{2,1,0:T(8,128)S(1)} %copy-done, f32[71,32,128]{2,1,0:T(8,128)S(1)} %copy-done.2, ...), custom_call_target="tpu_custom_call" | custom-call | flops 23592960 | bytes 9437184 | tf_op jit(solution)/shard_map/column/pallas_call | solution.py:649
  67.4 0.1 collective-permute-start.4
  67.5 0.1 collective-permute-start.5
  67.5 3.6 %inner.3 = (f32[4,72,32,128]{3,2,1,0:T(8,128)S(1)}, bf16[9,32,128]{2,1,0:T(8,128)(2,1)S(1)}, bf16[9,32,128]{2,1,0:T(8,128)(2,1)S(1)}) custom-call(f32[4,72,32,128]{3,2,1,0:T(8,128)S(1)} %get-tuple-element.42.state, f32[72,32,128]{2,1,0:T(8,128)S(1)} %copy-done.1, f32[72,32,128]{2,1,0:T(8,128)S(1)} %copy-done, bf16[256,512]{1,0:T(8,128)(2,1)S(1)} %copy-done.3), custom_call_target="tpu_custom_call" | custom-call | flops 23592960 | bytes 9437184 | tf_op jit(solution)/shard_map/inner/pallas_call | solution.py:596
  71.1 4.6 %collective-permute-done.5 = bf16[4,288,128]{2,1,0:T(8,128)(2,1)S(1)} collective-permute-done((bf16[4,288,128]{2,1,0:T(8,128)(2,1)S(1)}, bf16[4,288,128]{2,1,0:T(8,128)(2,1)S(1)}, u32[]{:S(2)}, u32[]{:S(2)}) %collective-permute-start.5) | collective-permute-done | bytes 294944 | tf_op jit(solution)/shard_map/ppermute | solution.py:519
  75.8 3.0 %outer.3 = (f32[4,72,16,128]{3,2,1,0:T(8,128)S(1)}, bf16[9,32,128]{2,1,0:T(8,128)(2,1)S(1)}, bf16[9,32,128]{2,1,0:T(8,128)(2,1)S(1)}) custom-call(f32[4,72,32,128]{3,2,1,0:T(8,128)S(1)} %get-tuple-element.42.state, f32[72,32,128]{2,1,0:T(8,128)S(1)} %copy-done.1, bf16[256,256]{1,0:T(8,128)(2,1)S(1)} %copy-done.6, ...), custom_call_target="tpu_custom_call", output_to_operand_aliasing={{1}: (5, {}), {2}: (6, {})} | custom-call | flops 23592960 | bytes 9437184 | tf_op jit(solution)/shard_map/outer/pallas_call | solution.py:606
  78.8 0.1 collective-permute-start.6
  78.9 4.5 %collective-permute-start.7 = (bf16[9,32,128]{2,1,0:T(8,128)(2,1)S(1)}, bf16[9,32,128]{2,1,0:T(8,128)(2,1)S(1)}, u32[]{:S(2)}, u32[]{:S(2)}) collective-permute-start(bf16[9,32,128]{2,1,0:T(8,128)(2,1)S(1)} %get-tuple-element.50), channel_id=1, source_target_pairs={{1,2},{2,1},{3,4},{4,3},{5,6},{6,5},{9,10},{10,9},{11,12},{12,11},... | collective-permute-start | bytes 221192 | tf_op jit(solution)/shard_map/ppermute | solution.py:519
  83.4 2.1 %lat.3.refs_0_ = f32[4,72,32,128]{3,2,1,0:T(8,128)S(1)} custom-call(f32[4,72,16,128]{3,2,1,0:T(8,128)S(1)} %get-tuple-element.47.zonal, f32[72,32,128]{2,1,0:T(8,128)S(1)} %copy-done, bf16[256,256]{1,0:T(8,128)(2,1)S(1)} %copy-done.5, f32[4,72,32,128]{3,2,1,0:T(8,128)S(1)} %get-tuple-element.48._result), custom_call_target="tpu_custom_call", output_to_operand_aliasing={{}: (3, {})} | custom-call | flops 23592960 | bytes 9437184 | tf_op jit(solution)/shard_map/lat/pallas_call | solution.py:627
  85.5 3.2 %collective-permute-done.7.refs_6_ = bf16[9,32,128]{2,1,0:T(8,128)(2,1)S(1)} collective-permute-done((bf16[9,32,128]{2,1,0:T(8,128)(2,1)S(1)}, bf16[9,32,128]{2,1,0:T(8,128)(2,1)S(1)}, u32[]{:S(2)}, u32[]{:S(2)}) %collective-permute-start.7) | collective-permute-done | bytes 73760 | tf_op jit(solution)/shard_map/ppermute | solution.py:519
  88.7 5.4 %column.3 = (f32[4,72,32,128]{3,2,1,0:T(8,128)}, f32[4,32,128]{2,1,0:T(8,128)}) custom-call(f32[4,72,32,128]{3,2,1,0:T(8,128)S(1)} %lat.3.refs_0_, f32[72,32,128]{2,1,0:T(8,128)S(1)} %copy-done, f32[71,32,128]{2,1,0:T(8,128)S(1)} %copy-done.2, f32[72,32,128]{2,1,0:T(8,128)S(1)} %get-tuple-element.38.refs_3_, f32[72,32,128]{2,1,0:T(8,128)S(1)} %get-tuple-element.39.refs_4_, ...), custom_call_target="tpu_custom_call" | custom-call | flops 23592960 | bytes 9437184 | tf_op jit(solution)/shard_map/column/pallas_call | solution.py:649
  (17 shorter events, 0.0 us)
Async XLA Ops:
  0.6 27.8 %copy-start.7 = (s32[4096]{0:T(1024)S(1)}, s32[4096]{0:T(1024)}, u32[]{:S(2)}) copy-start(s32[4096]{0:T(1024)} %param.22) | copy-start | bytes 49156
  3.3 25.1 %all-to-all-start = ((bf16[128,24,128]{2,1,0:T(8,128)(2,1)}), bf16[128,24,128]{2,1,0:T(8,128)(2,1)S(1)}, u32[]{:S(2)}, u32[]{:S(2)}) async-start(bf16[128,24,128]{2,1,0:T(8,128)(2,1)} %pack.1), calls=%async_computation | async-start | bytes 1572864 | tf_op jit(solution)/shard_map/all_to_all | solution.py:543
  31.9 10.3 %copy-start = (f32[72,32,128]{2,1,0:T(8,128)S(1)}, f32[72,32,128]{2,1,0:T(8,128)}, u32[]{:S(2)}) copy-start(f32[72,32,128]{2,1,0:T(8,128)} %refs_1_.3) | copy-start | bytes 3538948
  32.0 10.3 %copy-start.1 = (f32[72,32,128]{2,1,0:T(8,128)S(1)}, f32[72,32,128]{2,1,0:T(8,128)}, u32[]{:S(2)}) copy-start(f32[72,32,128]{2,1,0:T(8,128)} %courant.10) | copy-start | bytes 3538948
  32.0 10.3 %copy-start.3 = (bf16[256,512]{1,0:T(8,128)(2,1)S(1)}, bf16[256,512]{1,0:T(8,128)(2,1)}, u32[]{:S(2)}) copy-start(bf16[256,512]{1,0:T(8,128)(2,1)} %constant.24.clone.weights) | copy-start | bytes 786436
  40.7 8.4 %copy-start.6 = (bf16[256,256]{1,0:T(8,128)(2,1)S(1)}, bf16[256,256]{1,0:T(8,128)(2,1)}, u32[]{:S(2)}) copy-start(bf16[256,256]{1,0:T(8,128)(2,1)} %constant.25.clone.weights) | copy-start | bytes 393220
  40.7 5.2 %collective-permute-start = (bf16[4,288,128]{2,1,0:T(8,128)(2,1)S(1)}, bf16[4,288,128]{2,1,0:T(8,128)(2,1)S(1)}, u32[]{:S(2)}, u32[]{:S(2)}) collective-permute-start(bf16[4,288,128]{2,1,0:T(8,128)(2,1)S(1)} %get-tuple-element.32), channel_id=1, source_target_pairs={{0,8},{8,0},{16,24},{24,16},{32,40},{40,32},{48,56},{56,48},{64,72... | collective-permute-start | bytes 884744 | tf_op jit(solution)/shard_map/ppermute | solution.py:519
  40.8 8.3 %collective-permute-start.1 = (bf16[4,288,128]{2,1,0:T(8,128)(2,1)S(1)}, bf16[4,288,128]{2,1,0:T(8,128)(2,1)S(1)}, u32[]{:S(2)}, u32[]{:S(2)}) collective-permute-start(bf16[4,288,128]{2,1,0:T(8,128)(2,1)S(1)} %get-tuple-element.33), channel_id=1, source_target_pairs={{8,16},{16,8},{24,32},{32,24},{40,48},{48,40},{56,64},{64,56},{72,... | collective-permute-start | bytes 884744 | tf_op jit(solution)/shard_map/ppermute | solution.py:519
  45.9 11.8 %copy-start.2 = (f32[71,32,128]{2,1,0:T(8,128)S(1)}, f32[71,32,128]{2,1,0:T(8,128)}, u32[]{:S(2)}) copy-start(f32[71,32,128]{2,1,0:T(8,128)} %refs_2_.3) | copy-start | bytes 3489796
  45.9 12.7 %copy-start.5 = (bf16[256,256]{1,0:T(8,128)(2,1)S(1)}, bf16[256,256]{1,0:T(8,128)(2,1)}, u32[]{:S(2)}) copy-start(bf16[256,256]{1,0:T(8,128)(2,1)} %constant.26.clone.weights) | copy-start | bytes 393220
  52.1 8.6 %collective-permute-start.2 = (bf16[9,32,128]{2,1,0:T(8,128)(2,1)S(1)}, bf16[9,32,128]{2,1,0:T(8,128)(2,1)S(1)}, u32[]{:S(2)}, u32[]{:S(2)}) collective-permute-start(bf16[9,32,128]{2,1,0:T(8,128)(2,1)S(1)} %get-tuple-element.40), channel_id=1, source_target_pairs={{0,1},{1,0},{2,3},{3,2},{4,5},{5,4},{6,7},{7,6},{8,9},{9,8},{10,11... | collective-permute-start | bytes 221192 | tf_op jit(solution)/shard_map/ppermute | solution.py:519
  52.9 9.8 %collective-permute-start.3 = (bf16[9,32,128]{2,1,0:T(8,128)(2,1)S(1)}, bf16[9,32,128]{2,1,0:T(8,128)(2,1)S(1)}, u32[]{:S(2)}, u32[]{:S(2)}) collective-permute-start(bf16[9,32,128]{2,1,0:T(8,128)(2,1)S(1)} %get-tuple-element.41), channel_id=1, source_target_pairs={{1,2},{2,1},{3,4},{4,3},{5,6},{6,5},{9,10},{10,9},{11,12},{12,11},... | collective-permute-start | bytes 221192 | tf_op jit(solution)/shard_map/ppermute | solution.py:519
  58.6 4.2 %copy-start.4 = (bf16[256,256]{1,0:T(8,128)(2,1)S(1)}, bf16[256,256]{1,0:T(8,128)(2,1)}, u32[]{:S(2)}) copy-start(bf16[256,256]{1,0:T(8,128)(2,1)} %constant.27.clone.refs_7_) | copy-start | bytes 393220
  67.4 3.8 %collective-permute-start.4 = (bf16[4,288,128]{2,1,0:T(8,128)(2,1)S(1)}, bf16[4,288,128]{2,1,0:T(8,128)(2,1)S(1)}, u32[]{:S(2)}, u32[]{:S(2)}) collective-permute-start(bf16[4,288,128]{2,1,0:T(8,128)(2,1)S(1)} %get-tuple-element.43), channel_id=1, source_target_pairs={{0,8},{8,0},{16,24},{24,16},{32,40},{40,32},{48,56},{56,48},{64,72... | collective-permute-start | bytes 884744 | tf_op jit(solution)/shard_map/ppermute | solution.py:519
  67.5 8.3 %collective-permute-start.5 = (bf16[4,288,128]{2,1,0:T(8,128)(2,1)S(1)}, bf16[4,288,128]{2,1,0:T(8,128)(2,1)S(1)}, u32[]{:S(2)}, u32[]{:S(2)}) collective-permute-start(bf16[4,288,128]{2,1,0:T(8,128)(2,1)S(1)} %get-tuple-element.44), channel_id=1, source_target_pairs={{8,16},{16,8},{24,32},{32,24},{40,48},{48,40},{56,64},{64,56},{72,... | collective-permute-start | bytes 884744 | tf_op jit(solution)/shard_map/ppermute | solution.py:519
  78.8 6.7 %collective-permute-start.6 = (bf16[9,32,128]{2,1,0:T(8,128)(2,1)S(1)}, bf16[9,32,128]{2,1,0:T(8,128)(2,1)S(1)}, u32[]{:S(2)}, u32[]{:S(2)}) collective-permute-start(bf16[9,32,128]{2,1,0:T(8,128)(2,1)S(1)} %get-tuple-element.49), channel_id=1, source_target_pairs={{0,1},{1,0},{2,3},{3,2},{4,5},{5,4},{6,7},{7,6},{8,9},{9,8},{10,11... | collective-permute-start | bytes 221192 | tf_op jit(solution)/shard_map/ppermute | solution.py:519
  78.9 9.9 %collective-permute-start.7 = (bf16[9,32,128]{2,1,0:T(8,128)(2,1)S(1)}, bf16[9,32,128]{2,1,0:T(8,128)(2,1)S(1)}, u32[]{:S(2)}, u32[]{:S(2)}) collective-permute-start(bf16[9,32,128]{2,1,0:T(8,128)(2,1)S(1)} %get-tuple-element.50), channel_id=1, source_target_pairs={{1,2},{2,1},{3,4},{4,3},{5,6},{6,5},{9,10},{10,9},{11,12},{12,11},... | collective-permute-start | bytes 221192 | tf_op jit(solution)/shard_map/ppermute | solution.py:519

commit v6 on v5

--- a/solution.py
+++ b/solution.py
@@ -158,13 +158,22 @@
                 lhs[half + 72 * t : half + 72 * t + 72, lanes] = lo
 
 
-def forcing_kernel(starts, lhs, places, adjoint_hbm, state, x_a, x_b, adjoint, turned, arrived):
-    copy = pltpu.make_async_copy(adjoint_hbm, adjoint, arrived)
-    copy.start()
+def forcing_kernel(outer, starts, lhs, places, adjoint_hbm, *rest):
+    if outer:
+        state, x_a, x_b, adjoint, turned, arrived = rest
+        order = (0, 3)
+    else:
+        _, state, adjoint, turned, arrived = rest
+        order = (1, 2)
+    copies = [
+        pltpu.make_async_copy(adjoint_hbm.at[:, pl.ds(8 * step, 8), :], adjoint.at[n], arrived.at[n])
+        for n, step in enumerate(order)
+    ]
+    for copy in copies:
+        copy.start()
     fields = state.shape[0]
     chunks = lhs.shape[1] // CHUNK
     last = CHUNK // 128 - 2
-    steps = state.shape[1] // 8
     row = lax.broadcasted_iota(jnp.int32, (128, 256), 0).astype(f32)
     window = lax.broadcasted_iota(jnp.int32, (1, 256), 1)
 
@@ -196,7 +205,8 @@
         first = jnp.minimum(low >> 7, last)
         return first, jnp.maximum(((high + 127) >> 7) - first - 1, 0) >> 1
 
-    def eight(step, _):
+    def eight(n, _):
+        step = order[0] + n * (order[1] - order[0])
         rest = jnp.int32(0)
         for pair in range(4):
             number = step * 4 + pair
@@ -231,13 +241,15 @@
 
             lax.fori_loop(0, 4 * chunks, each, 0)
 
-        @pl.when(step == 0)
-        def _():
-            copy.wait()
+        for k in range(2):
+
+            @pl.when(n == k)
+            def _(k=k):
+                copies[k].wait()
 
         rows = pl.ds(pl.multiple_of(8 * step, 8), 8)
         for f in range(fields):
-            cell = adjoint[f, rows, :] + turned[9 * f : 9 * f + 8, :]
+            cell = adjoint[n, f] + turned[9 * f : 9 * f + 8, :]
             state[f, rows, :] = cell
             turned[9 * f : 9 * f + 8, :] = cell
 
@@ -247,20 +259,21 @@
             out[2] = second.astype(bf16)
             out[3] = third.astype(bf16)
 
-        odd = is_odd("gx")
-        for when, order, swapped in ((0, (0, 1, 2), odd), (steps - 1, (7, 6, 5), jnp.logical_not(odd))):
-            for out, mine in ((x_a, swapped), (x_b, jnp.logical_not(swapped))):
-
-                @pl.when((step == when) & mine)
-                def _(out=out, order=order):
-                    edge(out, order)
+        if outer:
+            odd = is_odd("gx")
+            for when, sides, swapped in ((0, (0, 1, 2), odd), (1, (7, 6, 5), jnp.logical_not(odd))):
+                for out, mine in ((x_a, swapped), (x_b, jnp.logical_not(swapped))):
+
+                    @pl.when((n == when) & mine)
+                    def _(out=out, sides=sides):
+                        edge(out, sides)
 
         return 0
 
-    lax.fori_loop(0, steps, eight, 0)
-
-
-def zonal_rows(outer, state, courant, courant_y, weights, halos, result, to_a, to_b, halves, kept, pad):
+    lax.fori_loop(0, 2, eight, 0)
+
+
+def zonal_rows(outer, state, courant, spread, halos, zonal, to_a, to_b, halves, pad):
     lane = lax.broadcasted_iota(jnp.int32, (16, 128), 1)
     group = lane >> 2
     odd_x = is_odd("gx")
@@ -307,26 +320,16 @@
                     out = v[0] * factors[0]
                     for k in (-1, 1, -2, 2, -3, 3):
                         out = out + v[k] * factors[k]
+                    if outer:
+                        zonal[t, level, 0:8, :] = out[:8]
+                        zonal[t, level, 24:32, :] = out[8:]
+                    else:
+                        zonal[t, level, 8:24, :] = out
                     at = slice(16 * (4 * l + t), 16 * (4 * l + t) + 16)
-                    if outer:
-                        result[t, level] = out
-                    else:
-                        kept[at, :] = out
                     halves[at, 0:128], halves[at, 128:256] = split(out)
             at = slice(64 * first, 64 * first + 256)
-            edges = jnp.dot(halves[at, :], weights[...], preferred_element_type=f32)
+            edges = jnp.dot(halves[at, :], spread[...], preferred_element_type=f32)
             for l in range(4):
-                if not outer:
-                    level = b * LB + first + l
-                    rows = slice(64 * l, 64 * l + 64)
-                    kept_rows = slice(64 * (first + l), 64 * (first + l) + 64)
-                    part = edges[rows, 256:512].reshape(4, 16, 256)
-                    c = courant_y[level, 8:24, :]
-                    result[:, level, 8:24, :] = (
-                        kept[kept_rows, :].reshape(4, 16, 128)
-                        + (c * (1.0 / 60.0)) * part[:, :, :128]
-                        + (c * c * (1.0 / 360.0)) * part[:, :, 128:]
-                    )
                 for t in range(4):
                     mine = group == t * LB + first + l
                     rows = slice(16 * (4 * l + t), 16 * (4 * l + t) + 16)
@@ -345,12 +348,12 @@
     lax.fori_loop(0, courant.shape[0] // LB, block, 0)
 
 
-def inner_kernel(state, courant, courant_y, weights, result, to_a, to_b, halves, kept):
-    zonal_rows(False, state, courant, courant_y, weights, None, result, to_a, to_b, halves, kept, None)
-
-
-def outer_kernel(state, courant, weights, from_a, from_b, _a, _b, zonal, to_a, to_b, halves, pad):
-    zonal_rows(True, state, courant, None, weights, (from_a, from_b), zonal, to_a, to_b, halves, None, pad)
+def inner_kernel(state, courant, spread, zonal, to_a, to_b, halves):
+    zonal_rows(False, state, courant, spread, None, zonal, to_a, to_b, halves, None)
+
+
+def outer_kernel(state, courant, spread, from_a, from_b, _z, _a, _b, zonal, to_a, to_b, halves, pad):
+    zonal_rows(True, state, courant, spread, (from_a, from_b), zonal, to_a, to_b, halves, pad)
 
 
 def stencil_factors(c):
@@ -363,7 +366,7 @@
     return factors
 
 
-def lat_kernel(zonal, courant, weights, _result, result, halves):
+def lat_kernel(zonal, courant, weights, result, halves):
     tracers, levels, lons, lats = zonal.shape
     rows = tracers * lons
 
@@ -372,80 +375,81 @@
             level = b * LB + l
             at = slice(l * rows, (l + 1) * rows)
             halves[at, 0:128], halves[at, 128:256] = split(zonal[:, level].reshape(rows, lats))
-        for l in range(0, LB, 4):
-            at = slice(l * rows, (l + 4) * rows)
-            several = jnp.dot(halves[at, :], weights[...], preferred_element_type=f32)
-            for n in range(4):
-                level = b * LB + l + n
-                both = several[n * rows : (n + 1) * rows].reshape(tracers, lons, 256)
-                c = jnp.concatenate([courant[level, 0:8, :], courant[level, 24:32, :]], axis=0)
-                out = (
-                    zonal[:, level]
-                    + (c * (1.0 / 60.0)) * both[:, :, :128]
-                    + (c * c * (1.0 / 360.0)) * both[:, :, 128:]
-                )
-                result[:, level, 0:8, :] = out[:, :8]
-                result[:, level, 24:32, :] = out[:, 8:]
+        for l in range(LB):
+            level = b * LB + l
+            at = slice(l * rows, (l + 1) * rows)
+            both = jnp.dot(halves[at, :], weights[...], preferred_element_type=f32).reshape(tracers, lons, 256)
+            c = courant[level]
+            result[:, level] = (
+                zonal[:, level] + (c * (1.0 / 60.0)) * both[:, :, :128] + (c * c * (1.0 / 360.0)) * both[:, :, 128:]
+            )
         return 0
 
     lax.fori_loop(0, levels // LB, block, 0)
 
 
-def column_kernel(first, inner, courant, mixing, inv, q, from_a, from_b, weights, *rest):
+def column_kernel(pieces, first, inner, courant, mixing, inv, q, from_a, from_b, weights, *rest):
     lhs = rest[-1]
-    if first:
+    x_a = x_b = before = None
+    if not first:
+        before, state, gradient = rest[:-1]
+    elif len(pieces) == 2:
         state, gradient, x_a, x_b = rest[:-1]
     else:
-        before, state, gradient = rest[:-1]
+        _, _, state, gradient = rest[:-1]
     levels = inv.shape[0]
-    lons = 32
+    lons = sum(count for _, count in pieces)
     rows = 4 * lons
+
+    def get(ref, *index):
+        parts = [ref[(*index, slice(start, start + count), slice(None))] for start, count in pieces]
+        return parts[0] if len(parts) == 1 else jnp.concatenate(parts, axis=-2)
+
+    def put(ref, value, *index):
+        done = 0
+        for start, count in pieces:
+            ref[(*index, slice(start, start + count), slice(None))] = value[..., done : done + count, :]
+            done += count
+
     lane = lax.broadcasted_iota(jnp.int32, (rows, 128), 1)
     row = lax.broadcasted_iota(jnp.int32, (rows, 128), 0)
-    owner = ((lane >> 2) - (row >> 5) * LB).astype(f32).astype(bf16)
+    owner = ((lane >> 2) - (row // lons) * LB).astype(f32).astype(bf16)
     zero = jnp.zeros((), bf16)
     odd_y = is_odd("gy")
 
-    def tile(r, _):
-        here = pl.ds(pl.multiple_of(lons * r, lons), lons)
-        carry = None
-        for b in range(levels // LB):
-            a, z = from_a[b, here, :].astype(f32), from_b[b, here, :].astype(f32)
-            notes = [
-                jnp.concatenate([note] * 4, axis=0).astype(bf16)
-                for note in (jnp.where(odd_y, a, z), jnp.where(odd_y, z, a))
-            ]
-            for l in range(LB):
-                at = slice((b * LB + l) * rows, (b * LB + l + 1) * rows)
-                mine = owner == jnp.asarray(l, bf16)
-                lhs[at, 0:128] = jnp.where(mine, notes[0], zero)
-                lhs[at, 128:256] = jnp.where(mine, notes[1], zero)
-            both = jnp.dot(
-                lhs[b * LB * rows : (b + 1) * LB * rows, :], weights[...], preferred_element_type=f32
-            )
-            for l in range(LB):
-                level = b * LB + l
-                c = courant[level, here, :]
-                part = both[l * rows : l * rows + rows].reshape(4, lons, 256)
-                y = inner[:, level, here, :]
-                y = y + (c * (1.0 / 60.0)) * part[:, :, :128] + (c * c * (1.0 / 360.0)) * part[:, :, 128:]
-                if level > 0:
-                    y = y + mixing[level - 1, here, :] * carry
-                carry = y * inv[level, here, :]
-                state[:, level, here, :] = carry
-
-        def back(j, carry):
-            level = levels - 2 - j
-            carry = state[:, level, here, :] + q[level, here, :] * carry
-            state[:, level, here, :] = carry
-            return carry
-
-        carry = lax.fori_loop(0, levels - 1, back, carry, unroll=8)
-        gradient[:, here, :] = carry if first else before[:, here, :] + carry
-        return 0
-
-    lax.fori_loop(0, inner.shape[2] // lons, tile, 0)
-    if first:
+    every = slice(None)
+    carry = None
+    for b in range(levels // LB):
+        a, z = get(from_a, b).astype(f32), get(from_b, b).astype(f32)
+        notes = [
+            jnp.concatenate([note] * 4, axis=0).astype(bf16) for note in (jnp.where(odd_y, a, z), jnp.where(odd_y, z, a))
+        ]
+        for l in range(LB):
+            at = slice((b * LB + l) * rows, (b * LB + l + 1) * rows)
+            mine = owner == jnp.asarray(l, bf16)
+            lhs[at, 0:128] = jnp.where(mine, notes[0], zero)
+            lhs[at, 128:256] = jnp.where(mine, notes[1], zero)
+        both = jnp.dot(lhs[b * LB * rows : (b + 1) * LB * rows, :], weights[...], preferred_element_type=f32)
+        for l in range(LB):
+            level = b * LB + l
+            c = get(courant, level)
+            part = both[l * rows : l * rows + rows].reshape(4, lons, 256)
+            y = get(inner, every, level)
+            y = y + (c * (1.0 / 60.0)) * part[:, :, :128] + (c * c * (1.0 / 360.0)) * part[:, :, 128:]
+            if level > 0:
+                y = y + get(mixing, level - 1) * carry
+            carry = y * get(inv, level)
+            put(state, carry, every, level)
+
+    def back(j, carry):
+        level = levels - 2 - j
+        carry = get(state, every, level) + get(q, level) * carry
+        put(state, carry, every, level)
+        return carry
+
+    carry = lax.fori_loop(0, levels - 1, back, carry, unroll=8)
+    put(gradient, carry if first else get(before, every) + carry, every)
+    if x_a is not None:
 
         def edge(out, order):
             for t in range(4):
@@ -568,47 +572,58 @@
 
     vmem = pl.BlockSpec(memory_space=pltpu.VMEM)
     edge = shape((4, fields, lats), bf16)
-    state, x_a, x_b = pl.pallas_call(
-        forcing_kernel,
-        in_specs=[pl.BlockSpec(memory_space=pltpu.SMEM), vmem, vmem, pl.BlockSpec(memory_space=pl.ANY)],
-        out_specs=[vmem] * 3,
-        out_shape=[shape((fields, lons, lats)), edge, edge],
-        scratch_shapes=[
-            pltpu.VMEM((fields, lons, lats), f32),
-            pltpu.VMEM((fields * 9, lats), f32),
-            pltpu.SemaphoreType.DMA,
-        ],
-        compiler_params=params(40),
-        cost_estimate=cost(10**10, 2 * size),
-        name="forcing",
-    )(starts, lhs, places, adjoint_in.reshape(fields, lons, lats))
+    smem = pl.BlockSpec(memory_space=pltpu.SMEM)
+    forcing_args = [starts, lhs, places, adjoint_in.reshape(fields, lons, lats)]
+
+    def forcing(outer, *more):
+        def kernel(*refs):
+            forcing_kernel(outer, *refs)
+
+        return pl.pallas_call(
+            kernel,
+            in_specs=[smem, vmem, vmem, pl.BlockSpec(memory_space=pl.ANY)] + [vmem] * len(more),
+            out_specs=[vmem] * (3 if outer else 1),
+            out_shape=[shape((fields, lons, lats))] + [edge] * (2 if outer else 0),
+            input_output_aliases={} if outer else {4: 0},
+            scratch_shapes=[
+                pltpu.VMEM((2, fields, 8, lats), f32),
+                pltpu.VMEM((fields * 9, lats), f32),
+                pltpu.SemaphoreType.DMA((2,)),
+            ],
+            compiler_params=params(44),
+            cost_estimate=cost(5 * 10**9, size),
+            name="forcing",
+        )(*forcing_args, *more)
+
+    state, x_a, x_b = forcing(True)
+    (state,) = forcing(False, state)
 
     whole_field = shape((tracers, levels, lons, lats))
     blocks = levels // LB
     note = shape((blocks, lons, 128), bf16)
-    spread = edge_weights()
+    spread = jnp.asarray(edge_weights(), bf16)
     table = lat_weights()
     for step in range(STEPS):
         got_b = swap(x_b, "gx", False, True)
         got_a = swap(x_a, "gx", True, True)
         halves = pltpu.VMEM((tracers * LB * 16, 2 * lats), bf16)
         state = state.reshape(tracers, levels, lons, lats)
-        result, to_a, to_b = pl.pallas_call(
+        partial = pl.pallas_call(
             inner_kernel,
-            in_specs=[vmem] * 4,
+            in_specs=[vmem] * 3,
             out_specs=[vmem] * 3,
             out_shape=[whole_field, note, note],
-            scratch_shapes=[halves, pltpu.VMEM((tracers * LB * 16, lats), f32)],
+            scratch_shapes=[halves],
             compiler_params=params(24),
             cost_estimate=cost(5 * size, 2 * size),
             name="inner",
-        )(state, courant_x, courant_y, jnp.asarray(np.concatenate([spread, table[:256]], axis=1), bf16))
+        )(state, courant_x, spread)
         zonal, to_a, to_b = pl.pallas_call(
             outer_kernel,
-            in_specs=[vmem] * 7,
+            in_specs=[vmem] * 8,
             out_specs=[vmem] * 3,
-            out_shape=[shape((tracers, levels, 16, lats)), note, note],
-            input_output_aliases={5: 1, 6: 2},
+            out_shape=[whole_field, note, note],
+            input_output_aliases={5: 0, 6: 1, 7: 2},
             scratch_shapes=[halves, pltpu.VMEM((tracers * LB * 33, lats), f32)],
             compiler_params=params(24),
             cost_estimate=cost(5 * size, 2 * size),
@@ -616,50 +631,49 @@
         )(
             state,
             courant_x,
-            jnp.asarray(spread, bf16),
+            spread,
             got_a.reshape(4, tracers, levels, lats),
             got_b.reshape(4, tracers, levels, lats),
-            to_a,
-            to_b,
+            *partial,
         )
         y_b = swap(to_b, "gy", False, False)
         y_a = swap(to_a, "gy", True, False)
         inner = pl.pallas_call(
             lat_kernel,
-            in_specs=[vmem] * 4,
+            in_specs=[vmem] * 3,
             out_specs=vmem,
             out_shape=whole_field,
-            input_output_aliases={3: 0},
-            scratch_shapes=[halves],
+            scratch_shapes=[pltpu.VMEM((LB * tracers * lons, 2 * lats), bf16)],
             compiler_params=params(24),
             cost_estimate=cost(5 * size, 2 * size),
             name="lat",
-        )(zonal, courant_y, jnp.asarray(table[:256], bf16), result)
+        )(zonal, courant_y, jnp.asarray(table[:256], bf16))
         first = step == 0
         operands = [inner, courant_y, mixing, inv, q, y_a, y_b, jnp.asarray(table[256:], bf16)]
-        out_shape = [whole_field, shape((tracers, lons, lats))]
+        gradient_shape = shape((tracers, lons, lats))
+
+        def column(pieces, operands, extra, aliases):
+            def kernel(*refs):
+                column_kernel(pieces, first, *refs)
+
+            rows = sum(count for _, count in pieces)
+            return pl.pallas_call(
+                kernel,
+                in_specs=[vmem] * len(operands),
+                out_specs=[vmem] * (2 + len(extra)),
+                out_shape=[whole_field, gradient_shape] + extra,
+                input_output_aliases=aliases,
+                scratch_shapes=[pltpu.VMEM((levels * tracers * rows, 2 * lats), bf16)],
+                compiler_params=params(24),
+                cost_estimate=cost(5 * size, 2 * size),
+                name="column",
+            )(*operands)
+
         if first:
-            out_shape += [edge, edge]
+            state, gradient, x_a, x_b = column(((0, 8), (24, 8)), operands, [edge, edge], {})
+            state, gradient = column(((8, 16),), operands + [state, gradient], [], {8: 0, 9: 1})
         else:
-            operands.append(gradient)
-
-        def kernel(*refs, first=first):
-            column_kernel(first, *refs)
-
-        out = pl.pallas_call(
-            kernel,
-            in_specs=[vmem] * len(operands),
-            out_specs=[vmem] * len(out_shape),
-            out_shape=out_shape,
-            scratch_shapes=[pltpu.VMEM((levels * tracers * 32, 2 * lats), bf16)],
-            compiler_params=params(24),
-            cost_estimate=cost(5 * size, 2 * size),
-            name="column",
-        )(*operands)
-        if first:
-            state, gradient, x_a, x_b = out
-        else:
-            state, gradient = out
+            state, gradient = column(((0, 32),), operands + [gradient], [], {})
     return state, gradient
 
 

time: 94.4 us -> 88.5 us (0.937)
  waiting for transfers between devices: 24.8 us -> 16.4 us
  starting transfers between devices: 22.1 us -> 24.5 us
    ppermute x8, waiting for transfers between devices: 13.2 us -> 4.78 us  [swap(): return lax.ppermute(value, axis, pairs)]
    ppermute x8, starting transfers between devices: 11.9 us -> 14.2 us  [swap(): return lax.ppermute(value, axis, pairs)]
    pallas_call x9 -> x11, Pallas kernels: 36 us -> 36.1 us  [the longest x3 10.1 us: column(): pl.pallas_call(kernel, in_specs=[vmem] * len(operands), out_specs=[vmem]...]
  transfers between devices with their start and end apart: 9 -> 9, of which waited for: 5 -> 4; matrix products, arithmetic and copies ran while one was open for 1% -> 2% of each run, Pallas kernels for 15% -> 23%
where the time goes in v6:
time: 88.5 us; the launch traced here: 88.2 us
  Pallas kernels  45.1 us (51%)
  starting transfers between devices  24.5 us (28%)
  waiting for transfers between devices  16.4 us (19%)
  between operations  0.91 us (1%)
    ppermute x8, starting transfers between devices, swap(): return lax.ppermute(value, axis, pairs)  14.2 us
    all_to_all x1, waiting for transfers between devices, local(): lax.all_to_all(packed, ('gx', 'gy'), split_axis=0, concat_axis=0, tiled=T...  11.6 us
    all_to_all x1, starting transfers between devices, local(): lax.all_to_all(packed, ('gx', 'gy'), split_axis=0, concat_axis=0, tiled=T...  10.3 us
    pallas_call x3, Pallas kernels, column(): pl.pallas_call(kernel, in_specs=[vmem] * len(operands), out_specs=[vmem]...  10.1 us
    pallas_call x2, Pallas kernels, forcing(): pl.pallas_call(kernel, in_specs=[smem, vmem, vmem, pl.BlockSpec(memory_sp...  8.51 us
    pallas_call x2, Pallas kernels, local(): pl.pallas_call(outer_kernel, in_specs=[vmem] * 8, out_specs=[vmem] * 3, o...  5.94 us
    pallas_call x2, Pallas kernels, local(): pl.pallas_call(lat_kernel, in_specs=[vmem] * 3, out_specs=vmem, out_shape...  5.9 us
    pallas_call x2, Pallas kernels, local(): pl.pallas_call(inner_kernel, in_specs=[vmem] * 3, out_specs=[vmem] * 3, o...  5.67 us
  transfers between devices with their start and end apart: 9, of which 4 were waited for; matrix products, arithmetic and copies ran while one was open for 2% of the time, Pallas kernels for 23%

profile of v6, /device:TPU:24, one launch (start us, length us, event | category | flops | bytes accessed | tf_op | source)
XLA Modules:
  0.0 88.2 jit_solution(13152595642528675049)
XLA Ops:
  0.6 2.6 %pack.1 = bf16[128,24,128]{2,1,0:T(8,128)(2,1)} custom-call(s32[1,128]{1,0:T(1,128)} %counts.1, bf16[72,4096]{1,0:T(8,128)(2,1)} %rows.1, bf16[4,4096]{1,0:T(4,128)(2,1)} %weights.3), custom_call_target="tpu_custom_call" | custom-call | tf_op jit(solution)/shard_map/pack/pallas_call | solution.py:533
  3.3 10.3 %all-to-all-start = ((bf16[128,24,128]{2,1,0:T(8,128)(2,1)}), bf16[128,24,128]{2,1,0:T(8,128)(2,1)S(1)}, u32[]{:S(2)}, u32[]{:S(2)}) async-start(bf16[128,24,128]{2,1,0:T(8,128)(2,1)} %pack.1), calls=%async_computation | async-start | bytes 1572864 | tf_op jit(solution)/shard_map/all_to_all | solution.py:547
  13.5 0.7 fusion.1
  14.3 0.6 broadcast_in_dim.2.bins
  14.9 1.9 %rank.1 = (bf16[4096,128]{1,0:T(8,128)(2,1)S(1)}, s32[32,128]{1,0:T(8,128)S(1)}) custom-call(bf16[4096,128]{1,0:T(8,128)(2,1)S(1)} %broadcast_in_dim.2.bins), custom_call_target="tpu_custom_call" | custom-call | flops 1000000000 | bytes 2000000 | tf_op jit(solution)/shard_map/rank/pallas_call | solution.py:557
  16.8 11.6 %all-to-all-done.got = bf16[128,24,128]{2,1,0:T(8,128)(2,1)S(1)} async-done(((bf16[128,24,128]{2,1,0:T(8,128)(2,1)}), bf16[128,24,128]{2,1,0:T(8,128)(2,1)S(1)}, u32[]{:S(2)}, u32[]{:S(2)}) %all-to-all-start) | async-done | bytes 786464 | tf_op jit(solution)/shard_map/all_to_all | solution.py:547
  28.4 3.5 %order.1 = (bf16[576,4096]{1,0:T(8,128)(2,1)S(1)}, f32[8,4096]{1,0:T(8,128)S(1)}) custom-call(bf16[128,24,128]{2,1,0:T(8,128)(2,1)S(1)} %all-to-all-done.got, s32[1,4096]{1,0:T(1,128)S(1)} %bitcast.13, bf16[4096,128]{1,0:T(8,128)(2,1)S(1)} %get-tuple-element.30.code), custom_call_target="tpu_custom_call" | custom-call | flops 1000000000 | bytes 8000000 | tf_op jit(solution)/shard_map/order/pallas_call | solution.py:564
  31.9 4.3 %forcing.2 = (f32[288,32,128]{2,1,0:T(8,128)S(1)}, bf16[4,288,128]{2,1,0:T(8,128)(2,1)S(1)}, bf16[4,288,128]{2,1,0:T(8,128)(2,1)S(1)}) custom-call(s32[32,128]{1,0:T(8,128)S(1)} %get-tuple-element.29.refs_0_, bf16[576,4096]{1,0:T(8,128)(2,1)S(1)} %get-tuple-element.31.refs_1_, f32[8,4096]{1,0:T(8,128)S(1)} %get-tuple-element.32.refs_2_, f32[288,32,128]{2,1,0:T(8,128)} %bitcast.14), custom_call_target="tpu_custom_call" | custom-call | flops 5000000000 | bytes 4718592 | tf_op jit(solution)/shard_map/forcing/pallas_call | solution.py:582
  36.2 0.1 collective-permute-start
  36.3 1.5 %collective-permute-start.1 = (bf16[4,288,128]{2,1,0:T(8,128)(2,1)S(1)}, bf16[4,288,128]{2,1,0:T(8,128)(2,1)S(1)}, u32[]{:S(2)}, u32[]{:S(2)}) collective-permute-start(bf16[4,288,128]{2,1,0:T(8,128)(2,1)S(1)} %get-tuple-element.35), channel_id=1, source_target_pairs={{8,16},{16,8},{24,32},{32,24},{40,48},{48,40},{56,64},{64,56},{72,... | collective-permute-start | bytes 884744 | tf_op jit(solution)/shard_map/ppermute | solution.py:523
  37.8 4.2 %forcing.3 = f32[288,32,128]{2,1,0:T(8,128)S(1)} custom-call(s32[32,128]{1,0:T(8,128)S(1)} %get-tuple-element.29.refs_0_, bf16[576,4096]{1,0:T(8,128)(2,1)S(1)} %get-tuple-element.31.refs_1_, f32[8,4096]{1,0:T(8,128)S(1)} %get-tuple-element.32.refs_2_, f32[288,32,128]{2,1,0:T(8,128)} %bitcast.15, ...), custom_call_target="tpu_custom_call", output_to_operand_aliasing={{}: (4, {})} | custom-call | flops 5000000000 | bytes 4718592 | tf_op jit(solution)/shard_map/forcing/pallas_call | solution.py:582
  42.1 2.8 %inner.2 = (f32[4,72,32,128]{3,2,1,0:T(8,128)S(1)}, bf16[9,32,128]{2,1,0:T(8,128)(2,1)S(1)}, bf16[9,32,128]{2,1,0:T(8,128)(2,1)S(1)}) custom-call(f32[4,72,32,128]{3,2,1,0:T(8,128)S(1)} %bitcast.7, f32[72,32,128]{2,1,0:T(8,128)S(1)} %copy-done.1, bf16[256,256]{1,0:T(8,128)(2,1)S(1)} %copy-done.3), custom_call_target="tpu_custom_call" | custom-call | flops 23592960 | bytes 9437184 | tf_op jit(solution)/shard_map/inner/pallas_call | solution.py:611
  44.9 0.0 copy-start.5
  45.0 3.0 %outer.2 = (f32[4,72,32,128]{3,2,1,0:T(8,128)S(1)}, bf16[9,32,128]{2,1,0:T(8,128)(2,1)S(1)}, bf16[9,32,128]{2,1,0:T(8,128)(2,1)S(1)}) custom-call(f32[4,72,32,128]{3,2,1,0:T(8,128)S(1)} %bitcast.8, f32[72,32,128]{2,1,0:T(8,128)S(1)} %copy-done.1, bf16[256,256]{1,0:T(8,128)(2,1)S(1)} %copy-done.3, ...), custom_call_target="tpu_custom_call", output_to_operand_aliasing={{0}: (5, {}), {1}: (6, {}), {2}: (7, {})} | custom-call | flops 23592960 | bytes 9437184 | tf_op jit(solution)/shard_map/outer/pallas_call | solution.py:621
  47.9 0.6 collective-permute-start.2
  48.6 5.4 %collective-permute-start.3 = (bf16[9,32,128]{2,1,0:T(8,128)(2,1)S(1)}, bf16[9,32,128]{2,1,0:T(8,128)(2,1)S(1)}, u32[]{:S(2)}, u32[]{:S(2)}) collective-permute-start(bf16[9,32,128]{2,1,0:T(8,128)(2,1)S(1)} %get-tuple-element.43), channel_id=1, source_target_pairs={{1,2},{2,1},{3,4},{4,3},{5,6},{6,5},{9,10},{10,9},{11,12},{12,11},... | collective-permute-start | bytes 221192 | tf_op jit(solution)/shard_map/ppermute | solution.py:523
  53.9 0.9 %factor.1 = (f32[72,32,128]{2,1,0:T(8,128)S(1)}, f32[72,32,128]{2,1,0:T(8,128)S(1)}) custom-call(f32[71,32,128]{2,1,0:T(8,128)S(1)} %copy-done.2), custom_call_target="tpu_custom_call" | custom-call | flops 8847360 | bytes 3538944 | tf_op jit(solution)/shard_map/factor/pallas_call | solution.py:549
  54.9 0.0 copy-start.4
  54.9 3.0 %lat.2.refs_0_ = f32[4,72,32,128]{3,2,1,0:T(8,128)S(1)} custom-call(f32[4,72,32,128]{3,2,1,0:T(8,128)S(1)} %get-tuple-element.39.zonal, f32[72,32,128]{2,1,0:T(8,128)S(1)} %copy-done, bf16[256,256]{1,0:T(8,128)(2,1)S(1)} %copy-done.5), custom_call_target="tpu_custom_call" | custom-call | flops 23592960 | bytes 9437184 | tf_op jit(solution)/shard_map/lat/pallas_call | solution.py:641
  57.9 0.5 collective-permute-done.3.refs_6_
  58.4 3.0 %column.3 = (f32[4,72,32,128]{3,2,1,0:T(8,128)S(1)}, f32[4,32,128]{2,1,0:T(8,128)S(1)}, bf16[4,288,128]{2,1,0:T(8,128)(2,1)S(1)}, bf16[4,288,128]{2,1,0:T(8,128)(2,1)S(1)}) custom-call(f32[4,72,32,128]{3,2,1,0:T(8,128)S(1)} %lat.2.refs_0_, f32[72,32,128]{2,1,0:T(8,128)S(1)} %copy-done, f32[71,32,128]{2,1,0:T(8,128)S(1)} %copy-done.2, ...), custom_call_target="tpu_custom_call" | custom-call | flops 23592960 | bytes 9437184 | tf_op jit(solution)/shard_map/column/pallas_call | solution.py:660
  61.4 0.1 collective-permute-start.4
  61.5 1.3 %collective-permute-start.5 = (bf16[4,288,128]{2,1,0:T(8,128)(2,1)S(1)}, bf16[4,288,128]{2,1,0:T(8,128)(2,1)S(1)}, u32[]{:S(2)}, u32[]{:S(2)}) collective-permute-start(bf16[4,288,128]{2,1,0:T(8,128)(2,1)S(1)} %get-tuple-element.48), channel_id=1, source_target_pairs={{8,16},{16,8},{24,32},{32,24},{40,48},{48,40},{56,64},{64,56},{72,... | collective-permute-start | bytes 884744 | tf_op jit(solution)/shard_map/ppermute | solution.py:523
  62.9 1.6 %column.4 = (f32[4,72,32,128]{3,2,1,0:T(8,128)S(1)}, f32[4,32,128]{2,1,0:T(8,128)S(1)}) custom-call(f32[4,72,32,128]{3,2,1,0:T(8,128)S(1)} %lat.2.refs_0_, f32[72,32,128]{2,1,0:T(8,128)S(1)} %copy-done, f32[71,32,128]{2,1,0:T(8,128)S(1)} %copy-done.2, f32[72,32,128]{2,1,0:T(8,128)S(1)} %get-tuple-element.40.refs_3_, ...), custom_call_target="tpu_custom_call", output_to_operand_aliasing={{0}: (8, {}), {1}: (9, {})} | custom-call | flops 23592960 | bytes 9437184 | tf_op jit(solution)/shard_map/column/pallas_call | solution.py:660
  64.5 2.8 %inner.3 = (f32[4,72,32,128]{3,2,1,0:T(8,128)S(1)}, bf16[9,32,128]{2,1,0:T(8,128)(2,1)S(1)}, bf16[9,32,128]{2,1,0:T(8,128)(2,1)S(1)}) custom-call(f32[4,72,32,128]{3,2,1,0:T(8,128)S(1)} %get-tuple-element.46.state, f32[72,32,128]{2,1,0:T(8,128)S(1)} %copy-done.1, bf16[256,256]{1,0:T(8,128)(2,1)S(1)} %copy-done.3), custom_call_target="tpu_custom_call" | custom-call | flops 23592960 | bytes 9437184 | tf_op jit(solution)/shard_map/inner/pallas_call | solution.py:611
  67.4 2.5 %collective-permute-done.5 = bf16[4,288,128]{2,1,0:T(8,128)(2,1)S(1)} collective-permute-done((bf16[4,288,128]{2,1,0:T(8,128)(2,1)S(1)}, bf16[4,288,128]{2,1,0:T(8,128)(2,1)S(1)}, u32[]{:S(2)}, u32[]{:S(2)}) %collective-permute-start.5) | collective-permute-done | bytes 294944 | tf_op jit(solution)/shard_map/ppermute | solution.py:523
  69.9 3.0 %outer.3 = (f32[4,72,32,128]{3,2,1,0:T(8,128)S(1)}, bf16[9,32,128]{2,1,0:T(8,128)(2,1)S(1)}, bf16[9,32,128]{2,1,0:T(8,128)(2,1)S(1)}) custom-call(f32[4,72,32,128]{3,2,1,0:T(8,128)S(1)} %get-tuple-element.46.state, f32[72,32,128]{2,1,0:T(8,128)S(1)} %copy-done.1, ...), custom_call_target="tpu_custom_call", output_to_operand_aliasing={{0}: (5, {}), {1}: (6, {}), {2}: (7, {})} | custom-call | flops 23592960 | bytes 9437184 | tf_op jit(solution)/shard_map/outer/pallas_call | solution.py:621
  72.9 0.1 collective-permute-start.6
  72.9 5.2 %collective-permute-start.7 = (bf16[9,32,128]{2,1,0:T(8,128)(2,1)S(1)}, bf16[9,32,128]{2,1,0:T(8,128)(2,1)S(1)}, u32[]{:S(2)}, u32[]{:S(2)}) collective-permute-start(bf16[9,32,128]{2,1,0:T(8,128)(2,1)S(1)} %get-tuple-element.54), channel_id=1, source_target_pairs={{1,2},{2,1},{3,4},{4,3},{5,6},{6,5},{9,10},{10,9},{11,12},{12,11},... | collective-permute-start | bytes 221192 | tf_op jit(solution)/shard_map/ppermute | solution.py:523
  78.2 2.9 %lat.3.refs_0_ = f32[4,72,32,128]{3,2,1,0:T(8,128)S(1)} custom-call(f32[4,72,32,128]{3,2,1,0:T(8,128)S(1)} %get-tuple-element.52.zonal, f32[72,32,128]{2,1,0:T(8,128)S(1)} %copy-done, bf16[256,256]{1,0:T(8,128)(2,1)S(1)} %copy-done.5), custom_call_target="tpu_custom_call" | custom-call | flops 23592960 | bytes 9437184 | tf_op jit(solution)/shard_map/lat/pallas_call | solution.py:641
  81.0 1.8 %collective-permute-done.7.refs_6_ = bf16[9,32,128]{2,1,0:T(8,128)(2,1)S(1)} collective-permute-done((bf16[9,32,128]{2,1,0:T(8,128)(2,1)S(1)}, bf16[9,32,128]{2,1,0:T(8,128)(2,1)S(1)}, u32[]{:S(2)}, u32[]{:S(2)}) %collective-permute-start.7) | collective-permute-done | bytes 73760 | tf_op jit(solution)/shard_map/ppermute | solution.py:523
  82.8 5.4 %column.5 = (f32[4,72,32,128]{3,2,1,0:T(8,128)}, f32[4,32,128]{2,1,0:T(8,128)}) custom-call(f32[4,72,32,128]{3,2,1,0:T(8,128)S(1)} %lat.3.refs_0_, f32[72,32,128]{2,1,0:T(8,128)S(1)} %copy-done, f32[71,32,128]{2,1,0:T(8,128)S(1)} %copy-done.2, f32[72,32,128]{2,1,0:T(8,128)S(1)} %get-tuple-element.40.refs_3_, f32[72,32,128]{2,1,0:T(8,128)S(1)} %get-tuple-element.41.refs_4_, ...), custom_call_target="tpu_custom_call" | custom-call | flops 23592960 | bytes 9437184 | tf_op jit(solution)/shard_map/column/pallas_call | solution.py:660
  (17 shorter events, 0.0 us)
Async XLA Ops:
  0.6 27.8 %copy-start.6 = (s32[4096]{0:T(1024)S(1)}, s32[4096]{0:T(1024)}, u32[]{:S(2)}) copy-start(s32[4096]{0:T(1024)} %param.19) | copy-start | bytes 49156
  3.3 25.1 %all-to-all-start = ((bf16[128,24,128]{2,1,0:T(8,128)(2,1)}), bf16[128,24,128]{2,1,0:T(8,128)(2,1)S(1)}, u32[]{:S(2)}, u32[]{:S(2)}) async-start(bf16[128,24,128]{2,1,0:T(8,128)(2,1)} %pack.1), calls=%async_computation | async-start | bytes 1572864 | tf_op jit(solution)/shard_map/all_to_all | solution.py:547
  36.2 8.7 %collective-permute-start = (bf16[4,288,128]{2,1,0:T(8,128)(2,1)S(1)}, bf16[4,288,128]{2,1,0:T(8,128)(2,1)S(1)}, u32[]{:S(2)}, u32[]{:S(2)}) collective-permute-start(bf16[4,288,128]{2,1,0:T(8,128)(2,1)S(1)} %get-tuple-element.34), channel_id=1, source_target_pairs={{0,8},{8,0},{16,24},{24,16},{32,40},{40,32},{48,56},{56,48},{64,72... | collective-permute-start | bytes 884744 | tf_op jit(solution)/shard_map/ppermute | solution.py:523
  36.3 8.6 %collective-permute-start.1 = (bf16[4,288,128]{2,1,0:T(8,128)(2,1)S(1)}, bf16[4,288,128]{2,1,0:T(8,128)(2,1)S(1)}, u32[]{:S(2)}, u32[]{:S(2)}) collective-permute-start(bf16[4,288,128]{2,1,0:T(8,128)(2,1)S(1)} %get-tuple-element.35), channel_id=1, source_target_pairs={{8,16},{16,8},{24,32},{32,24},{40,48},{48,40},{56,64},{64,56},{72,... | collective-permute-start | bytes 884744 | tf_op jit(solution)/shard_map/ppermute | solution.py:523
  37.8 4.2 %copy-start.1 = (f32[72,32,128]{2,1,0:T(8,128)S(1)}, f32[72,32,128]{2,1,0:T(8,128)}, u32[]{:S(2)}) copy-start(f32[72,32,128]{2,1,0:T(8,128)} %courant.10) | copy-start | bytes 3538948
  37.8 4.2 %copy-start.3 = (bf16[256,256]{1,0:T(8,128)(2,1)S(1)}, bf16[256,256]{1,0:T(8,128)(2,1)}, u32[]{:S(2)}) copy-start(bf16[256,256]{1,0:T(8,128)(2,1)} %constant.22.clone.spread) | copy-start | bytes 393220
  44.9 9.0 %copy-start.2 = (f32[71,32,128]{2,1,0:T(8,128)S(1)}, f32[71,32,128]{2,1,0:T(8,128)}, u32[]{:S(2)}) copy-start(f32[71,32,128]{2,1,0:T(8,128)} %refs_2_.5) | copy-start | bytes 3489796
  44.9 9.9 %copy-start = (f32[72,32,128]{2,1,0:T(8,128)S(1)}, f32[72,32,128]{2,1,0:T(8,128)}, u32[]{:S(2)}) copy-start(f32[72,32,128]{2,1,0:T(8,128)} %refs_1_.5) | copy-start | bytes 3538948
  44.9 9.9 %copy-start.5 = (bf16[256,256]{1,0:T(8,128)(2,1)S(1)}, bf16[256,256]{1,0:T(8,128)(2,1)}, u32[]{:S(2)}) copy-start(bf16[256,256]{1,0:T(8,128)(2,1)} %constant.23.clone.weights) | copy-start | bytes 393220
  47.9 10.0 %collective-permute-start.2 = (bf16[9,32,128]{2,1,0:T(8,128)(2,1)S(1)}, bf16[9,32,128]{2,1,0:T(8,128)(2,1)S(1)}, u32[]{:S(2)}, u32[]{:S(2)}) collective-permute-start(bf16[9,32,128]{2,1,0:T(8,128)(2,1)S(1)} %get-tuple-element.42), channel_id=1, source_target_pairs={{0,1},{1,0},{2,3},{3,2},{4,5},{5,4},{6,7},{7,6},{8,9},{9,8},{10,11... | collective-permute-start | bytes 221192 | tf_op jit(solution)/shard_map/ppermute | solution.py:523
  48.6 9.8 %collective-permute-start.3 = (bf16[9,32,128]{2,1,0:T(8,128)(2,1)S(1)}, bf16[9,32,128]{2,1,0:T(8,128)(2,1)S(1)}, u32[]{:S(2)}, u32[]{:S(2)}) collective-permute-start(bf16[9,32,128]{2,1,0:T(8,128)(2,1)S(1)} %get-tuple-element.43), channel_id=1, source_target_pairs={{1,2},{2,1},{3,4},{4,3},{5,6},{6,5},{9,10},{10,9},{11,12},{12,11},... | collective-permute-start | bytes 221192 | tf_op jit(solution)/shard_map/ppermute | solution.py:523
  54.9 3.6 %copy-start.4 = (bf16[256,256]{1,0:T(8,128)(2,1)S(1)}, bf16[256,256]{1,0:T(8,128)(2,1)}, u32[]{:S(2)}) copy-start(bf16[256,256]{1,0:T(8,128)(2,1)} %constant.24.clone.refs_7_) | copy-start | bytes 393220
  61.4 5.9 %collective-permute-start.4 = (bf16[4,288,128]{2,1,0:T(8,128)(2,1)S(1)}, bf16[4,288,128]{2,1,0:T(8,128)(2,1)S(1)}, u32[]{:S(2)}, u32[]{:S(2)}) collective-permute-start(bf16[4,288,128]{2,1,0:T(8,128)(2,1)S(1)} %get-tuple-element.47), channel_id=1, source_target_pairs={{0,8},{8,0},{16,24},{24,16},{32,40},{40,32},{48,56},{56,48},{64,72... | collective-permute-start | bytes 884744 | tf_op jit(solution)/shard_map/ppermute | solution.py:523
  61.5 8.3 %collective-permute-start.5 = (bf16[4,288,128]{2,1,0:T(8,128)(2,1)S(1)}, bf16[4,288,128]{2,1,0:T(8,128)(2,1)S(1)}, u32[]{:S(2)}, u32[]{:S(2)}) collective-permute-start(bf16[4,288,128]{2,1,0:T(8,128)(2,1)S(1)} %get-tuple-element.48), channel_id=1, source_target_pairs={{8,16},{16,8},{24,32},{32,24},{40,48},{48,40},{56,64},{64,56},{72,... | collective-permute-start | bytes 884744 | tf_op jit(solution)/shard_map/ppermute | solution.py:523
  72.9 8.2 %collective-permute-start.6 = (bf16[9,32,128]{2,1,0:T(8,128)(2,1)S(1)}, bf16[9,32,128]{2,1,0:T(8,128)(2,1)S(1)}, u32[]{:S(2)}, u32[]{:S(2)}) collective-permute-start(bf16[9,32,128]{2,1,0:T(8,128)(2,1)S(1)} %get-tuple-element.53), channel_id=1, source_target_pairs={{0,1},{1,0},{2,3},{3,2},{4,5},{5,4},{6,7},{7,6},{8,9},{9,8},{10,11... | collective-permute-start | bytes 221192 | tf_op jit(solution)/shard_map/ppermute | solution.py:523
  72.9 9.9 %collective-permute-start.7 = (bf16[9,32,128]{2,1,0:T(8,128)(2,1)S(1)}, bf16[9,32,128]{2,1,0:T(8,128)(2,1)S(1)}, u32[]{:S(2)}, u32[]{:S(2)}) collective-permute-start(bf16[9,32,128]{2,1,0:T(8,128)(2,1)S(1)} %get-tuple-element.54), channel_id=1, source_target_pairs={{1,2},{2,1},{3,4},{4,3},{5,6},{6,5},{9,10},{10,9},{11,12},{12,11},... | collective-permute-start | bytes 221192 | tf_op jit(solution)/shard_map/ppermute | solution.py:523

commit v7 on v6

--- a/solution.py
+++ b/solution.py
@@ -394,7 +394,7 @@
     if not first:
         before, state, gradient = rest[:-1]
     elif len(pieces) == 2:
-        state, gradient, x_a, x_b = rest[:-1]
+        state, gradient, x_a, x_b, turned = rest[:-1]
     else:
         _, _, state, gradient = rest[:-1]
     levels = inv.shape[0]
@@ -441,11 +441,21 @@
             carry = y * get(inv, level)
             put(state, carry, every, level)
 
+    def keep(carry, level):
+        if x_a is not None:
+            for t in range(4):
+                for side in range(2):
+                    place = pl.ds(9 * (levels * t + level), 8)
+                    turned[side, place, :] = carry[t, 8 * side : 8 * side + 8]
+
     def back(j, carry):
         level = levels - 2 - j
         carry = get(state, every, level) + get(q, level) * carry
         put(state, carry, every, level)
+        keep(carry, level)
         return carry
+
+    keep(carry, levels - 1)
 
     carry = lax.fori_loop(0, levels - 1, back, carry, unroll=8)
     put(gradient, carry if first else get(before, every) + carry, every)
@@ -454,7 +464,9 @@
         def edge(out, order):
             for t in range(4):
                 rows = slice(levels * t, levels * t + levels)
-                near, second, third = (state[t, :, j, :] for j in order)
+                near, second, third = (
+                    turned[order[0] // 16, pl.ds(9 * levels * t + j % 8, levels, stride=9), :] for j in order
+                )
                 out[0, rows], out[1, rows] = split(near)
                 out[2, rows] = second.astype(bf16)
                 out[3, rows] = third.astype(bf16)
@@ -663,7 +675,8 @@
                 out_specs=[vmem] * (2 + len(extra)),
                 out_shape=[whole_field, gradient_shape] + extra,
                 input_output_aliases=aliases,
-                scratch_shapes=[pltpu.VMEM((levels * tracers * rows, 2 * lats), bf16)],
+                scratch_shapes=([pltpu.VMEM((2, fields * 9, lats), f32)] if extra else [])
+                + [pltpu.VMEM((levels * tracers * rows, 2 * lats), bf16)],
                 compiler_params=params(24),
                 cost_estimate=cost(5 * size, 2 * size),
                 name="column",

time: 88.5 us -> 87.4 us (0.988)
  Pallas kernels: 45.1 us -> 44 us
    pallas_call x3, Pallas kernels: 10.1 us -> 8.96 us  [column(): pl.pallas_call(kernel, in_specs=[vmem] * len(operands), out_specs=[vmem]...]
where the time goes in v7:
time: 87.4 us; the launch traced here: 87.1 us
  Pallas kernels  44 us (50%)
  starting transfers between devices  24.5 us (28%)
  waiting for transfers between devices  16.4 us (19%)
  between operations  0.91 us (1%)
    ppermute x8, starting transfers between devices, swap(): return lax.ppermute(value, axis, pairs)  14.2 us
    all_to_all x1, waiting for transfers between devices, local(): lax.all_to_all(packed, ('gx', 'gy'), split_axis=0, concat_axis=0, tiled=T...  11.6 us
    all_to_all x1, starting transfers between devices, local(): lax.all_to_all(packed, ('gx', 'gy'), split_axis=0, concat_axis=0, tiled=T...  10.3 us
    pallas_call x3, Pallas kernels, column(): pl.pallas_call(kernel, in_specs=[vmem] * len(operands), out_specs=[vmem]...  8.96 us
    pallas_call x2, Pallas kernels, forcing(): pl.pallas_call(kernel, in_specs=[smem, vmem, vmem, pl.BlockSpec(memory_sp...  8.51 us
    pallas_call x2, Pallas kernels, local(): pl.pallas_call(outer_kernel, in_specs=[vmem] * 8, out_specs=[vmem] * 3, o...  5.94 us
    pallas_call x2, Pallas kernels, local(): pl.pallas_call(lat_kernel, in_specs=[vmem] * 3, out_specs=vmem, out_shape...  5.91 us
    pallas_call x2, Pallas kernels, local(): pl.pallas_call(inner_kernel, in_specs=[vmem] * 3, out_specs=[vmem] * 3, o...  5.67 us
  transfers between devices with their start and end apart: 9, of which 4 were waited for; matrix products, arithmetic and copies ran while one was open for 2% of the time, Pallas kernels for 23%

profile of v7, /device:TPU:24, one launch (start us, length us, event | category | flops | bytes accessed | tf_op | source)
XLA Modules:
  0.0 87.1 jit_solution(1274651982589761445)
XLA Ops:
  0.6 2.6 %pack.1 = bf16[128,24,128]{2,1,0:T(8,128)(2,1)} custom-call(s32[1,128]{1,0:T(1,128)} %counts.1, bf16[72,4096]{1,0:T(8,128)(2,1)} %rows.1, bf16[4,4096]{1,0:T(4,128)(2,1)} %weights.3), custom_call_target="tpu_custom_call" | custom-call | tf_op jit(solution)/shard_map/pack/pallas_call | solution.py:545
  3.3 10.3 %all-to-all-start = ((bf16[128,24,128]{2,1,0:T(8,128)(2,1)}), bf16[128,24,128]{2,1,0:T(8,128)(2,1)S(1)}, u32[]{:S(2)}, u32[]{:S(2)}) async-start(bf16[128,24,128]{2,1,0:T(8,128)(2,1)} %pack.1), calls=%async_computation | async-start | bytes 1572864 | tf_op jit(solution)/shard_map/all_to_all | solution.py:559
  13.5 0.7 fusion.1
  14.3 0.6 broadcast_in_dim.2.bins
  14.9 1.9 %rank.1 = (bf16[4096,128]{1,0:T(8,128)(2,1)S(1)}, s32[32,128]{1,0:T(8,128)S(1)}) custom-call(bf16[4096,128]{1,0:T(8,128)(2,1)S(1)} %broadcast_in_dim.2.bins), custom_call_target="tpu_custom_call" | custom-call | flops 1000000000 | bytes 2000000 | tf_op jit(solution)/shard_map/rank/pallas_call | solution.py:569
  16.8 11.6 %all-to-all-done.got = bf16[128,24,128]{2,1,0:T(8,128)(2,1)S(1)} async-done(((bf16[128,24,128]{2,1,0:T(8,128)(2,1)}), bf16[128,24,128]{2,1,0:T(8,128)(2,1)S(1)}, u32[]{:S(2)}, u32[]{:S(2)}) %all-to-all-start) | async-done | bytes 786464 | tf_op jit(solution)/shard_map/all_to_all | solution.py:559
  28.4 3.5 %order.1 = (bf16[576,4096]{1,0:T(8,128)(2,1)S(1)}, f32[8,4096]{1,0:T(8,128)S(1)}) custom-call(bf16[128,24,128]{2,1,0:T(8,128)(2,1)S(1)} %all-to-all-done.got, s32[1,4096]{1,0:T(1,128)S(1)} %bitcast.13, bf16[4096,128]{1,0:T(8,128)(2,1)S(1)} %get-tuple-element.30.code), custom_call_target="tpu_custom_call" | custom-call | flops 1000000000 | bytes 8000000 | tf_op jit(solution)/shard_map/order/pallas_call | solution.py:576
  31.9 4.3 %forcing.2 = (f32[288,32,128]{2,1,0:T(8,128)S(1)}, bf16[4,288,128]{2,1,0:T(8,128)(2,1)S(1)}, bf16[4,288,128]{2,1,0:T(8,128)(2,1)S(1)}) custom-call(s32[32,128]{1,0:T(8,128)S(1)} %get-tuple-element.29.refs_0_, bf16[576,4096]{1,0:T(8,128)(2,1)S(1)} %get-tuple-element.31.refs_1_, f32[8,4096]{1,0:T(8,128)S(1)} %get-tuple-element.32.refs_2_, f32[288,32,128]{2,1,0:T(8,128)} %bitcast.14), custom_call_target="tpu_custom_call" | custom-call | flops 5000000000 | bytes 4718592 | tf_op jit(solution)/shard_map/forcing/pallas_call | solution.py:594
  36.2 0.1 collective-permute-start
  36.3 1.5 %collective-permute-start.1 = (bf16[4,288,128]{2,1,0:T(8,128)(2,1)S(1)}, bf16[4,288,128]{2,1,0:T(8,128)(2,1)S(1)}, u32[]{:S(2)}, u32[]{:S(2)}) collective-permute-start(bf16[4,288,128]{2,1,0:T(8,128)(2,1)S(1)} %get-tuple-element.35), channel_id=1, source_target_pairs={{8,16},{16,8},{24,32},{32,24},{40,48},{48,40},{56,64},{64,56},{72,... | collective-permute-start | bytes 884744 | tf_op jit(solution)/shard_map/ppermute | solution.py:535
  37.8 4.2 %forcing.3 = f32[288,32,128]{2,1,0:T(8,128)S(1)} custom-call(s32[32,128]{1,0:T(8,128)S(1)} %get-tuple-element.29.refs_0_, bf16[576,4096]{1,0:T(8,128)(2,1)S(1)} %get-tuple-element.31.refs_1_, f32[8,4096]{1,0:T(8,128)S(1)} %get-tuple-element.32.refs_2_, f32[288,32,128]{2,1,0:T(8,128)} %bitcast.15, ...), custom_call_target="tpu_custom_call", output_to_operand_aliasing={{}: (4, {})} | custom-call | flops 5000000000 | bytes 4718592 | tf_op jit(solution)/shard_map/forcing/pallas_call | solution.py:594
  42.1 2.8 %inner.2 = (f32[4,72,32,128]{3,2,1,0:T(8,128)S(1)}, bf16[9,32,128]{2,1,0:T(8,128)(2,1)S(1)}, bf16[9,32,128]{2,1,0:T(8,128)(2,1)S(1)}) custom-call(f32[4,72,32,128]{3,2,1,0:T(8,128)S(1)} %bitcast.7, f32[72,32,128]{2,1,0:T(8,128)S(1)} %copy-done.1, bf16[256,256]{1,0:T(8,128)(2,1)S(1)} %copy-done.3), custom_call_target="tpu_custom_call" | custom-call | flops 23592960 | bytes 9437184 | tf_op jit(solution)/shard_map/inner/pallas_call | solution.py:623
  44.9 0.0 copy-start.5
  45.0 3.0 %outer.2 = (f32[4,72,32,128]{3,2,1,0:T(8,128)S(1)}, bf16[9,32,128]{2,1,0:T(8,128)(2,1)S(1)}, bf16[9,32,128]{2,1,0:T(8,128)(2,1)S(1)}) custom-call(f32[4,72,32,128]{3,2,1,0:T(8,128)S(1)} %bitcast.8, f32[72,32,128]{2,1,0:T(8,128)S(1)} %copy-done.1, bf16[256,256]{1,0:T(8,128)(2,1)S(1)} %copy-done.3, ...), custom_call_target="tpu_custom_call", output_to_operand_aliasing={{0}: (5, {}), {1}: (6, {}), {2}: (7, {})} | custom-call | flops 23592960 | bytes 9437184 | tf_op jit(solution)/shard_map/outer/pallas_call | solution.py:633
  47.9 0.6 collective-permute-start.2
  48.6 5.4 %collective-permute-start.3 = (bf16[9,32,128]{2,1,0:T(8,128)(2,1)S(1)}, bf16[9,32,128]{2,1,0:T(8,128)(2,1)S(1)}, u32[]{:S(2)}, u32[]{:S(2)}) collective-permute-start(bf16[9,32,128]{2,1,0:T(8,128)(2,1)S(1)} %get-tuple-element.43), channel_id=1, source_target_pairs={{1,2},{2,1},{3,4},{4,3},{5,6},{6,5},{9,10},{10,9},{11,12},{12,11},... | collective-permute-start | bytes 221192 | tf_op jit(solution)/shard_map/ppermute | solution.py:535
  53.9 0.9 %factor.1 = (f32[72,32,128]{2,1,0:T(8,128)S(1)}, f32[72,32,128]{2,1,0:T(8,128)S(1)}) custom-call(f32[71,32,128]{2,1,0:T(8,128)S(1)} %copy-done.2), custom_call_target="tpu_custom_call" | custom-call | flops 8847360 | bytes 3538944 | tf_op jit(solution)/shard_map/factor/pallas_call | solution.py:561
  54.8 0.0 copy-start.4
  54.9 3.1 %lat.2.refs_0_ = f32[4,72,32,128]{3,2,1,0:T(8,128)S(1)} custom-call(f32[4,72,32,128]{3,2,1,0:T(8,128)S(1)} %get-tuple-element.39.zonal, f32[72,32,128]{2,1,0:T(8,128)S(1)} %copy-done, bf16[256,256]{1,0:T(8,128)(2,1)S(1)} %copy-done.5), custom_call_target="tpu_custom_call" | custom-call | flops 23592960 | bytes 9437184 | tf_op jit(solution)/shard_map/lat/pallas_call | solution.py:653
  57.9 0.5 collective-permute-done.3.refs_6_
  58.4 1.9 %column.3 = (f32[4,72,32,128]{3,2,1,0:T(8,128)S(1)}, f32[4,32,128]{2,1,0:T(8,128)S(1)}, bf16[4,288,128]{2,1,0:T(8,128)(2,1)S(1)}, bf16[4,288,128]{2,1,0:T(8,128)(2,1)S(1)}) custom-call(f32[4,72,32,128]{3,2,1,0:T(8,128)S(1)} %lat.2.refs_0_, f32[72,32,128]{2,1,0:T(8,128)S(1)} %copy-done, f32[71,32,128]{2,1,0:T(8,128)S(1)} %copy-done.2, ...), custom_call_target="tpu_custom_call" | custom-call | flops 23592960 | bytes 9437184 | tf_op jit(solution)/shard_map/column/pallas_call | solution.py:672
  60.3 0.1 collective-permute-start.4
  60.4 1.3 %collective-permute-start.5 = (bf16[4,288,128]{2,1,0:T(8,128)(2,1)S(1)}, bf16[4,288,128]{2,1,0:T(8,128)(2,1)S(1)}, u32[]{:S(2)}, u32[]{:S(2)}) collective-permute-start(bf16[4,288,128]{2,1,0:T(8,128)(2,1)S(1)} %get-tuple-element.48), channel_id=1, source_target_pairs={{8,16},{16,8},{24,32},{32,24},{40,48},{48,40},{56,64},{64,56},{72,... | collective-permute-start | bytes 884744 | tf_op jit(solution)/shard_map/ppermute | solution.py:535
  61.8 1.6 %column.4 = (f32[4,72,32,128]{3,2,1,0:T(8,128)S(1)}, f32[4,32,128]{2,1,0:T(8,128)S(1)}) custom-call(f32[4,72,32,128]{3,2,1,0:T(8,128)S(1)} %lat.2.refs_0_, f32[72,32,128]{2,1,0:T(8,128)S(1)} %copy-done, f32[71,32,128]{2,1,0:T(8,128)S(1)} %copy-done.2, f32[72,32,128]{2,1,0:T(8,128)S(1)} %get-tuple-element.40.refs_3_, ...), custom_call_target="tpu_custom_call", output_to_operand_aliasing={{0}: (8, {}), {1}: (9, {})} | custom-call | flops 23592960 | bytes 9437184 | tf_op jit(solution)/shard_map/column/pallas_call | solution.py:672
  63.4 2.8 %inner.3 = (f32[4,72,32,128]{3,2,1,0:T(8,128)S(1)}, bf16[9,32,128]{2,1,0:T(8,128)(2,1)S(1)}, bf16[9,32,128]{2,1,0:T(8,128)(2,1)S(1)}) custom-call(f32[4,72,32,128]{3,2,1,0:T(8,128)S(1)} %get-tuple-element.46.state, f32[72,32,128]{2,1,0:T(8,128)S(1)} %copy-done.1, bf16[256,256]{1,0:T(8,128)(2,1)S(1)} %copy-done.3), custom_call_target="tpu_custom_call" | custom-call | flops 23592960 | bytes 9437184 | tf_op jit(solution)/shard_map/inner/pallas_call | solution.py:623
  66.3 2.5 %collective-permute-done.5 = bf16[4,288,128]{2,1,0:T(8,128)(2,1)S(1)} collective-permute-done((bf16[4,288,128]{2,1,0:T(8,128)(2,1)S(1)}, bf16[4,288,128]{2,1,0:T(8,128)(2,1)S(1)}, u32[]{:S(2)}, u32[]{:S(2)}) %collective-permute-start.5) | collective-permute-done | bytes 294944 | tf_op jit(solution)/shard_map/ppermute | solution.py:535
  68.8 3.0 %outer.3 = (f32[4,72,32,128]{3,2,1,0:T(8,128)S(1)}, bf16[9,32,128]{2,1,0:T(8,128)(2,1)S(1)}, bf16[9,32,128]{2,1,0:T(8,128)(2,1)S(1)}) custom-call(f32[4,72,32,128]{3,2,1,0:T(8,128)S(1)} %get-tuple-element.46.state, f32[72,32,128]{2,1,0:T(8,128)S(1)} %copy-done.1, ...), custom_call_target="tpu_custom_call", output_to_operand_aliasing={{0}: (5, {}), {1}: (6, {}), {2}: (7, {})} | custom-call | flops 23592960 | bytes 9437184 | tf_op jit(solution)/shard_map/outer/pallas_call | solution.py:633
  71.8 0.1 collective-permute-start.6
  71.9 5.2 %collective-permute-start.7 = (bf16[9,32,128]{2,1,0:T(8,128)(2,1)S(1)}, bf16[9,32,128]{2,1,0:T(8,128)(2,1)S(1)}, u32[]{:S(2)}, u32[]{:S(2)}) collective-permute-start(bf16[9,32,128]{2,1,0:T(8,128)(2,1)S(1)} %get-tuple-element.54), channel_id=1, source_target_pairs={{1,2},{2,1},{3,4},{4,3},{5,6},{6,5},{9,10},{10,9},{11,12},{12,11},... | collective-permute-start | bytes 221192 | tf_op jit(solution)/shard_map/ppermute | solution.py:535
  77.0 2.9 %lat.3.refs_0_ = f32[4,72,32,128]{3,2,1,0:T(8,128)S(1)} custom-call(f32[4,72,32,128]{3,2,1,0:T(8,128)S(1)} %get-tuple-element.52.zonal, f32[72,32,128]{2,1,0:T(8,128)S(1)} %copy-done, bf16[256,256]{1,0:T(8,128)(2,1)S(1)} %copy-done.5), custom_call_target="tpu_custom_call" | custom-call | flops 23592960 | bytes 9437184 | tf_op jit(solution)/shard_map/lat/pallas_call | solution.py:653
  79.9 1.8 %collective-permute-done.7.refs_6_ = bf16[9,32,128]{2,1,0:T(8,128)(2,1)S(1)} collective-permute-done((bf16[9,32,128]{2,1,0:T(8,128)(2,1)S(1)}, bf16[9,32,128]{2,1,0:T(8,128)(2,1)S(1)}, u32[]{:S(2)}, u32[]{:S(2)}) %collective-permute-start.7) | collective-permute-done | bytes 73760 | tf_op jit(solution)/shard_map/ppermute | solution.py:535
  81.7 5.4 %column.5 = (f32[4,72,32,128]{3,2,1,0:T(8,128)}, f32[4,32,128]{2,1,0:T(8,128)}) custom-call(f32[4,72,32,128]{3,2,1,0:T(8,128)S(1)} %lat.3.refs_0_, f32[72,32,128]{2,1,0:T(8,128)S(1)} %copy-done, f32[71,32,128]{2,1,0:T(8,128)S(1)} %copy-done.2, f32[72,32,128]{2,1,0:T(8,128)S(1)} %get-tuple-element.40.refs_3_, f32[72,32,128]{2,1,0:T(8,128)S(1)} %get-tuple-element.41.refs_4_, ...), custom_call_target="tpu_custom_call" | custom-call | flops 23592960 | bytes 9437184 | tf_op jit(solution)/shard_map/column/pallas_call | solution.py:672
  (17 shorter events, 0.0 us)
Async XLA Ops:
  0.6 27.8 %copy-start.6 = (s32[4096]{0:T(1024)S(1)}, s32[4096]{0:T(1024)}, u32[]{:S(2)}) copy-start(s32[4096]{0:T(1024)} %param.19) | copy-start | bytes 49156
  3.3 25.1 %all-to-all-start = ((bf16[128,24,128]{2,1,0:T(8,128)(2,1)}), bf16[128,24,128]{2,1,0:T(8,128)(2,1)S(1)}, u32[]{:S(2)}, u32[]{:S(2)}) async-start(bf16[128,24,128]{2,1,0:T(8,128)(2,1)} %pack.1), calls=%async_computation | async-start | bytes 1572864 | tf_op jit(solution)/shard_map/all_to_all | solution.py:559
  36.2 8.7 %collective-permute-start = (bf16[4,288,128]{2,1,0:T(8,128)(2,1)S(1)}, bf16[4,288,128]{2,1,0:T(8,128)(2,1)S(1)}, u32[]{:S(2)}, u32[]{:S(2)}) collective-permute-start(bf16[4,288,128]{2,1,0:T(8,128)(2,1)S(1)} %get-tuple-element.34), channel_id=1, source_target_pairs={{0,8},{8,0},{16,24},{24,16},{32,40},{40,32},{48,56},{56,48},{64,72... | collective-permute-start | bytes 884744 | tf_op jit(solution)/shard_map/ppermute | solution.py:535
  36.3 8.6 %collective-permute-start.1 = (bf16[4,288,128]{2,1,0:T(8,128)(2,1)S(1)}, bf16[4,288,128]{2,1,0:T(8,128)(2,1)S(1)}, u32[]{:S(2)}, u32[]{:S(2)}) collective-permute-start(bf16[4,288,128]{2,1,0:T(8,128)(2,1)S(1)} %get-tuple-element.35), channel_id=1, source_target_pairs={{8,16},{16,8},{24,32},{32,24},{40,48},{48,40},{56,64},{64,56},{72,... | collective-permute-start | bytes 884744 | tf_op jit(solution)/shard_map/ppermute | solution.py:535
  37.8 4.2 %copy-start.1 = (f32[72,32,128]{2,1,0:T(8,128)S(1)}, f32[72,32,128]{2,1,0:T(8,128)}, u32[]{:S(2)}) copy-start(f32[72,32,128]{2,1,0:T(8,128)} %courant.10) | copy-start | bytes 3538948
  37.8 4.2 %copy-start.3 = (bf16[256,256]{1,0:T(8,128)(2,1)S(1)}, bf16[256,256]{1,0:T(8,128)(2,1)}, u32[]{:S(2)}) copy-start(bf16[256,256]{1,0:T(8,128)(2,1)} %constant.22.clone.spread) | copy-start | bytes 393220
  44.9 9.0 %copy-start.2 = (f32[71,32,128]{2,1,0:T(8,128)S(1)}, f32[71,32,128]{2,1,0:T(8,128)}, u32[]{:S(2)}) copy-start(f32[71,32,128]{2,1,0:T(8,128)} %refs_2_.5) | copy-start | bytes 3489796
  44.9 9.9 %copy-start = (f32[72,32,128]{2,1,0:T(8,128)S(1)}, f32[72,32,128]{2,1,0:T(8,128)}, u32[]{:S(2)}) copy-start(f32[72,32,128]{2,1,0:T(8,128)} %refs_1_.5) | copy-start | bytes 3538948
  44.9 9.9 %copy-start.5 = (bf16[256,256]{1,0:T(8,128)(2,1)S(1)}, bf16[256,256]{1,0:T(8,128)(2,1)}, u32[]{:S(2)}) copy-start(bf16[256,256]{1,0:T(8,128)(2,1)} %constant.23.clone.weights) | copy-start | bytes 393220
  47.9 10.0 %collective-permute-start.2 = (bf16[9,32,128]{2,1,0:T(8,128)(2,1)S(1)}, bf16[9,32,128]{2,1,0:T(8,128)(2,1)S(1)}, u32[]{:S(2)}, u32[]{:S(2)}) collective-permute-start(bf16[9,32,128]{2,1,0:T(8,128)(2,1)S(1)} %get-tuple-element.42), channel_id=1, source_target_pairs={{0,1},{1,0},{2,3},{3,2},{4,5},{5,4},{6,7},{7,6},{8,9},{9,8},{10,11... | collective-permute-start | bytes 221192 | tf_op jit(solution)/shard_map/ppermute | solution.py:535
  48.6 9.8 %collective-permute-start.3 = (bf16[9,32,128]{2,1,0:T(8,128)(2,1)S(1)}, bf16[9,32,128]{2,1,0:T(8,128)(2,1)S(1)}, u32[]{:S(2)}, u32[]{:S(2)}) collective-permute-start(bf16[9,32,128]{2,1,0:T(8,128)(2,1)S(1)} %get-tuple-element.43), channel_id=1, source_target_pairs={{1,2},{2,1},{3,4},{4,3},{5,6},{6,5},{9,10},{10,9},{11,12},{12,11},... | collective-permute-start | bytes 221192 | tf_op jit(solution)/shard_map/ppermute | solution.py:535
  54.8 3.6 %copy-start.4 = (bf16[256,256]{1,0:T(8,128)(2,1)S(1)}, bf16[256,256]{1,0:T(8,128)(2,1)}, u32[]{:S(2)}) copy-start(bf16[256,256]{1,0:T(8,128)(2,1)} %constant.24.clone.refs_7_) | copy-start | bytes 393220
  60.3 5.9 %collective-permute-start.4 = (bf16[4,288,128]{2,1,0:T(8,128)(2,1)S(1)}, bf16[4,288,128]{2,1,0:T(8,128)(2,1)S(1)}, u32[]{:S(2)}, u32[]{:S(2)}) collective-permute-start(bf16[4,288,128]{2,1,0:T(8,128)(2,1)S(1)} %get-tuple-element.47), channel_id=1, source_target_pairs={{0,8},{8,0},{16,24},{24,16},{32,40},{40,32},{48,56},{56,48},{64,72... | collective-permute-start | bytes 884744 | tf_op jit(solution)/shard_map/ppermute | solution.py:535
  60.4 8.3 %collective-permute-start.5 = (bf16[4,288,128]{2,1,0:T(8,128)(2,1)S(1)}, bf16[4,288,128]{2,1,0:T(8,128)(2,1)S(1)}, u32[]{:S(2)}, u32[]{:S(2)}) collective-permute-start(bf16[4,288,128]{2,1,0:T(8,128)(2,1)S(1)} %get-tuple-element.48), channel_id=1, source_target_pairs={{8,16},{16,8},{24,32},{32,24},{40,48},{48,40},{56,64},{64,56},{72,... | collective-permute-start | bytes 884744 | tf_op jit(solution)/shard_map/ppermute | solution.py:535
  71.8 8.2 %collective-permute-start.6 = (bf16[9,32,128]{2,1,0:T(8,128)(2,1)S(1)}, bf16[9,32,128]{2,1,0:T(8,128)(2,1)S(1)}, u32[]{:S(2)}, u32[]{:S(2)}) collective-permute-start(bf16[9,32,128]{2,1,0:T(8,128)(2,1)S(1)} %get-tuple-element.53), channel_id=1, source_target_pairs={{0,1},{1,0},{2,3},{3,2},{4,5},{5,4},{6,7},{7,6},{8,9},{9,8},{10,11... | collective-permute-start | bytes 221192 | tf_op jit(solution)/shard_map/ppermute | solution.py:535
  71.9 9.9 %collective-permute-start.7 = (bf16[9,32,128]{2,1,0:T(8,128)(2,1)S(1)}, bf16[9,32,128]{2,1,0:T(8,128)(2,1)S(1)}, u32[]{:S(2)}, u32[]{:S(2)}) collective-permute-start(bf16[9,32,128]{2,1,0:T(8,128)(2,1)S(1)} %get-tuple-element.54), channel_id=1, source_target_pairs={{1,2},{2,1},{3,4},{4,3},{5,6},{6,5},{9,10},{10,9},{11,12},{12,11},... | collective-permute-start | bytes 221192 | tf_op jit(solution)/shard_map/ppermute | solution.py:535
